TPU v7x, 32 devices: a whole 2x2x4 slice. The times are simulated.
32 devices in a mesh: aux: 16 (over z, y, x), occ: 2 (over core).
Axes of the slice: x: 2, y: 2, z: 4, core: 2. Of those that a mesh axis runs over, the one named last changes fastest.
Arguments:
- three_index: bfloat16 [2, 64, 6, 128, 1024], P('occ', 'aux'), may hold values from -6 to 6
- fit_factor: bfloat16 [64, 128, 128], P('aux'), may hold values from -0.046875 to 0.046875
- slots: int32 [2, 64, 6], P('occ', 'aux'), may hold values from 0 to 15, all different within a row; in each aligned block of 4 rows (0 to 3, 4 to 7, ..., all dimensions but the last counted through in order) at most 2 rows name the same one
- owner: int32 [16], replicated, may hold values from 0 to 15, each once
Outputs:
- exchange_rows: float32 [16, 128, 2048], P('aux', None, 'occ')
Inputs may be any that keep to these rules, and one draw needn't show every extreme that they name: `slots`: the 6 blocks of one row differ. In each aligned block of 4 rows (one device's auxiliary blocks for one occupied block) no basis block is listed more than 2 times, and some block exactly 2 times.
All inputs are finite; a program needn't handle non-finite values.
Results may differ from a plain program's by a relative error of at most 0.00054.
Values sent between devices are 32-bit elements; how exact they have to be, the bound alone decides.
No kernel may reach another device: no remote copies, remote signals or barrier semaphores. Data moves between devices by JAX's collectives and lax.ppermute only.
A program may use at most 128 MiB of HBM per device.

v0:
```python
import jax
import jax.numpy as jnp
from jax import lax
from jax.sharding import PartitionSpec as P


def local(three_index, fit_factor, slots, owner):
    tiles = three_index[0]
    blocks = slots[0]
    count_a, count_s, tile_rows, width = tiles.shape
    orbitals = width // tile_rows
    groups = lax.axis_size("aux")
    total_blocks = owner.shape[0]
    strip_count = count_a * count_s
    capacity = max(2, (strip_count + groups - 1) // groups)
    fitted = jnp.einsum(
        "apq,asqf->aspf", fit_factor, tiles, preferred_element_type=jnp.float32
    ).astype(jnp.bfloat16)
    shaped = fitted.reshape(count_a, count_s, tile_rows, tile_rows, orbitals)
    partial_value = jnp.einsum(
        "aspni,atpmi->asntm", shaped, shaped, preferred_element_type=jnp.float32
    )
    partial_value = partial_value.reshape(strip_count, tile_rows, count_s * tile_rows)
    flat_blocks = blocks.reshape(strip_count)
    block_range = jnp.arange(total_blocks, dtype=jnp.int32)
    target = jnp.sum(
        jnp.where(flat_blocks[:, None] == block_range[None, :], owner[None, :], 0), axis=1
    )
    order = jnp.arange(strip_count, dtype=jnp.int32)
    earlier = (target[:, None] == target[None, :]) & (order[None, :] < order[:, None])
    rank = jnp.sum(earlier.astype(jnp.int32), axis=1)
    place = target * capacity + rank
    send_rows = (
        jnp.zeros((groups * capacity, tile_rows, count_s * tile_rows), jnp.float32)
        .at[place]
        .set(partial_value)
    )
    column_ids = jnp.repeat(blocks, count_s, axis=0)
    send_ids = jnp.full((groups * capacity, count_s), -1, jnp.int32).at[place].set(column_ids)
    received, received_ids = (
        lax.all_to_all(send_rows, "aux", split_axis=0, concat_axis=0, tiled=True),
        lax.all_to_all(send_ids, "aux", split_axis=0, concat_axis=0, tiled=True),
    )
    pieces = received.reshape(groups * capacity, tile_rows, count_s, tile_rows)
    pieces = jnp.transpose(pieces, (0, 2, 1, 3)).reshape(
        groups * capacity * count_s, tile_rows, tile_rows
    )
    flat_ids = received_ids.reshape(groups * capacity * count_s)
    flat_ids = jnp.where(flat_ids < 0, total_blocks, flat_ids)
    placed = (
        jnp.zeros((total_blocks, tile_rows, tile_rows), jnp.float32)
        .at[flat_ids]
        .add(pieces, mode="drop")
    )
    owned_rows = jnp.transpose(placed, (1, 0, 2)).reshape(tile_rows, total_blocks * tile_rows)
    result = lax.psum_scatter(owned_rows, "occ", scatter_dimension=1, tiled=True)
    return result[None]


def solution(mesh):
    placed = (P("occ", "aux", None, None, None), P("aux", None, None), P("occ", "aux", None), P())
    return jax.shard_map(
        local, mesh=mesh, in_specs=placed, out_specs=P("aux", None, "occ"), check_vma=False
    )
```

profile of v0, /device:TPU:0, one launch (start us, length us, event | category | flops | bytes accessed | tf_op | source)
XLA Modules:
  0.0 427.9 jit_solution(10563906519721406196)
XLA Ops:
  6.5 0.8 eq.28
  7.3 0.7 select_reduce_fusion
  8.1 0.2 convert_reduce_fusion
  8.3 0.8 copy.25
  9.0 0.1 broadcast_in_dim.44
  9.1 0.1 reshape.93
  9.2 0.1 copy.26
  9.3 1.2 scatter_custom_fusion
  10.5 8.3 %all-to-all-start = ((s32[16,2,6]{2,1,0:T(2,128)}), s32[16,2,6]{2,1,0:T(2,128)S(1)}, u32[]{:S(2)}, u32[]{:S(2)}) async-start(s32[16,2,6]{2,1,0:T(2,128)} %bitcast.3), calls=%async_computation | async-start | bytes 32768 | tf_op jit(solution)/shard_map/all_to_all | solution.py:42
  18.8 5.0 %convert_bitcast_fusion = bf16[4,6,128,128,8,1]{2,4,3,1,0,5:T(8,128)(2,1)S(1)} fusion(bf16[1,4,6,128,1024]{4,3,2,1,0:T(8,128)(2,1)} %param.4, bf16[4,128,128]{2,1,0:T(8,128)(2,1)S(1)} %copy-done), kind=kOutput, calls=%fused_computation.8 | convolution fusion | flops 808452096 | bytes 12713984 | tf_op jit(solution)/shard_map/apq,asqf->aspf/dot_general | solution.py:16
  23.9 7.4 %fusion = f32[4,6,128,6,128,1]{2,4,5,3,1,0:T(8,128)} fusion(bf16[4,6,128,128,8,1]{2,4,3,1,0,5:T(8,128)(2,1)S(1)} %convert_bitcast_fusion), kind=kOutput, calls=%fused_computation.3 | convolution fusion | flops 4831838208 | bytes 15728640 | tf_op jit(solution)/shard_map/aspni,atpmi->asntm/dot_general | solution.py:20
  31.3 9.6 %copy.30 = f32[24,128,768]{2,1,0:T(8,128)} copy(f32[24,128,768]{1,2,0:T(8,128)} %bitcast.43) | data formatting | bytes 18874368 | tf_op jit(solution)/shard_map/reshape | solution.py:23
  40.9 5.9 %broadcast_in_dim.46 = f32[32,128,768]{2,1,0:T(8,128)} broadcast(f32[]{:T(128)} %constant.6.clone.1), dimensions={} | broadcast | bytes 12582916 | tf_op jit(solution)/shard_map/broadcast_in_dim | solution.py:34
  46.9 19.5 %scatter_fusion = f32[32,128,768]{2,1,0:T(8,128)} fusion(f32[32,128,768]{2,1,0:T(8,128)} %broadcast_in_dim.46, s32[24]{0:T(128)S(1)} %fusion.11, f32[24,128,768]{2,1,0:T(8,128)} %copy.30), kind=kCustom, calls=%fused_computation.1 | custom fusion | bytes 28311648 | tf_op jit(solution)/shard_map/scatter | solution.py:36
  66.3 6.9 %all-to-all-start.1 = ((f32[32,128,768]{2,1,0:T(8,128)}), f32[32,128,768]{2,1,0:T(8,128)}, u32[]{:S(2)}, u32[]{:S(2)}) async-start(f32[32,128,768]{2,1,0:T(8,128)} %scatter_fusion), calls=%async_computation.1 | async-start | bytes 25165824 | tf_op jit(solution)/shard_map/all_to_all | solution.py:41
  73.3 0.1 reshape.83
  73.5 235.1 %all-to-all-done.1 = f32[32,128,768]{2,1,0:T(8,128)} async-done(((f32[32,128,768]{2,1,0:T(8,128)}), f32[32,128,768]{2,1,0:T(8,128)}, u32[]{:S(2)}, u32[]{:S(2)}) %all-to-all-start.1) | async-done | bytes 12582944 | tf_op jit(solution)/shard_map/all_to_all | solution.py:41
  308.5 12.6 %copy.31 = f32[32,128,768]{1,2,0:T(8,128)} copy(f32[32,128,768]{2,1,0:T(8,128)} %all-to-all-done.1) | data formatting | bytes 25165824 | tf_op jit(solution)/shard_map/all_to_all | solution.py:41
  321.1 12.6 %copy.32 = f32[32,6,128,128]{3,2,1,0:T(8,128)} copy(f32[32,6,128,128]{2,3,1,0:T(8,128)} %bitcast.41) | data formatting | bytes 25165824 | tf_op jit(solution)/shard_map/transpose | solution.py:45
  333.7 0.1 broadcast_in_dim.40
  333.8 25.3 %scatter_fusion.1 = f32[16,128,128]{2,1,0:T(8,128)S(1)} fusion(f32[16,128,128]{2,1,0:T(8,128)S(1)} %broadcast_in_dim.40, s32[192]{0:T(256)S(1)} %bitcast.47, f32[192,128,128]{2,1,0:T(8,128)} %bitcast.42), kind=kCustom, calls=%fused_computation.2 | custom fusion | flops 3145728 | bytes 37749504 | tf_op jit(solution)/shard_map/scatter-add | solution.py:53
  359.0 1.3 copy.33
  360.4 58.6 %reduce-scatter.2.cloned.1.call-done = f32[128,1024]{0,1:T(8,128)} async-done(((f32[128,2048]{0,1:T(8,128)}), f32[128,1024]{0,1:T(8,128)}) %reduce-scatter.2.cloned.1.call-update) | async-done | bytes 524304 | tf_op jit(solution)/shard_map/reduce_scatter | solution.py:56
  419.0 2.0 copy.34
  (9 shorter events, 0.1 us)
Async XLA Ops:
  6.5 12.3 %copy-start = (bf16[4,128,128]{2,1,0:T(8,128)(2,1)S(1)}, bf16[4,128,128]{2,1,0:T(8,128)(2,1)}, u32[]{:S(2)}) copy-start(bf16[4,128,128]{2,1,0:T(8,128)(2,1)} %param.5) | copy-start | bytes 393220
  10.5 55.8 %all-to-all-start = ((s32[16,2,6]{2,1,0:T(2,128)}), s32[16,2,6]{2,1,0:T(2,128)S(1)}, u32[]{:S(2)}, u32[]{:S(2)}) async-start(s32[16,2,6]{2,1,0:T(2,128)} %bitcast.3), calls=%async_computation | async-start | bytes 32768 | tf_op jit(solution)/shard_map/all_to_all | solution.py:42
  66.3 242.2 %all-to-all-start.1 = ((f32[32,128,768]{2,1,0:T(8,128)}), f32[32,128,768]{2,1,0:T(8,128)}, u32[]{:S(2)}, u32[]{:S(2)}) async-start(f32[32,128,768]{2,1,0:T(8,128)} %scatter_fusion), calls=%async_computation.1 | async-start | bytes 25165824 | tf_op jit(solution)/shard_map/all_to_all | solution.py:41
  73.3 345.7 %reduce-scatter.2.cloned.1.call-start = ((), (), s32[]{:S(2)}) async-start(), calls=%async_computation.3 | async-start | bytes 1572864 | tf_op jit(solution)/shard_map/reduce_scatter | solution.py:56
  333.8 87.3 %copy-start.1 = (bf16[4,128,128]{2,1,0:T(8,128)(2,1)S(1)}, bf16[4,128,128]{2,1,0:T(8,128)(2,1)}, u32[]{:S(2)}) copy-start(bf16[4,128,128]{2,1,0:T(8,128)(2,1)} %param.5) | copy-start | bytes 393220
Sparse Core Ops, SparseCore 0:
  360.5 58.4 reduce-scatter.1
where the time goes:
time: 429 us; the launch traced here: 428 us
  waiting for transfers between devices  294 us (69%)
  local copies, waits for them, and re-layouts  66.8 us (16%)
  other arithmetic  26.2 us (6%)
  starting transfers between devices  15.3 us (4%)
  between operations  13.5 us (3%)
  matrix products  12.5 us (3%)
    all_to_all x1, waiting for transfers between devices, local(): lax.all_to_all(send_rows, 'aux', split_axis=0, concat_axis=0, tiled=True)  235 us
    reduce_scatter x1, waiting for transfers between devices, local(): lax.psum_scatter(owned_rows, 'occ', scatter_dimension=1, tiled=True)  58.6 us
    scatter-add x1, other arithmetic, local(): placed = jnp.zeros((total_blocks, tile_rows, tile_rows), jnp.float32).at[...  25.3 us
    scatter x1, local copies, waits for them, and re-layouts, local(): send_rows = jnp.zeros((groups * capacity, tile_rows, count_s * tile_rows)...  19.5 us
    all_to_all x1, local copies, waits for them, and re-layouts, local(): lax.all_to_all(send_rows, 'aux', split_axis=0, concat_axis=0, tiled=True)  12.6 us
    transpose x1, local copies, waits for them, and re-layouts, local(): jnp.transpose(pieces, (0, 2, 1, 3))  12.6 us
    reshape x1, local copies, waits for them, and re-layouts, local(): partial_value.reshape(strip_count, tile_rows, count_s * tile_rows)  9.63 us
  transfers between devices with their start and end apart: 3, of which 2 were waited for; matrix products, arithmetic and copies ran while one was open for 11% of the time, Pallas kernels for 0%

commit v1 on v0

v1 whole, which is shorter than its diff:
```python
import functools

import jax
import jax.numpy as jnp
from jax import lax
from jax.experimental import pallas as pl
from jax.experimental.pallas import tpu as pltpu
from jax.sharding import PartitionSpec as P

PLANE = 4


def pair_kernel(
    cfg, slots_ref, owner_ref, x_ref, fit_ref, send_s, send_k, keep_s, keep_k,
    xbuf, gbuf, fbuf, res, acc, ranked, insem, outsem,
):
    chips, cores, count_a, count_s, orbitals, rows, slices, sub, lines = cfg
    me = lax.axis_index("aux")
    core = lax.axis_index("occ")
    half = rows * cores
    for a in range(count_a):
        own = [owner_ref[slots_ref[a * count_s + s]] for s in range(count_s)]
        for s in range(count_s):
            rank = jnp.int32(0)
            for t in range(count_s):
                if t != s:
                    rank = rank + (own[t] < own[s]).astype(jnp.int32)
            place = a * count_s + rank
            ranked[place] = own[s]
            pltpu.make_async_copy(x_ref.at[a, s], xbuf.at[place], insem.at[place]).start()
    acc[...] = jnp.zeros_like(acc)

    def one(a, carry):
        base = a * count_s
        for p in range(count_s):
            pltpu.make_async_copy(x_ref.at[a, p], xbuf.at[base + p], insem.at[base + p]).wait()
            fitted = jnp.dot(fit_ref[a], xbuf[base + p], preferred_element_type=jnp.float32)
            gbuf[p] = fitted.T
            for i in range(orbitals):
                fbuf[p * 128:(p + 1) * 128, i * 128:(i + 1) * 128] = gbuf[
                    p, pl.ds(i, 128, stride=orbitals), :
                ].astype(jnp.bfloat16)
        for g in range(0, count_s, 2):
            res[g // 2, :, g * 128:] = lax.dot_general(
                fbuf[g * 128:(g + 2) * 128, :], fbuf[g * 128:, :],
                (((1,), (1,)), ((), ())), preferred_element_type=jnp.float32,
            )
        for p in range(count_s):
            for q in range(p, count_s):
                first, second = ranked[base + p], ranked[base + q]
                d = first ^ second
                unit = 1 + (d & (PLANE - 1)) * lines + (d >> 2)
                for h in range(2):
                    jr = (second if h else first) ^ me
                    u = 0 if (h and p == q) else unit
                    for o in range(cores):
                        for f in range(slices):
                            row = (p % 2) * 128 + h * half + (o ^ core) * rows + f * sub
                            tile = res[
                                p // 2, pl.ds(pl.multiple_of(row, sub), sub),
                                q * 128:(q + 1) * 128,
                            ]
                            bit = (jr >> f) & 1
                            rest = ((jr >> (f + 1)) << f) | (jr & ((1 << f) - 1))
                            acc[o, f, bit, rest, u] += tile
        return carry

    lax.fori_loop(0, count_a, one, 0)
    copies = []
    for o in range(cores):
        for f in range(slices):
            if o:
                copies.append((acc.at[o, f, 1], send_s.at[o - 1, f]))
                copies.append((acc.at[o, f, 0], send_k.at[o - 1, f]))
            else:
                copies.append((acc.at[o, f, 1], keep_s.at[f]))
                copies.append((acc.at[o, f, 0], keep_k.at[f]))
    copies = [pltpu.make_async_copy(a, b, outsem.at[i]) for i, (a, b) in enumerate(copies)]
    for c in copies:
        c.start()
    for c in copies:
        c.wait()


def place_kernel(cfg, owner_ref, *refs):
    chips, cores, rows, slices, sub, lines = cfg
    out, tiles = refs[-2], refs[-1]
    refs = refs[:-2]
    me = lax.axis_index("aux")
    core = lax.axis_index("occ")
    half = rows * cores
    per = len(refs) // cores
    for o in range(cores):
        line, own = refs[o * per], refs[o * per + 1]
        near, far = refs[o * per + 2], refs[o * per + 3]
        shift = (o ^ core) * rows
        for f in range(slices):
            for d in range(chips):
                dp, dz = d & (PLANE - 1), d >> 2
                if dp == 0:
                    mine = line[f, 1 + dz]
                    other = line[f, 0] if dz == 0 else line[f, lines + dz]
                else:
                    mine = own[f, dp - 1, dz]
                    other = near[dp - 1, f] if dz == 0 else far[dz - 1, dp - 1, f]
                top = (me >> (d.bit_length() - 1)) & 1 if d else 0
                at = shift + f * sub
                tiles[d, pl.ds(pl.multiple_of(top * half + at, sub), sub), :] = mine
                tiles[d, pl.ds(pl.multiple_of((1 - top) * half + at, sub), sub), :] = other
    blocks = chips // cores
    for i in range(blocks):
        k = owner_ref[core * blocks + i]
        d = k ^ me

        @pl.when(me <= k)
        def _():
            out[:, i * 128:(i + 1) * 128] = tiles[d]

        @pl.when(me > k)
        def _():
            out[:, i * 128:(i + 1) * 128] = tiles[d].T


def local(three_index, fit_factor, slots, owner):
    tiles = three_index[0]
    count_a, count_s, tile, width = tiles.shape
    orbitals = width // tile
    chips, cores = lax.axis_size("aux"), lax.axis_size("occ")
    lines = chips // PLANE
    rows = tile // 2 // cores
    slices = 2 if rows >= 16 else 1
    sub = rows // slices
    units = chips + 1
    inline = lines + 1
    f32 = jnp.float32

    def go(x, chip=0, core=0):
        if chip:
            return lax.ppermute(x, "aux", [(j, j ^ chip) for j in range(chips)])
        return lax.ppermute(x, "occ", [(j, j ^ core) for j in range(cores)])

    piece = (slices, chips // 2, units, sub, tile)
    any_spec = pl.BlockSpec(memory_space=pl.ANY)
    smem = pl.BlockSpec(memory_space=pltpu.SMEM)
    cfg = (chips, cores, count_a, count_s, orbitals, rows, slices, sub, lines)
    send_s, send_k, keep_s, keep_k = pl.pallas_call(
        functools.partial(pair_kernel, cfg),
        out_shape=[jax.ShapeDtypeStruct((cores - 1,) + piece, f32)] * 2
        + [jax.ShapeDtypeStruct(piece, f32)] * 2,
        in_specs=[smem, smem, any_spec, pl.BlockSpec(memory_space=pltpu.VMEM)],
        out_specs=[any_spec] * 4,
        scratch_shapes=[
            pltpu.VMEM((count_a * count_s, tile, width), jnp.bfloat16),
            pltpu.VMEM((count_s, width, tile), f32),
            pltpu.VMEM((count_s * tile, width), jnp.bfloat16),
            pltpu.VMEM((count_s // 2, 2 * tile, count_s * tile), f32),
            pltpu.VMEM((cores, slices, 2, chips // 2, units, sub, tile), f32),
            pltpu.SMEM((count_a * count_s,), jnp.int32),
            pltpu.SemaphoreType.DMA((count_a * count_s,)),
            pltpu.SemaphoreType.DMA((2 * cores * slices,)),
        ],
        compiler_params=pltpu.CompilerParams(vmem_limit_bytes=56 * 2**20),
        name="pairs",
    )(slots.reshape(-1), owner, tiles, fit_factor)

    got_s = [go(send_s[e - 1], core=e) for e in range(1, cores)]
    got_k = [go(send_k[e - 1], core=e) for e in range(1, cores)]

    def reduced(lo, hi):
        parts = []
        for f in range(slices):
            s = keep_s[f, :, lo:hi] + sum(g[f, :, lo:hi] for g in got_s)
            parts.append(go(s, chip=1 << f))
        nxt = []
        for f in range(slices):
            k = keep_k[f, :, lo:hi] + sum(g[f, :, lo:hi] for g in got_k)
            v = (k + parts[f]).reshape(lines, 2, hi - lo, sub, tile)
            nxt.append((v[:, 0], go(v[:, 1], chip=2 >> f)))
        return [a + b for a, b in nxt]

    pairs = jnp.stack(reduced(inline, units), axis=1)
    line = jnp.stack(reduced(0, inline), axis=1)

    got = [go(pairs[e], chip=e * PLANE) for e in range(1, lines)]
    own = pairs[0] + sum(got)
    own = own.reshape(slices, PLANE - 1, lines, sub, tile)

    def both(e):
        more = [line[e ^ dz, :, 1 + dz] for dz in range(1, lines)]
        return jnp.concatenate([line[e], jnp.stack(more, axis=1)], axis=1)

    got = [go(both(e), chip=e * PLANE) for e in range(1, lines)]
    line = both(0) + sum(got)

    near = [go(own[:, dp - 1], chip=dp) for dp in range(1, PLANE)]
    far = [
        go(jnp.stack([n[:, dz] for n in near]), chip=dz * PLANE) for dz in range(1, lines)
    ]
    near = jnp.stack([n[:, 0] for n in near])
    far = jnp.stack(far)
    mine = [line, own, near, far]
    every = list(mine)
    for e in range(1, cores):
        every += [go(m, core=e) for m in mine]

    vmem = pl.BlockSpec(memory_space=pltpu.VMEM)
    cfg = (chips, cores, rows, slices, sub, lines)
    result = pl.pallas_call(
        functools.partial(place_kernel, cfg),
        out_shape=jax.ShapeDtypeStruct((tile, chips // cores * tile), f32),
        in_specs=[smem] + [vmem] * len(every),
        out_specs=vmem,
        scratch_shapes=[pltpu.VMEM((chips, tile, tile), f32)],
        compiler_params=pltpu.CompilerParams(vmem_limit_bytes=24 * 2**20),
        name="place",
    )(owner, *every)
    return result[None]


def solution(mesh):
    placed = (P("occ", "aux", None, None, None), P("aux", None, None), P("occ", "aux", None), P())
    return jax.shard_map(
        local, mesh=mesh, in_specs=placed, out_specs=P("aux", None, "occ"), check_vma=False
    )
```

time: 429 us -> 111 us (0.26)
  waiting for transfers between devices: 294 us -> 52.5 us
  local copies, waits for them, and re-layouts: 66.8 us -> 1.42 us
  other arithmetic: 26.2 us -> 3.59 us
  Pallas kernels: 0 us -> 21.8 us
  starting transfers between devices: 15.3 us -> 30.7 us
  between operations: 13.5 us -> 0.24 us
  matrix products: 12.5 us -> 0 us
    all_to_all x2 -> x0, waiting for transfers between devices: 235 us -> none  [the longest x1 235 us: local(): lax.all_to_all(send_rows, 'aux', split_axis=0, concat_axis=0, tiled=True)]
    reduce_scatter x1 -> x0, waiting for transfers between devices: 58.6 us -> none  [local(): lax.psum_scatter(owned_rows, 'occ', scatter_dimension=1, tiled=True)]
    ppermute x0 -> x26, waiting for transfers between devices: none -> 52.5 us  [the longest x20 47.6 us: go(): return lax.ppermute(x, 'aux', [(j, j ^ chip) for j in range(chips)])]
    ppermute x0 -> x26, starting transfers between devices: none -> 30.7 us  [the longest x20 29 us: go(): return lax.ppermute(x, 'aux', [(j, j ^ chip) for j in range(chips)])]
    scatter-add x1 -> x0, other arithmetic: 25.3 us -> none  [local(): placed = jnp.zeros((total_blocks, tile_rows, tile_rows), jnp.float32).at[...]
    pallas_call x0 -> x2, Pallas kernels: none -> 21.8 us  [the longest x1 20.2 us: local(): pl.pallas_call(functools.partial(pair_kernel, cfg), out_shape=[jax.ShapeD...]
    scatter x2 -> x0, local copies, waits for them, and re-layouts: 20.7 us -> none  [the longest x1 19.5 us: local(): send_rows = jnp.zeros((groups * capacity, tile_rows, count_s * tile_rows)...]
    all_to_all x2 -> x0, starting transfers between devices: 15.2 us -> none  [the longest x1 8.31 us: local(): lax.all_to_all(send_ids, 'aux', split_axis=0, concat_axis=0, tiled=True)]
  transfers between devices with their start and end apart: 3 -> 26, of which waited for: 2 -> 14; matrix products, arithmetic and copies ran while one was open for 11% -> 3% of each run, Pallas kernels for 0% -> 0%
where the time goes in v1:
time: 111 us; the launch traced here: 110 us
  waiting for transfers between devices  52.5 us (47%)
  starting transfers between devices  30.7 us (28%)
  Pallas kernels  21.8 us (20%)
  other arithmetic  3.59 us (3%)
  local copies, waits for them, and re-layouts  1.42 us (1%)
    ppermute x20, waiting for transfers between devices, go(): return lax.ppermute(x, 'aux', [(j, j ^ chip) for j in range(chips)])  47.6 us
    ppermute x20, starting transfers between devices, go(): return lax.ppermute(x, 'aux', [(j, j ^ chip) for j in range(chips)])  29 us
    pallas_call x1, Pallas kernels, local(): pl.pallas_call(functools.partial(pair_kernel, cfg), out_shape=[jax.ShapeD...  20.2 us
    ppermute x6, waiting for transfers between devices, go(): return lax.ppermute(x, 'occ', [(j, j ^ core) for j in range(cores)])  4.93 us
    add x2, other arithmetic, reduced(): s = keep_s[f, :, lo:hi] + sum((g[f, :, lo:hi] for g in got_s))  2.74 us
  transfers between devices with their start and end apart: 26, of which 14 were waited for; matrix products, arithmetic and copies ran while one was open for 3% of the time, Pallas kernels for 0%

profile of v1, /device:TPU:0, one launch (start us, length us, event | category | flops | bytes accessed | tf_op | source)
XLA Modules:
  0.0 110.2 jit_solution(4350945316149578879)
XLA Ops:
  0.0 1.3 %reshape.26.slots_ref = s32[24]{0:T(128)} reshape(s32[1,4,6]{2,1,0:T(4,128)} %param.6) | data formatting | bytes 192 | tf_op jit(solution)/shard_map/reshape | solution.py:164
  1.3 20.2 %pairs.1 = (f32[1,2,8,17,16,128]{5,4,3,2,1,0:T(8,128)}, f32[1,2,8,17,16,128]{5,4,3,2,1,0:T(8,128)}, f32[2,8,17,16,128]{4,3,2,1,0:T(8,128)}, f32[2,8,17,16,128]{4,3,2,1,0:T(8,128)}) custom-call(s32[24]{0:T(128)} %reshape.26.slots_ref, s32[16]{0:T(128)} %owner_ref.3, bf16[4,6,128,1024]{3,2,1,0:T(8,128)(2,1)} %bitcast.168, bf16[4,128,128]{2,1,0:T(8,128)(2,1)} %fit_ref.1), custom_call_target="tpu_custom_call" | custom-call | tf_op jit(solution)/shard_map/pairs/pallas_call | solution.py:146
  22.1 4.0 %collective-permute-done.1 = f32[2,8,17,16,128]{4,3,2,1,0:T(8,128)S(1)} collective-permute-done((f32[2,8,17,16,128]{4,3,2,1,0:T(8,128)}, f32[2,8,17,16,128]{4,3,2,1,0:T(8,128)S(1)}, u32[]{:S(2)}, u32[]{:S(2)}) %collective-permute-start.1) | collective-permute-done | bytes 2228256 | tf_op jit(solution)/shard_map/ppermute | solution.py:140
  26.2 1.2 %fusion.13 = (f32[8,5,16,128]{3,2,1,0:T(8,128)S(1)}, f32[8,5,16,128]{3,2,1,0:T(8,128)S(1)}) fusion(f32[2,8,17,16,128]{4,3,2,1,0:T(8,128)S(1)} %collective-permute-done.1, f32[2,8,17,16,128]{4,3,2,1,0:T(8,128)} %get-tuple-element.11), kind=kLoop, calls=%fused_computation.60 | loop fusion | flops 163840 | bytes 1966080 | tf_op jit(solution)/shard_map/add | solution.py:172
  27.3 3.0 %collective-permute-start.2 = (f32[8,5,16,128]{3,2,1,0:T(8,128)S(1)}, f32[8,5,16,128]{3,2,1,0:T(8,128)S(1)}, u32[]{:S(2)}, u32[]{:S(2)}) collective-permute-start(f32[8,5,16,128]{3,2,1,0:T(8,128)S(1)} %get-tuple-element.19), channel_id=1, source_target_pairs={{0,2},{2,0},{4,6},{6,4},{8,10},{10,8},{12,14},{14,12},{16,18},{18,... | collective-permute-start | bytes 983048 | tf_op jit(solution)/shard_map/ppermute | solution.py:139
  31.5 1.6 %fusion = (f32[8,12,16,128]{3,2,1,0:T(8,128)S(1)}, f32[8,12,16,128]{3,2,1,0:T(8,128)S(1)}) fusion(f32[2,8,17,16,128]{4,3,2,1,0:T(8,128)S(1)} %collective-permute-done.1, f32[2,8,17,16,128]{4,3,2,1,0:T(8,128)} %get-tuple-element.11), kind=kLoop, calls=%fused_computation.37 | loop fusion | flops 393216 | bytes 4718592 | tf_op jit(solution)/shard_map/add | solution.py:172
  34.3 4.5 %collective-permute-done.2 = f32[8,5,16,128]{3,2,1,0:T(8,128)S(1)} collective-permute-done((f32[8,5,16,128]{3,2,1,0:T(8,128)S(1)}, f32[8,5,16,128]{3,2,1,0:T(8,128)S(1)}, u32[]{:S(2)}, u32[]{:S(2)}) %collective-permute-start.2) | collective-permute-done | bytes 327712 | tf_op jit(solution)/shard_map/ppermute | solution.py:139
  38.8 2.1 %collective-permute-done.4 = f32[8,5,16,128]{3,2,1,0:T(8,128)S(1)} collective-permute-done((f32[8,5,16,128]{3,2,1,0:T(8,128)S(1)}, f32[8,5,16,128]{3,2,1,0:T(8,128)S(1)}, u32[]{:S(2)}, u32[]{:S(2)}) %collective-permute-start.4) | collective-permute-done | bytes 327712 | tf_op jit(solution)/shard_map/ppermute | solution.py:139
  41.1 1.2 %collective-permute-start.3 = (f32[4,5,16,128]{3,2,1,0:T(8,128)S(1)}, f32[4,5,16,128]{3,2,1,0:T(8,128)S(1)}, u32[]{:S(2)}, u32[]{:S(2)}) collective-permute-start(f32[4,5,16,128]{3,2,1,0:T(8,128)S(1)} %slice_bitcast_fusion.6), channel_id=1, source_target_pairs={{0,4},{2,6},{4,0},{6,2},{8,12},{10,14},{12,8},{14,10},{16,20},{18,... | collective-permute-start | bytes 491528 | tf_op jit(solution)/shard_map/ppermute | solution.py:139
  42.9 17.3 %collective-permute-done.3 = f32[4,5,16,128]{3,2,1,0:T(8,128)S(1)} collective-permute-done((f32[4,5,16,128]{3,2,1,0:T(8,128)S(1)}, f32[4,5,16,128]{3,2,1,0:T(8,128)S(1)}, u32[]{:S(2)}, u32[]{:S(2)}) %collective-permute-start.3) | collective-permute-done | bytes 163872 | tf_op jit(solution)/shard_map/ppermute | solution.py:139
  61.1 1.4 %collective-permute-start.10 = (f32[4,12,16,128]{3,2,1,0:T(8,128)S(1)}, f32[4,12,16,128]{3,2,1,0:T(8,128)S(1)}, u32[]{:S(2)}, u32[]{:S(2)}) collective-permute-start(f32[4,12,16,128]{3,2,1,0:T(8,128)S(1)} %slice_bitcast_fusion.2), channel_id=1, source_target_pairs={{0,4},{2,6},{4,0},{6,2},{8,12},{10,14},{12,8},{14,10},{16,20},{18,... | collective-permute-start | bytes 1179656 | tf_op jit(solution)/shard_map/ppermute | solution.py:139
  62.6 3.6 %collective-permute-start.8 = (f32[2,8,16,128]{3,2,1,0:T(8,128)S(1)}, f32[2,8,16,128]{3,2,1,0:T(8,128)S(1)}, u32[]{:S(2)}, u32[]{:S(2)}) collective-permute-start(f32[2,8,16,128]{3,2,1,0:T(8,128)S(1)} %pad_maximum_fusion.5), channel_id=1, source_target_pairs={{0,24},{2,26},{4,28},{6,30},{8,16},{10,18},{12,20},{14,22},{16,8},... | collective-permute-start | bytes 393224 | tf_op jit(solution)/shard_map/ppermute | solution.py:139
  66.2 4.5 %collective-permute-done.12 = f32[4,12,16,128]{3,2,1,0:T(8,128)S(1)} collective-permute-done((f32[4,12,16,128]{3,2,1,0:T(8,128)S(1)}, f32[4,12,16,128]{3,2,1,0:T(8,128)S(1)}, u32[]{:S(2)}, u32[]{:S(2)}) %collective-permute-start.12) | collective-permute-done | bytes 393248 | tf_op jit(solution)/shard_map/ppermute | solution.py:139
  71.3 2.4 %collective-permute-start.14 = (f32[2,12,16,128]{3,2,0,1:T(8,128)S(1)}, f32[2,12,16,128]{3,2,0,1:T(8,128)S(1)}, u32[]{:S(2)}, u32[]{:S(2)}) collective-permute-start(f32[2,12,16,128]{3,2,0,1:T(8,128)S(1)} %get-tuple-element.21), channel_id=1, source_target_pairs={{0,16},{2,18},{4,20},{6,22},{8,24},{10,26},{12,28},{14,30},{16,0},... | collective-permute-start | bytes 589832 | tf_op jit(solution)/shard_map/ppermute | solution.py:139
  73.8 1.7 %collective-permute-start.13 = (f32[2,12,16,128]{3,2,0,1:T(8,128)S(1)}, f32[2,12,16,128]{3,2,0,1:T(8,128)S(1)}, u32[]{:S(2)}, u32[]{:S(2)}) collective-permute-start(f32[2,12,16,128]{3,2,0,1:T(8,128)S(1)} %get-tuple-element.22), channel_id=1, source_target_pairs={{0,8},{2,10},{4,12},{6,14},{8,0},{10,2},{12,4},{14,6},{16,24},{18,... | collective-permute-start | bytes 589832 | tf_op jit(solution)/shard_map/ppermute | solution.py:139
  76.3 8.1 %collective-permute-done.14 = f32[2,12,16,128]{3,2,0,1:T(8,128)S(1)} collective-permute-done((f32[2,12,16,128]{3,2,0,1:T(8,128)S(1)}, f32[2,12,16,128]{3,2,0,1:T(8,128)S(1)}, u32[]{:S(2)}, u32[]{:S(2)}) %collective-permute-start.14) | collective-permute-done | bytes 196640 | tf_op jit(solution)/shard_map/ppermute | solution.py:139
  85.2 2.6 %collective-permute-done.15 = f32[2,12,16,128]{3,2,0,1:T(8,128)S(1)} collective-permute-done((f32[2,12,16,128]{3,2,0,1:T(8,128)S(1)}, f32[2,12,16,128]{3,2,0,1:T(8,128)S(1)}, u32[]{:S(2)}, u32[]{:S(2)}) %collective-permute-start.15) | collective-permute-done | bytes 196640 | tf_op jit(solution)/shard_map/ppermute | solution.py:139
  87.9 1.5 %collective-permute-start.16 = (f32[2,4,16,128]{3,2,0,1:T(8,128)S(1)}, f32[2,4,16,128]{3,2,0,1:T(8,128)S(1)}, u32[]{:S(2)}, u32[]{:S(2)}) collective-permute-start(f32[2,4,16,128]{3,2,0,1:T(8,128)S(1)} %get-tuple-element.40), channel_id=1, source_target_pairs={{0,2},{2,0},{4,6},{6,4},{8,10},{10,8},{12,14},{14,12},{16,18},{18,... | collective-permute-start | bytes 196616 | tf_op jit(solution)/shard_map/ppermute | solution.py:139
  89.4 4.1 %collective-permute-start.7 = (f32[2,8,16,128]{3,2,0,1:T(8,128)S(1)}, f32[2,8,16,128]{3,2,0,1:T(8,128)S(1)}, u32[]{:S(2)}, u32[]{:S(2)}) collective-permute-start(f32[2,8,16,128]{3,2,0,1:T(8,128)S(1)} %pad_maximum_fusion.4), channel_id=1, source_target_pairs={{0,16},{2,18},{4,20},{6,22},{8,24},{10,26},{12,28},{14,30},{16,0},... | collective-permute-start | bytes 393224 | tf_op jit(solution)/shard_map/ppermute | solution.py:139
  93.4 1.5 %collective-permute-start.18 = (f32[2,4,16,128]{3,2,0,1:T(8,128)S(1)}, f32[2,4,16,128]{3,2,0,1:T(8,128)S(1)}, u32[]{:S(2)}, u32[]{:S(2)}) collective-permute-start(f32[2,4,16,128]{3,2,0,1:T(8,128)S(1)} %get-tuple-element.41), channel_id=1, source_target_pairs={{0,6},{2,4},{4,2},{6,0},{8,14},{10,12},{12,10},{14,8},{16,22},{18,... | collective-permute-start | bytes 196616 | tf_op jit(solution)/shard_map/ppermute | solution.py:139
  95.6 3.0 %collective-permute-done.18 = f32[2,4,16,128]{3,2,0,1:T(8,128)S(1)} collective-permute-done((f32[2,4,16,128]{3,2,0,1:T(8,128)S(1)}, f32[2,4,16,128]{3,2,0,1:T(8,128)S(1)}, u32[]{:S(2)}, u32[]{:S(2)}) %collective-permute-start.18) | collective-permute-done | bytes 65568 | tf_op jit(solution)/shard_map/ppermute | solution.py:139
  99.3 1.9 %collective-permute-start.20 = (f32[3,2,16,128]{3,2,1,0:T(8,128)S(1)}, f32[3,2,16,128]{3,2,1,0:T(8,128)S(1)}, u32[]{:S(2)}, u32[]{:S(2)}) collective-permute-start(f32[3,2,16,128]{3,2,1,0:T(8,128)S(1)} %pad_maximum_fusion.8), channel_id=1, source_target_pairs={{0,16},{2,18},{4,20},{6,22},{8,24},{10,26},{12,28},{14,30},{16,0},... | collective-permute-start | bytes 147464 | tf_op jit(solution)/shard_map/ppermute | solution.py:139
  104.7 2.4 %collective-permute-done.21 = f32[3,2,16,128]{3,2,1,0:T(8,128)S(1)} collective-permute-done((f32[3,2,16,128]{3,2,1,0:T(8,128)S(1)}, f32[3,2,16,128]{3,2,1,0:T(8,128)S(1)}, u32[]{:S(2)}, u32[]{:S(2)}) %collective-permute-start.21) | collective-permute-done | bytes 49184 | tf_op jit(solution)/shard_map/ppermute | solution.py:139
  108.6 1.6 %place.1 = f32[128,1024]{1,0:T(8,128)} custom-call(s32[16]{0:T(128)S(1)} %copy-done, f32[2,8,16,128]{3,2,1,0:T(8,128)S(1)} %copy_add_fusion.refs_0_, f32[2,3,4,16,128]{4,3,2,1,0:T(8,128)S(1)} %copy.29.refs_1_, f32[3,2,16,128]{3,2,1,0:T(8,128)S(1)} %pad_maximum_fusion.6.refs_2_, f32[3,3,2,16,128]{4,3,2,1,0:T(8,128)S(1)} %pad_maximum_fusion.1.refs_3_, ...), custom_call_target="tpu_custom_call" | custom-call | tf_op jit(solution)/shard_map/place/pallas_call | solution.py:208
  (67 shorter events, 13.3 us)
Async XLA Ops:
  21.5 4.6 %collective-permute-start.1 = (f32[2,8,17,16,128]{4,3,2,1,0:T(8,128)}, f32[2,8,17,16,128]{4,3,2,1,0:T(8,128)S(1)}, u32[]{:S(2)}, u32[]{:S(2)}) collective-permute-start(f32[2,8,17,16,128]{4,3,2,1,0:T(8,128)} %bitcast.184), channel_id=1, source_target_pairs={{0,1},{1,0},{2,3},{3,2},{4,5},{5,4},{6,7},{7,6},{8,9},{9,8},{10,11... | collective-permute-start | bytes 6684680 | tf_op jit(solution)/shard_map/ppermute | solution.py:140
  22.0 12.3 %collective-permute-start = (f32[2,8,17,16,128]{4,3,2,1,0:T(8,128)}, f32[2,8,17,16,128]{4,3,2,1,0:T(8,128)S(1)}, u32[]{:S(2)}, u32[]{:S(2)}) collective-permute-start(f32[2,8,17,16,128]{4,3,2,1,0:T(8,128)} %bitcast.183), channel_id=1, source_target_pairs={{0,1},{1,0},{2,3},{3,2},{4,5},{5,4},{6,7},{7,6},{8,9},{9,8},{10,11... | collective-permute-start | bytes 6684680 | tf_op jit(solution)/shard_map/ppermute | solution.py:140
  27.3 11.5 %collective-permute-start.2 = (f32[8,5,16,128]{3,2,1,0:T(8,128)S(1)}, f32[8,5,16,128]{3,2,1,0:T(8,128)S(1)}, u32[]{:S(2)}, u32[]{:S(2)}) collective-permute-start(f32[8,5,16,128]{3,2,1,0:T(8,128)S(1)} %get-tuple-element.19), channel_id=1, source_target_pairs={{0,2},{2,0},{4,6},{6,4},{8,10},{10,8},{12,14},{14,12},{16,18},{18,... | collective-permute-start | bytes 983048 | tf_op jit(solution)/shard_map/ppermute | solution.py:139
  30.3 10.6 %collective-permute-start.4 = (f32[8,5,16,128]{3,2,1,0:T(8,128)S(1)}, f32[8,5,16,128]{3,2,1,0:T(8,128)S(1)}, u32[]{:S(2)}, u32[]{:S(2)}) collective-permute-start(f32[8,5,16,128]{3,2,1,0:T(8,128)S(1)} %get-tuple-element.20), channel_id=1, source_target_pairs={{0,4},{2,6},{4,0},{6,2},{8,12},{10,14},{12,8},{14,10},{16,20},{18,... | collective-permute-start | bytes 983048 | tf_op jit(solution)/shard_map/ppermute | solution.py:139
  33.0 27.2 %collective-permute-start.11 = (f32[8,12,16,128]{3,2,1,0:T(8,128)S(1)}, f32[8,12,16,128]{3,2,1,0:T(8,128)S(1)}, u32[]{:S(2)}, u32[]{:S(2)}) collective-permute-start(f32[8,12,16,128]{3,2,1,0:T(8,128)S(1)} %get-tuple-element.15), channel_id=1, source_target_pairs={{0,4},{2,6},{4,0},{6,2},{8,12},{10,14},{12,8},{14,10},{16,20},{18,... | collective-permute-start | bytes 2359304 | tf_op jit(solution)/shard_map/ppermute | solution.py:139
  34.0 26.3 %collective-permute-start.9 = (f32[8,12,16,128]{3,2,1,0:T(8,128)S(1)}, f32[8,12,16,128]{3,2,1,0:T(8,128)S(1)}, u32[]{:S(2)}, u32[]{:S(2)}) collective-permute-start(f32[8,12,16,128]{3,2,1,0:T(8,128)S(1)} %get-tuple-element.16), channel_id=1, source_target_pairs={{0,2},{2,0},{4,6},{6,4},{8,10},{10,8},{12,14},{14,12},{16,18},{18,... | collective-permute-start | bytes 2359304 | tf_op jit(solution)/shard_map/ppermute | solution.py:139
  41.1 19.1 %collective-permute-start.3 = (f32[4,5,16,128]{3,2,1,0:T(8,128)S(1)}, f32[4,5,16,128]{3,2,1,0:T(8,128)S(1)}, u32[]{:S(2)}, u32[]{:S(2)}) collective-permute-start(f32[4,5,16,128]{3,2,1,0:T(8,128)S(1)} %slice_bitcast_fusion.6), channel_id=1, source_target_pairs={{0,4},{2,6},{4,0},{6,2},{8,12},{10,14},{12,8},{14,10},{16,20},{18,... | collective-permute-start | bytes 491528 | tf_op jit(solution)/shard_map/ppermute | solution.py:139
  42.3 17.9 %collective-permute-start.5 = (f32[4,5,16,128]{3,2,1,0:T(8,128)S(1)}, f32[4,5,16,128]{3,2,1,0:T(8,128)S(1)}, u32[]{:S(2)}, u32[]{:S(2)}) collective-permute-start(f32[4,5,16,128]{3,2,1,0:T(8,128)S(1)} %slice_bitcast_fusion.4), channel_id=1, source_target_pairs={{0,2},{2,0},{4,6},{6,4},{8,10},{10,8},{12,14},{14,12},{16,18},{18,... | collective-permute-start | bytes 491528 | tf_op jit(solution)/shard_map/ppermute | solution.py:139
  60.7 10.1 %collective-permute-start.12 = (f32[4,12,16,128]{3,2,1,0:T(8,128)S(1)}, f32[4,12,16,128]{3,2,1,0:T(8,128)S(1)}, u32[]{:S(2)}, u32[]{:S(2)}) collective-permute-start(f32[4,12,16,128]{3,2,1,0:T(8,128)S(1)} %slice_bitcast_fusion), channel_id=1, source_target_pairs={{0,2},{2,0},{4,6},{6,4},{8,10},{10,8},{12,14},{14,12},{16,18},{18,... | collective-permute-start | bytes 1179656 | tf_op jit(solution)/shard_map/ppermute | solution.py:139
  61.1 10.1 %collective-permute-start.10 = (f32[4,12,16,128]{3,2,1,0:T(8,128)S(1)}, f32[4,12,16,128]{3,2,1,0:T(8,128)S(1)}, u32[]{:S(2)}, u32[]{:S(2)}) collective-permute-start(f32[4,12,16,128]{3,2,1,0:T(8,128)S(1)} %slice_bitcast_fusion.2), channel_id=1, source_target_pairs={{0,4},{2,6},{4,0},{6,2},{8,12},{10,14},{12,8},{14,10},{16,20},{18,... | collective-permute-start | bytes 1179656 | tf_op jit(solution)/shard_map/ppermute | solution.py:139
  62.6 39.5 %collective-permute-start.8 = (f32[2,8,16,128]{3,2,1,0:T(8,128)S(1)}, f32[2,8,16,128]{3,2,1,0:T(8,128)S(1)}, u32[]{:S(2)}, u32[]{:S(2)}) collective-permute-start(f32[2,8,16,128]{3,2,1,0:T(8,128)S(1)} %pad_maximum_fusion.5), channel_id=1, source_target_pairs={{0,24},{2,26},{4,28},{6,30},{8,16},{10,18},{12,20},{14,22},{16,8},... | collective-permute-start | bytes 393224 | tf_op jit(solution)/shard_map/ppermute | solution.py:139
  71.3 13.0 %collective-permute-start.14 = (f32[2,12,16,128]{3,2,0,1:T(8,128)S(1)}, f32[2,12,16,128]{3,2,0,1:T(8,128)S(1)}, u32[]{:S(2)}, u32[]{:S(2)}) collective-permute-start(f32[2,12,16,128]{3,2,0,1:T(8,128)S(1)} %get-tuple-element.21), channel_id=1, source_target_pairs={{0,16},{2,18},{4,20},{6,22},{8,24},{10,26},{12,28},{14,30},{16,0},... | collective-permute-start | bytes 589832 | tf_op jit(solution)/shard_map/ppermute | solution.py:139
  73.8 11.5 %collective-permute-start.13 = (f32[2,12,16,128]{3,2,0,1:T(8,128)S(1)}, f32[2,12,16,128]{3,2,0,1:T(8,128)S(1)}, u32[]{:S(2)}, u32[]{:S(2)}) collective-permute-start(f32[2,12,16,128]{3,2,0,1:T(8,128)S(1)} %get-tuple-element.22), channel_id=1, source_target_pairs={{0,8},{2,10},{4,12},{6,14},{8,0},{10,2},{12,4},{14,6},{16,24},{18,... | collective-permute-start | bytes 589832 | tf_op jit(solution)/shard_map/ppermute | solution.py:139
  75.4 12.4 %collective-permute-start.15 = (f32[2,12,16,128]{3,2,0,1:T(8,128)S(1)}, f32[2,12,16,128]{3,2,0,1:T(8,128)S(1)}, u32[]{:S(2)}, u32[]{:S(2)}) collective-permute-start(f32[2,12,16,128]{3,2,0,1:T(8,128)S(1)} %get-tuple-element.23), channel_id=1, source_target_pairs={{0,24},{2,26},{4,28},{6,30},{8,16},{10,18},{12,20},{14,22},{16,8},... | collective-permute-start | bytes 589832 | tf_op jit(solution)/shard_map/ppermute | solution.py:139
  75.8 27.1 %collective-permute-start.6 = (f32[2,8,16,128]{3,2,0,1:T(8,128)S(1)}, f32[2,8,16,128]{3,2,0,1:T(8,128)S(1)}, u32[]{:S(2)}, u32[]{:S(2)}) collective-permute-start(f32[2,8,16,128]{3,2,0,1:T(8,128)S(1)} %pad_maximum_fusion.3), channel_id=1, source_target_pairs={{0,8},{2,10},{4,12},{6,14},{8,0},{10,2},{12,4},{14,6},{16,24},{18,... | collective-permute-start | bytes 393224 | tf_op jit(solution)/shard_map/ppermute | solution.py:139
  87.9 7.1 %collective-permute-start.16 = (f32[2,4,16,128]{3,2,0,1:T(8,128)S(1)}, f32[2,4,16,128]{3,2,0,1:T(8,128)S(1)}, u32[]{:S(2)}, u32[]{:S(2)}) collective-permute-start(f32[2,4,16,128]{3,2,0,1:T(8,128)S(1)} %get-tuple-element.40), channel_id=1, source_target_pairs={{0,2},{2,0},{4,6},{6,4},{8,10},{10,8},{12,14},{14,12},{16,18},{18,... | collective-permute-start | bytes 196616 | tf_op jit(solution)/shard_map/ppermute | solution.py:139
  89.4 13.6 %collective-permute-start.7 = (f32[2,8,16,128]{3,2,0,1:T(8,128)S(1)}, f32[2,8,16,128]{3,2,0,1:T(8,128)S(1)}, u32[]{:S(2)}, u32[]{:S(2)}) collective-permute-start(f32[2,8,16,128]{3,2,0,1:T(8,128)S(1)} %pad_maximum_fusion.4), channel_id=1, source_target_pairs={{0,16},{2,18},{4,20},{6,22},{8,24},{10,26},{12,28},{14,30},{16,0},... | collective-permute-start | bytes 393224 | tf_op jit(solution)/shard_map/ppermute | solution.py:139
  93.4 5.2 %collective-permute-start.18 = (f32[2,4,16,128]{3,2,0,1:T(8,128)S(1)}, f32[2,4,16,128]{3,2,0,1:T(8,128)S(1)}, u32[]{:S(2)}, u32[]{:S(2)}) collective-permute-start(f32[2,4,16,128]{3,2,0,1:T(8,128)S(1)} %get-tuple-element.41), channel_id=1, source_target_pairs={{0,6},{2,4},{4,2},{6,0},{8,14},{10,12},{12,10},{14,8},{16,22},{18,... | collective-permute-start | bytes 196616 | tf_op jit(solution)/shard_map/ppermute | solution.py:139
  95.0 4.3 %collective-permute-start.17 = (f32[2,4,16,128]{3,2,0,1:T(8,128)S(1)}, f32[2,4,16,128]{3,2,0,1:T(8,128)S(1)}, u32[]{:S(2)}, u32[]{:S(2)}) collective-permute-start(f32[2,4,16,128]{3,2,0,1:T(8,128)S(1)} %get-tuple-element.42), channel_id=1, source_target_pairs={{0,4},{2,6},{4,0},{6,2},{8,12},{10,14},{12,8},{14,10},{16,20},{18,... | collective-permute-start | bytes 196616 | tf_op jit(solution)/shard_map/ppermute | solution.py:139
  99.3 5.4 %collective-permute-start.20 = (f32[3,2,16,128]{3,2,1,0:T(8,128)S(1)}, f32[3,2,16,128]{3,2,1,0:T(8,128)S(1)}, u32[]{:S(2)}, u32[]{:S(2)}) collective-permute-start(f32[3,2,16,128]{3,2,1,0:T(8,128)S(1)} %pad_maximum_fusion.8), channel_id=1, source_target_pairs={{0,16},{2,18},{4,20},{6,22},{8,24},{10,26},{12,28},{14,30},{16,0},... | collective-permute-start | bytes 147464 | tf_op jit(solution)/shard_map/ppermute | solution.py:139
  101.2 5.9 %collective-permute-start.21 = (f32[3,2,16,128]{3,2,1,0:T(8,128)S(1)}, f32[3,2,16,128]{3,2,1,0:T(8,128)S(1)}, u32[]{:S(2)}, u32[]{:S(2)}) collective-permute-start(f32[3,2,16,128]{3,2,1,0:T(8,128)S(1)} %pad_maximum_fusion.9), channel_id=1, source_target_pairs={{0,24},{2,26},{4,28},{6,30},{8,16},{10,18},{12,20},{14,22},{16,8},... | collective-permute-start | bytes 147464 | tf_op jit(solution)/shard_map/ppermute | solution.py:139
  102.1 5.0 %collective-permute-start.19 = (f32[3,2,16,128]{3,2,1,0:T(8,128)S(1)}, f32[3,2,16,128]{3,2,1,0:T(8,128)S(1)}, u32[]{:S(2)}, u32[]{:S(2)}) collective-permute-start(f32[3,2,16,128]{3,2,1,0:T(8,128)S(1)} %pad_maximum_fusion.7), channel_id=1, source_target_pairs={{0,8},{2,10},{4,12},{6,14},{8,0},{10,2},{12,4},{14,6},{16,24},{18,... | collective-permute-start | bytes 147464 | tf_op jit(solution)/shard_map/ppermute | solution.py:139
  103.0 4.8 %collective-permute-start.22 = (f32[2,8,16,128]{3,2,1,0:T(8,128)S(1)}, f32[2,8,16,128]{3,2,1,0:T(8,128)S(1)}, u32[]{:S(2)}, u32[]{:S(2)}) collective-permute-start(f32[2,8,16,128]{3,2,1,0:T(8,128)S(1)} %copy_add_fusion.refs_0_), channel_id=1, source_target_pairs={{0,1},{1,0},{2,3},{3,2},{4,5},{5,4},{6,7},{7,6},{8,9},{9,8},{10,11... | collective-permute-start | bytes 393224 | tf_op jit(solution)/shard_map/ppermute | solution.py:140
  103.1 4.7 %collective-permute-start.23 = (f32[2,3,4,16,128]{4,3,0,2,1:T(8,128)S(1)}, f32[2,3,4,16,128]{4,3,0,2,1:T(8,128)S(1)}, u32[]{:S(2)}, u32[]{:S(2)}) collective-permute-start(f32[2,3,4,16,128]{4,3,0,2,1:T(8,128)S(1)} %bitcast.174), channel_id=1, source_target_pairs={{0,1},{1,0},{2,3},{3,2},{4,5},{5,4},{6,7},{7,6},{8,9},{9,8},{10,11... | collective-permute-start | bytes 589832 | tf_op jit(solution)/shard_map/ppermute | solution.py:140
  (4 other events, 46.3 us)

commit v2 on v0

v2 whole, which is shorter than its diff:
```python
import functools

import jax
import jax.numpy as jnp
import numpy as np
from jax import lax
from jax.experimental import pallas as pl
from jax.experimental.pallas import tpu as pltpu
from jax.sharding import PartitionSpec as P

PLANE = 4


class Sizes:
    def __init__(self, chips, cores, tile):
        self.chips, self.cores = chips, cores
        self.lines = chips // PLANE
        self.rows = tile // 2 // cores
        self.bits = chips.bit_length() - 1
        self.count = {
            "cross": (PLANE - 1) * (self.lines - 1), "plane": PLANE - 1, "line": self.lines + 1,
        }
        self.at, total = {}, 0
        for half in ("s", "k"):
            for name, n in self.count.items():
                size = chips // 2 * n * self.rows
                self.at[name, half] = (total, total + size)
                total += size
        self.sent, self.total = total // 2, total

    def order(self, name, core):
        low, high = [0, 1], list(range(2, self.bits))
        if core % 2:
            low, high = low[::-1], high[::-1]
        return high + low if name == "line" else low + high

    def table(self):
        out = np.zeros((self.chips, self.chips + 1, 2), np.int32)
        for j in range(self.chips):
            for unit in range(self.chips + 1):
                dz, dp = (unit // PLANE, unit % PLANE) if unit < self.chips else (-1, 0)
                if dp == 0:
                    name, i = "line", 1 + dz
                elif dz == 0:
                    name, i = "plane", dp - 1
                else:
                    name, i = "cross", (dp - 1) * (self.lines - 1) + dz - 1
                for parity in range(2):
                    place = 0
                    at = j ^ dp if name == "cross" else j
                    for bit in self.order(name, parity):
                        place = 2 * place + (at >> bit & 1)
                    half = self.chips // 2
                    base = self.at[name, "s" if place >= half else "k"][0]
                    place = (place % half) * self.count[name] + i
                    out[j, unit, parity] = base + place * self.rows
        return out.reshape(-1)


def pair_kernel(
    sz, slots_hbm, owner_hbm, table_hbm, x_ref, fit_hbm, keep, send,
    xbuf, both, gbuf, fbuf, res, fit_ref, slots_ref, owner_ref, table_ref, ranked, insem, smallsem,
):
    _, count_a, count_s, tile, width = x_ref.shape
    orbitals = width // tile
    me = lax.axis_index("aux")
    core = lax.axis_index("occ")
    half = tile // 2
    small = [
        pltpu.make_async_copy(a, b, smallsem.at[i]) for i, (a, b) in enumerate([
            (slots_hbm, slots_ref), (owner_hbm, owner_ref), (fit_hbm, fit_ref),
            (table_hbm, table_ref),
        ])
    ]
    for c in small:
        c.start()
    small[0].wait()
    small[1].wait()
    for a in range(count_a):
        own = [owner_ref[slots_ref[0, a, s]] for s in range(count_s)]
        for s in range(count_s):
            rank = jnp.int32(0)
            for t in range(count_s):
                if t != s:
                    rank = rank + (own[t] < own[s]).astype(jnp.int32)
            place = a * count_s + rank
            ranked[place] = own[s]
            pltpu.make_async_copy(
                x_ref.at[0, a, s], xbuf.at[pl.ds(pl.multiple_of(place * tile, tile), tile)],
                insem.at[place],
            ).start()
    keep[...] = jnp.zeros_like(keep)
    send[...] = jnp.zeros_like(send)
    both[...] = jnp.zeros_like(both)
    wide = 2 * tile
    span = wide // orbitals
    to = lax.broadcasted_iota(jnp.int32, (wide, wide), 0)
    of = lax.broadcasted_iota(jnp.int32, (wide, wide), 1)
    perm = (of == (to % span) * orbitals + to // span).astype(jnp.float32).astype(jnp.bfloat16)
    nt = (((1,), (1,)), ((), ()))
    small[2].wait()
    small[3].wait()

    def tiles_of(a):
        base = a * count_s
        slot = lax.rem(a, 2)
        both[:tile, :tile] = fit_ref[a]
        both[tile:, tile:] = fit_ref[a]
        for p in range(count_s):
            pltpu.make_async_copy(
                x_ref.at[0, a, p],
                xbuf.at[pl.ds(pl.multiple_of((base + p) * tile, tile), tile)],
                insem.at[base + p],
            ).wait()
        for g in range(0, count_s, 2):
            at = pl.multiple_of((base + g) * tile, tile)
            for b in range(width // wide):
                gbuf[g // 2, b * wide:(b + 1) * wide, :] = lax.dot_general(
                    perm, xbuf[pl.ds(at, wide), b * wide:(b + 1) * wide], nt,
                    preferred_element_type=jnp.float32,
                ).astype(jnp.bfloat16)
                yield
            for b in range(width // wide):
                fitted = lax.dot_general(
                    gbuf[g // 2, b * wide:(b + 1) * wide, :], both[...], nt,
                    preferred_element_type=jnp.float32,
                ).astype(jnp.bfloat16)
                for t in range(2):
                    top = (g + t) * tile + b * span
                    for i in range(orbitals):
                        fbuf[top:top + span, i * tile:(i + 1) * tile] = fitted[
                            i * span:(i + 1) * span, t * tile:(t + 1) * tile
                        ]
                yield
        for g in range(0, count_s, 2):
            res[slot, g // 2, :(g + 2) * tile, :] = lax.dot_general(
                fbuf[:(g + 2) * tile, :], fbuf[g * tile:(g + 2) * tile, :], nt,
                preferred_element_type=jnp.float32,
            )
            yield

    def add(a, p, q):
        base = a * count_s
        slot = lax.rem(a, 2)
        first, second = ranked[base + p], ranked[base + q]
        d = first ^ second
        todo = []
        for h in range(2):
            jr = (second if h else first) ^ me
            unit = sz.chips if (h and p == q) else d
            entry = (jr * (sz.chips + 1) + unit) * 2
            for o in range(sz.cores):
                of_core = o ^ core
                row = pl.multiple_of(table_ref[entry + (of_core & 1)], sz.rows)
                where = pl.ds(row, sz.rows)
                at = pl.multiple_of(p * tile + h * half + of_core * sz.rows, sz.rows)
                new = res[
                    slot, q // 2, pl.ds(at, sz.rows), (q % 2) * tile:(q % 2 + 1) * tile
                ]
                old = send[o - 1, where, :] if o else keep[where, :]
                todo.append((o, where, old + new))
        for o, where, value in todo:
            if o:
                send[o - 1, where, :] = value
            else:
                keep[where, :] = value

    pairs = [(p, q) for p in range(count_s) for q in range(p, count_s)]

    def both_of(a, carry):
        left = list(pairs)
        for _ in tiles_of(a):
            if left:
                add(a - 1, *left.pop())
        while left:
            add(a - 1, *left.pop())
        return carry

    for _ in tiles_of(jnp.int32(0)):
        pass
    lax.fori_loop(1, count_a, both_of, 0)
    for p, q in pairs:
        add(jnp.int32(count_a - 1), p, q)


def place_kernel(sz, owner_ref, *refs):
    out, tiles = refs[-2], refs[-1]
    refs = refs[:-2]
    me = lax.axis_index("aux")
    core = lax.axis_index("occ")
    tile = out.shape[0]
    half = tile // 2
    n_plane = sz.count["plane"]
    for o in range(sz.cores):
        own, far = refs[2 * o:2 * o + 2]
        shift = (o ^ core) * sz.rows
        for d in range(sz.chips):
            dp, dz = d % PLANE, d // PLANE
            if dp == 0:
                mine = own[n_plane + 1 + dz]
            elif dz == 0:
                mine = own[dp - 1]
            else:
                mine = far[(dp - 1) * sz.lines + dz]
            if d == 0:
                other = own[n_plane]
            elif dz == 0:
                other = far[(dp - 1) * sz.lines]
            else:
                other = far[n_plane * sz.lines + (dz - 1) * PLANE + dp]
            top = (me >> (d.bit_length() - 1)) & 1 if d else 0
            tiles[d, pl.ds(pl.multiple_of(top * half + shift, sz.rows), sz.rows), :] = mine
            tiles[d, pl.ds(pl.multiple_of((1 - top) * half + shift, sz.rows), sz.rows), :] = other
    blocks = sz.chips // sz.cores
    for i in range(blocks):
        k = owner_ref[core * blocks + i]
        d = k ^ me

        @pl.when(me <= k)
        def _():
            out[:, i * tile:(i + 1) * tile] = tiles[d]

        @pl.when(me > k)
        def _():
            out[:, i * tile:(i + 1) * tile] = tiles[d].T


def local(three_index, fit_factor, slots, owner):
    _, count_a, count_s, tile, width = three_index.shape
    chips, cores = lax.axis_size("aux"), lax.axis_size("occ")
    sz = Sizes(chips, cores, tile)
    lines, rows = sz.lines, sz.rows
    f32 = jnp.float32

    def go(x, chip=0, core=0):
        if chip:
            return lax.ppermute(x, "aux", [(j, j ^ chip) for j in range(chips)])
        return lax.ppermute(x, "occ", [(j, j ^ core) for j in range(cores)])

    vmem = pl.BlockSpec(memory_space=pltpu.VMEM)
    smem = pl.BlockSpec(memory_space=pltpu.SMEM)
    hbm = pl.BlockSpec(memory_space=pltpu.HBM)
    small = 4 * cores * sz.total * tile < 2**24
    space = pltpu.VMEM if small else jax.ShapeDtypeStruct
    keep, send = pl.pallas_call(
        functools.partial(pair_kernel, sz),
        out_shape=[
            space((sz.total, tile), f32), space((cores - 1, sz.total, tile), f32),
        ],
        in_specs=[hbm] * 5,
        out_specs=[vmem, vmem],
        scratch_shapes=[
            pltpu.VMEM((count_a * count_s * tile, width), jnp.bfloat16),
            pltpu.VMEM((2 * tile, 2 * tile), jnp.bfloat16),
            pltpu.VMEM((count_s // 2, width, 2 * tile), jnp.bfloat16),
            pltpu.VMEM((count_s * tile, width), jnp.bfloat16),
            pltpu.VMEM((2, count_s // 2, count_s * tile, 2 * tile), f32),
            pltpu.VMEM(fit_factor.shape, jnp.bfloat16),
            pltpu.SMEM(slots.shape, jnp.int32),
            pltpu.SMEM(owner.shape, jnp.int32),
            pltpu.SMEM((chips * (chips + 1) * 2,), jnp.int32),
            pltpu.SMEM((count_a * count_s,), jnp.int32),
            pltpu.SemaphoreType.DMA((count_a * count_s,)),
            pltpu.SemaphoreType.DMA((4,)),
        ],
        compiler_params=pltpu.CompilerParams(
            vmem_limit_bytes=40 * 2**20 if small else 58 * 2**20
        ),
        name="pairs",
    )(*[
        pltpu.with_memory_space_constraint(x, pltpu.HBM)
        for x in (slots, owner, jnp.asarray(sz.table()), three_index, fit_factor)
    ])

    first = sz.at["cross", "s"][1]
    cuts = [(0, first), (first, sz.sent), (sz.sent, sz.total)]
    got = [[go(send[e - 1, lo:hi], core=e) for e in range(1, cores)] for lo, hi in cuts]

    def step(x, name, k):
        pairs = []
        for j in range(chips):
            for c in range(cores):
                pairs.append((j * cores + c, (j ^ (1 << sz.order(name, c)[k])) * cores + c))
        return lax.ppermute(x, ("aux", "occ"), pairs)

    def total(terms):
        return functools.reduce(lambda a, b: a + b, terms)

    def terms(name, half):
        lo, hi = sz.at[name, half]
        shape = (chips // 2, sz.count[name], rows, tile)
        cut = 2 if half == "k" else int(name != "cross")
        off = cuts[cut][0]
        return [x.reshape(shape) for x in [keep[lo:hi]] + [g[lo - off:hi - off] for g in got[cut]]]

    parts, tail = {}, {}
    for k in range(sz.bits):
        for name in ("cross", "line", "plane"):
            if k:
                n = parts[name][0].shape[0] // 2
                sent, parts[name] = [x[n:] for x in parts[name]], [x[:n] for x in parts[name]]
            else:
                sent, parts[name] = terms(name, "s"), terms(name, "k")
            sent = total(sent)
            come = step(sent, name, k)
            tail[name, k] = come[-1:, -1:, -1:, -1:]
            parts[name].append(come)
    cross, line, plane = [total(parts[name])[0] for name in ("cross", "line", "plane")]
    cross = cross.reshape(PLANE - 1, lines - 1, rows, tile)
    near = [
        go(jnp.concatenate([plane[dp - 1:dp], cross[dp - 1]]), chip=dp) for dp in range(1, PLANE)
    ]
    far = [
        go(jnp.concatenate([line[1 + dz:2 + dz], cross[:, dz - 1]]), chip=dz * PLANE)
        for dz in range(1, lines)
    ]
    own = jnp.concatenate([plane, line])
    far = jnp.concatenate(near + far)
    every = [own, far]
    for e in range(1, cores):
        every += [go(own, core=e), go(far, core=e)]

    result = pl.pallas_call(
        functools.partial(place_kernel, sz),
        out_shape=jax.ShapeDtypeStruct((tile, chips // cores * tile), f32),
        in_specs=[smem] + [vmem] * len(every),
        out_specs=vmem,
        scratch_shapes=[pltpu.VMEM((chips, tile, tile), f32)],
        compiler_params=pltpu.CompilerParams(vmem_limit_bytes=24 * 2**20),
        name="place",
    )(owner, *every)
    return result[None]


def solution(mesh):
    placed = (P("occ", "aux", None, None, None), P("aux", None, None), P("occ", "aux", None), P())
    return jax.shard_map(
        local, mesh=mesh, in_specs=placed, out_specs=P("aux", None, "occ"), check_vma=False
    )
```

time: 429 us -> 91 us (0.21)
  waiting for transfers between devices: 294 us -> 46.6 us
  local copies, waits for them, and re-layouts: 66.8 us -> 0.37 us
  other arithmetic: 26.2 us -> 1.01 us
  starting transfers between devices: 15.3 us -> 30.3 us
  between operations: 13.5 us -> 0.28 us
  matrix products: 12.5 us -> 0 us
  Pallas kernels: 0 us -> 12.2 us
    all_to_all x2 -> x0, waiting for transfers between devices: 235 us -> none  [the longest x1 235 us: local(): lax.all_to_all(send_rows, 'aux', split_axis=0, concat_axis=0, tiled=True)]
    reduce_scatter x1 -> x0, waiting for transfers between devices: 58.6 us -> none  [local(): lax.psum_scatter(owned_rows, 'occ', scatter_dimension=1, tiled=True)]
    ppermute x0 -> x23, waiting for transfers between devices: none -> 46.6 us  [the longest x12 37 us: step(): return lax.ppermute(x, ('aux', 'occ'), pairs)]
    ppermute x0 -> x23, starting transfers between devices: none -> 30.3 us  [the longest x12 21.3 us: step(): return lax.ppermute(x, ('aux', 'occ'), pairs)]
    scatter-add x1 -> x0, other arithmetic: 25.3 us -> none  [local(): placed = jnp.zeros((total_blocks, tile_rows, tile_rows), jnp.float32).at[...]
    scatter x2 -> x0, local copies, waits for them, and re-layouts: 20.7 us -> none  [the longest x1 19.5 us: local(): send_rows = jnp.zeros((groups * capacity, tile_rows, count_s * tile_rows)...]
    all_to_all x2 -> x0, starting transfers between devices: 15.2 us -> none  [the longest x1 8.31 us: local(): lax.all_to_all(send_ids, 'aux', split_axis=0, concat_axis=0, tiled=True)]
    transpose x2 -> x0, local copies, waits for them, and re-layouts: 13.9 us -> none  [the longest x1 12.6 us: local(): jnp.transpose(pieces, (0, 2, 1, 3))]
  transfers between devices with their start and end apart: 3 -> 23, of which waited for: 2 -> 14; matrix products, arithmetic and copies ran while one was open for 11% -> 1% of each run, Pallas kernels for 0% -> 0%
where the time goes in v2:
time: 91 us; the launch traced here: 90.8 us
  waiting for transfers between devices  46.6 us (51%)
  starting transfers between devices  30.3 us (33%)
  Pallas kernels  12.2 us (13%)
  other arithmetic  1.01 us (1%)
    ppermute x12, waiting for transfers between devices, step(): return lax.ppermute(x, ('aux', 'occ'), pairs)  37 us
    ppermute x12, starting transfers between devices, step(): return lax.ppermute(x, ('aux', 'occ'), pairs)  21.3 us
    pallas_call x1, Pallas kernels, local(): pl.pallas_call(functools.partial(pair_kernel, sz), out_shape=[space((sz.t...  10.7 us
    ppermute x6, starting transfers between devices, go(): return lax.ppermute(x, 'aux', [(j, j ^ chip) for j in range(chips)])  7.22 us
    ppermute x6, waiting for transfers between devices, go(): return lax.ppermute(x, 'aux', [(j, j ^ chip) for j in range(chips)])  6.64 us
    ppermute x5, waiting for transfers between devices, go(): return lax.ppermute(x, 'occ', [(j, j ^ core) for j in range(cores)])  2.94 us
  transfers between devices with their start and end apart: 23, of which 14 were waited for; matrix products, arithmetic and copies ran while one was open for 1% of the time, Pallas kernels for 0%

profile of v2, /device:TPU:0, one launch (start us, length us, event | category | flops | bytes accessed | tf_op | source)
XLA Modules:
  0.0 90.8 jit_solution(433768523297818819)
XLA Ops:
  0.0 10.7 %pairs.1 = (f32[8704,128]{1,0:T(8,128)S(1)}, f32[1,8704,128]{2,1,0:T(8,128)S(1)}) custom-call(s32[1,4,6]{2,1,0:T(4,128)} %slots_hbm.1, s32[16]{0:T(128)} %owner_ref.1, s32[544]{0:T(1024)} %constant.2.clone.table_hbm, bf16[1,4,6,128,1024]{4,3,2,1,0:T(8,128)(2,1)} %x_ref.1, bf16[4,128,128]{2,1,0:T(8,128)(2,1)} %fit_hbm.1), custom_call_target="tpu_custom_call" | custom-call | tf_op jit(solution)/shard_map/pairs/pallas_call | solution.py:245
  12.1 1.4 %collective-permute-done.1 = f32[2048,128]{1,0:T(8,128)S(1)} collective-permute-done((f32[2048,128]{1,0:T(8,128)S(1)}, f32[2048,128]{1,0:T(8,128)S(1)}, u32[]{:S(2)}, u32[]{:S(2)}) %collective-permute-start.1) | collective-permute-done | bytes 1048608 | tf_op jit(solution)/shard_map/ppermute | solution.py:238
  13.6 2.9 %collective-permute-start.2 = (f32[8,3,32,128]{3,2,1,0:T(8,128)S(1)}, f32[8,3,32,128]{3,2,1,0:T(8,128)S(1)}, u32[]{:S(2)}, u32[]{:S(2)}) collective-permute-start(f32[8,3,32,128]{3,2,1,0:T(8,128)S(1)} %bitcast.67), channel_id=1, source_target_pairs={{0,2},{1,5},{2,0},{3,7},{4,6},{5,1},{6,4},{7,3},{8,10},{9,13},{10,... | collective-permute-start | bytes 1179656 | tf_op jit(solution)/shard_map/ppermute | solution.py:284
  16.6 1.6 %collective-permute-start.6 = (f32[8,5,32,128]{3,2,1,0:T(8,128)S(1)}, f32[8,5,32,128]{3,2,1,0:T(8,128)S(1)}, u32[]{:S(2)}, u32[]{:S(2)}) collective-permute-start(f32[8,5,32,128]{3,2,1,0:T(8,128)S(1)} %bitcast.62), channel_id=1, source_target_pairs={{0,8},{1,17},{2,10},{3,19},{4,12},{5,21},{6,14},{7,23},{8,0},{9,25... | collective-permute-start | bytes 1966088 | tf_op jit(solution)/shard_map/ppermute | solution.py:284
  18.6 2.9 %collective-permute-start.11 = (f32[8,9,32,128]{3,2,1,0:T(8,128)S(1)}, f32[8,9,32,128]{3,2,1,0:T(8,128)S(1)}, u32[]{:S(2)}, u32[]{:S(2)}) collective-permute-start(f32[8,9,32,128]{3,2,1,0:T(8,128)S(1)} %bitcast.58), channel_id=1, source_target_pairs={{0,2},{1,5},{2,0},{3,7},{4,6},{5,1},{6,4},{7,3},{8,10},{9,13},{10,... | collective-permute-start | bytes 3538952 | tf_op jit(solution)/shard_map/ppermute | solution.py:284
  22.3 2.1 %collective-permute-start.3 = (f32[4,3,32,128]{3,2,1,0:T(8,128)S(1)}, f32[4,3,32,128]{3,2,1,0:T(8,128)S(1)}, u32[]{:S(2)}, u32[]{:S(2)}) collective-permute-start(f32[4,3,32,128]{3,2,1,0:T(8,128)S(1)} %slice_add_fusion.10), channel_id=1, source_target_pairs={{0,4},{1,3},{2,6},{3,1},{4,0},{5,7},{6,2},{7,5},{8,12},{9,11},{10,... | collective-permute-start | bytes 589832 | tf_op jit(solution)/shard_map/ppermute | solution.py:284
  24.5 9.5 %collective-permute-done.6 = f32[8,5,32,128]{3,2,1,0:T(8,128)S(1)} collective-permute-done((f32[8,5,32,128]{3,2,1,0:T(8,128)S(1)}, f32[8,5,32,128]{3,2,1,0:T(8,128)S(1)}, u32[]{:S(2)}, u32[]{:S(2)}) %collective-permute-start.6) | collective-permute-done | bytes 655392 | tf_op jit(solution)/shard_map/ppermute | solution.py:284
  34.0 1.9 %collective-permute-start.7 = (f32[4,5,32,128]{3,2,1,0:T(8,128)S(1)}, f32[4,5,32,128]{3,2,1,0:T(8,128)S(1)}, u32[]{:S(2)}, u32[]{:S(2)}) collective-permute-start(f32[4,5,32,128]{3,2,1,0:T(8,128)S(1)} %slice_add_fusion.5), channel_id=1, source_target_pairs={{0,16},{1,9},{2,18},{3,11},{4,20},{5,13},{6,22},{7,15},{8,24},{9,1... | collective-permute-start | bytes 983048 | tf_op jit(solution)/shard_map/ppermute | solution.py:284
  36.2 2.6 %collective-permute-start.4 = (f32[2,3,32,128]{3,2,1,0:T(8,128)S(1)}, f32[2,3,32,128]{3,2,1,0:T(8,128)S(1)}, u32[]{:S(2)}, u32[]{:S(2)}) collective-permute-start(f32[2,3,32,128]{3,2,1,0:T(8,128)S(1)} %slice_add_fusion.23), channel_id=1, source_target_pairs={{0,8},{1,17},{2,10},{3,19},{4,12},{5,21},{6,14},{7,23},{8,0},{9,25... | collective-permute-start | bytes 294920 | tf_op jit(solution)/shard_map/ppermute | solution.py:284
  38.9 1.6 %collective-permute-start.12 = (f32[4,9,32,128]{3,2,1,0:T(8,128)S(1)}, f32[4,9,32,128]{3,2,1,0:T(8,128)S(1)}, u32[]{:S(2)}, u32[]{:S(2)}) collective-permute-start(f32[4,9,32,128]{3,2,1,0:T(8,128)S(1)} %slice_add_fusion.2), channel_id=1, source_target_pairs={{0,4},{1,3},{2,6},{3,1},{4,0},{5,7},{6,2},{7,5},{8,12},{9,11},{10,... | collective-permute-start | bytes 1769480 | tf_op jit(solution)/shard_map/ppermute | solution.py:284
  40.5 4.1 %collective-permute-done.4 = f32[2,3,32,128]{3,2,1,0:T(8,128)S(1)} collective-permute-done((f32[2,3,32,128]{3,2,1,0:T(8,128)S(1)}, f32[2,3,32,128]{3,2,1,0:T(8,128)S(1)}, u32[]{:S(2)}, u32[]{:S(2)}) %collective-permute-start.4) | collective-permute-done | bytes 98336 | tf_op jit(solution)/shard_map/ppermute | solution.py:284
  44.6 3.8 %collective-permute-start.5 = (f32[1,3,32,128]{3,2,1,0:T(8,128)S(1)}, f32[1,3,32,128]{3,2,1,0:T(8,128)S(1)}, u32[]{:S(2)}, u32[]{:S(2)}) collective-permute-start(f32[1,3,32,128]{3,2,1,0:T(8,128)S(1)} %slice_add_fusion.34), channel_id=1, source_target_pairs={{0,16},{1,9},{2,18},{3,11},{4,20},{5,13},{6,22},{7,15},{8,24},{9,1... | collective-permute-start | bytes 147464 | tf_op jit(solution)/shard_map/ppermute | solution.py:284
  49.1 1.4 %collective-permute-done.5 = f32[1,3,32,128]{3,2,1,0:T(8,128)S(1)} collective-permute-done((f32[1,3,32,128]{3,2,1,0:T(8,128)S(1)}, f32[1,3,32,128]{3,2,1,0:T(8,128)S(1)}, u32[]{:S(2)}, u32[]{:S(2)}) %collective-permute-start.5) | collective-permute-done | bytes 49184 | tf_op jit(solution)/shard_map/ppermute | solution.py:284
  50.5 3.3 %collective-permute-done.8 = f32[2,5,32,128]{3,2,1,0:T(8,128)S(1)} collective-permute-done((f32[2,5,32,128]{3,2,1,0:T(8,128)S(1)}, f32[2,5,32,128]{3,2,1,0:T(8,128)S(1)}, u32[]{:S(2)}, u32[]{:S(2)}) %collective-permute-start.8) | collective-permute-done | bytes 163872 | tf_op jit(solution)/shard_map/ppermute | solution.py:284
  55.0 3.4 %collective-permute-done.9 = f32[1,5,32,128]{3,2,1,0:T(8,128)S(1)} collective-permute-done((f32[1,5,32,128]{3,2,1,0:T(8,128)S(1)}, f32[1,5,32,128]{3,2,1,0:T(8,128)S(1)}, u32[]{:S(2)}, u32[]{:S(2)}) %collective-permute-start.9) | collective-permute-done | bytes 81952 | tf_op jit(solution)/shard_map/ppermute | solution.py:284
  58.4 6.4 %collective-permute-done.13 = f32[2,9,32,128]{3,2,1,0:T(8,128)S(1)} collective-permute-done((f32[2,9,32,128]{3,2,1,0:T(8,128)S(1)}, f32[2,9,32,128]{3,2,1,0:T(8,128)S(1)}, u32[]{:S(2)}, u32[]{:S(2)}) %collective-permute-start.13) | collective-permute-done | bytes 294944 | tf_op jit(solution)/shard_map/ppermute | solution.py:284
  65.0 8.2 %collective-permute-done.14 = f32[1,9,32,128]{3,2,1,0:T(8,128)S(1)} collective-permute-done((f32[1,9,32,128]{3,2,1,0:T(8,128)S(1)}, f32[1,9,32,128]{3,2,1,0:T(8,128)S(1)}, u32[]{:S(2)}, u32[]{:S(2)}) %collective-permute-start.14) | collective-permute-done | bytes 147488 | tf_op jit(solution)/shard_map/ppermute | solution.py:284
  73.4 2.2 %collective-permute-start.19 = (f32[4,32,128]{2,1,0:T(8,128)S(1)}, f32[4,32,128]{2,1,0:T(8,128)S(1)}, u32[]{:S(2)}, u32[]{:S(2)}) collective-permute-start(f32[4,32,128]{2,1,0:T(8,128)S(1)} %pad_maximum_fusion.5), channel_id=1, source_target_pairs={{0,16},{2,18},{4,20},{6,22},{8,24},{10,26},{12,28},{14,30},{16,0},... | collective-permute-start | bytes 196616 | tf_op jit(solution)/shard_map/ppermute | solution.py:237
  75.6 2.2 %collective-permute-start.20 = (f32[4,32,128]{2,1,0:T(8,128)S(1)}, f32[4,32,128]{2,1,0:T(8,128)S(1)}, u32[]{:S(2)}, u32[]{:S(2)}) collective-permute-start(f32[4,32,128]{2,1,0:T(8,128)S(1)} %pad_maximum_fusion.6), channel_id=1, source_target_pairs={{0,24},{2,26},{4,28},{6,30},{8,16},{10,18},{12,20},{14,22},{16,8},... | collective-permute-start | bytes 196616 | tf_op jit(solution)/shard_map/ppermute | solution.py:237
  77.8 2.1 %collective-permute-start.15 = (f32[4,32,128]{2,1,0:T(8,128)S(1)}, f32[4,32,128]{2,1,0:T(8,128)S(1)}, u32[]{:S(2)}, u32[]{:S(2)}) collective-permute-start(f32[4,32,128]{2,1,0:T(8,128)S(1)} %pad_maximum_fusion.1), channel_id=1, source_target_pairs={{0,2},{2,0},{4,6},{6,4},{8,10},{10,8},{12,14},{14,12},{16,18},{18,... | collective-permute-start | bytes 196616 | tf_op jit(solution)/shard_map/ppermute | solution.py:237
  79.9 2.2 %collective-permute-done.15 = f32[4,32,128]{2,1,0:T(8,128)S(1)} collective-permute-done((f32[4,32,128]{2,1,0:T(8,128)S(1)}, f32[4,32,128]{2,1,0:T(8,128)S(1)}, u32[]{:S(2)}, u32[]{:S(2)}) %collective-permute-start.15) | collective-permute-done | bytes 65568 | tf_op jit(solution)/shard_map/ppermute | solution.py:237
  84.1 3.1 %collective-permute-done.17 = f32[4,32,128]{2,1,0:T(8,128)S(1)} collective-permute-done((f32[4,32,128]{2,1,0:T(8,128)S(1)}, f32[4,32,128]{2,1,0:T(8,128)S(1)}, u32[]{:S(2)}, u32[]{:S(2)}) %collective-permute-start.17) | collective-permute-done | bytes 65568 | tf_op jit(solution)/shard_map/ppermute | solution.py:237
  88.0 1.3 %collective-permute-done.21.refs_2_ = f32[8,32,128]{2,1,0:T(8,128)S(1)} collective-permute-done((f32[8,32,128]{2,1,0:T(8,128)S(1)}, f32[8,32,128]{2,1,0:T(8,128)S(1)}, u32[]{:S(2)}, u32[]{:S(2)}) %collective-permute-start.21) | collective-permute-done | bytes 131104 | tf_op jit(solution)/shard_map/ppermute | solution.py:238
  89.3 1.5 %place.1 = f32[128,1024]{1,0:T(8,128)} custom-call(s32[16]{0:T(128)S(1)} %copy-done, f32[8,32,128]{2,1,0:T(8,128)S(1)} %pad_maximum_fusion.refs_0_, f32[24,32,128]{2,1,0:T(8,128)S(1)} %constant_dynamic-update-slice_fusion.refs_1_, f32[8,32,128]{2,1,0:T(8,128)S(1)} %collective-permute-done.21.refs_2_, f32[24,32,128]{2,1,0:T(8,128)S(1)} %collective-permute-done.22.refs_3_), custom_call_target="tpu_custom_call" | custom-call | tf_op jit(solution)/shard_map/place/pallas_call | solution.py:323
  (70 shorter events, 8.1 us)
Async XLA Ops:
  10.8 2.8 %collective-permute-start.1 = (f32[2048,128]{1,0:T(8,128)S(1)}, f32[2048,128]{1,0:T(8,128)S(1)}, u32[]{:S(2)}, u32[]{:S(2)}) collective-permute-start(f32[2048,128]{1,0:T(8,128)S(1)} %slice_bitcast_fusion.2), channel_id=1, source_target_pairs={{0,1},{1,0},{2,3},{3,2},{4,5},{5,4},{6,7},{7,6},{8,9},{9,8},{10,11... | collective-permute-start | bytes 3145736 | tf_op jit(solution)/shard_map/ppermute | solution.py:238
  11.4 10.1 %collective-permute-start = (f32[4352,128]{1,0:T(8,128)S(1)}, f32[4352,128]{1,0:T(8,128)S(1)}, u32[]{:S(2)}, u32[]{:S(2)}) collective-permute-start(f32[4352,128]{1,0:T(8,128)S(1)} %slice_bitcast_fusion), channel_id=1, source_target_pairs={{0,1},{1,0},{2,3},{3,2},{4,5},{5,4},{6,7},{7,6},{8,9},{9,8},{10,11... | collective-permute-start | bytes 6684680 | tf_op jit(solution)/shard_map/ppermute | solution.py:238
  11.6 6.8 %collective-permute-start.10 = (f32[2304,128]{1,0:T(8,128)S(1)}, f32[2304,128]{1,0:T(8,128)S(1)}, u32[]{:S(2)}, u32[]{:S(2)}) collective-permute-start(f32[2304,128]{1,0:T(8,128)S(1)} %slice_bitcast_fusion.1), channel_id=1, source_target_pairs={{0,1},{1,0},{2,3},{3,2},{4,5},{5,4},{6,7},{7,6},{8,9},{9,8},{10,11... | collective-permute-start | bytes 3538952 | tf_op jit(solution)/shard_map/ppermute | solution.py:238
  13.6 8.7 %collective-permute-start.2 = (f32[8,3,32,128]{3,2,1,0:T(8,128)S(1)}, f32[8,3,32,128]{3,2,1,0:T(8,128)S(1)}, u32[]{:S(2)}, u32[]{:S(2)}) collective-permute-start(f32[8,3,32,128]{3,2,1,0:T(8,128)S(1)} %bitcast.67), channel_id=1, source_target_pairs={{0,2},{1,5},{2,0},{3,7},{4,6},{5,1},{6,4},{7,3},{8,10},{9,13},{10,... | collective-permute-start | bytes 1179656 | tf_op jit(solution)/shard_map/ppermute | solution.py:284
  16.6 17.4 %collective-permute-start.6 = (f32[8,5,32,128]{3,2,1,0:T(8,128)S(1)}, f32[8,5,32,128]{3,2,1,0:T(8,128)S(1)}, u32[]{:S(2)}, u32[]{:S(2)}) collective-permute-start(f32[8,5,32,128]{3,2,1,0:T(8,128)S(1)} %bitcast.62), channel_id=1, source_target_pairs={{0,8},{1,17},{2,10},{3,19},{4,12},{5,21},{6,14},{7,23},{8,0},{9,25... | collective-permute-start | bytes 1966088 | tf_op jit(solution)/shard_map/ppermute | solution.py:284
  18.6 20.3 %collective-permute-start.11 = (f32[8,9,32,128]{3,2,1,0:T(8,128)S(1)}, f32[8,9,32,128]{3,2,1,0:T(8,128)S(1)}, u32[]{:S(2)}, u32[]{:S(2)}) collective-permute-start(f32[8,9,32,128]{3,2,1,0:T(8,128)S(1)} %bitcast.58), channel_id=1, source_target_pairs={{0,2},{1,5},{2,0},{3,7},{4,6},{5,1},{6,4},{7,3},{8,10},{9,13},{10,... | collective-permute-start | bytes 3538952 | tf_op jit(solution)/shard_map/ppermute | solution.py:284
  22.3 13.9 %collective-permute-start.3 = (f32[4,3,32,128]{3,2,1,0:T(8,128)S(1)}, f32[4,3,32,128]{3,2,1,0:T(8,128)S(1)}, u32[]{:S(2)}, u32[]{:S(2)}) collective-permute-start(f32[4,3,32,128]{3,2,1,0:T(8,128)S(1)} %slice_add_fusion.10), channel_id=1, source_target_pairs={{0,4},{1,3},{2,6},{3,1},{4,0},{5,7},{6,2},{7,5},{8,12},{9,11},{10,... | collective-permute-start | bytes 589832 | tf_op jit(solution)/shard_map/ppermute | solution.py:284
  34.0 14.4 %collective-permute-start.7 = (f32[4,5,32,128]{3,2,1,0:T(8,128)S(1)}, f32[4,5,32,128]{3,2,1,0:T(8,128)S(1)}, u32[]{:S(2)}, u32[]{:S(2)}) collective-permute-start(f32[4,5,32,128]{3,2,1,0:T(8,128)S(1)} %slice_add_fusion.5), channel_id=1, source_target_pairs={{0,16},{1,9},{2,18},{3,11},{4,20},{5,13},{6,22},{7,15},{8,24},{9,1... | collective-permute-start | bytes 983048 | tf_op jit(solution)/shard_map/ppermute | solution.py:284
  36.2 8.4 %collective-permute-start.4 = (f32[2,3,32,128]{3,2,1,0:T(8,128)S(1)}, f32[2,3,32,128]{3,2,1,0:T(8,128)S(1)}, u32[]{:S(2)}, u32[]{:S(2)}) collective-permute-start(f32[2,3,32,128]{3,2,1,0:T(8,128)S(1)} %slice_add_fusion.23), channel_id=1, source_target_pairs={{0,8},{1,17},{2,10},{3,19},{4,12},{5,21},{6,14},{7,23},{8,0},{9,25... | collective-permute-start | bytes 294920 | tf_op jit(solution)/shard_map/ppermute | solution.py:284
  38.9 15.9 %collective-permute-start.12 = (f32[4,9,32,128]{3,2,1,0:T(8,128)S(1)}, f32[4,9,32,128]{3,2,1,0:T(8,128)S(1)}, u32[]{:S(2)}, u32[]{:S(2)}) collective-permute-start(f32[4,9,32,128]{3,2,1,0:T(8,128)S(1)} %slice_add_fusion.2), channel_id=1, source_target_pairs={{0,4},{1,3},{2,6},{3,1},{4,0},{5,7},{6,2},{7,5},{8,12},{9,11},{10,... | collective-permute-start | bytes 1769480 | tf_op jit(solution)/shard_map/ppermute | solution.py:284
  44.6 5.8 %collective-permute-start.5 = (f32[1,3,32,128]{3,2,1,0:T(8,128)S(1)}, f32[1,3,32,128]{3,2,1,0:T(8,128)S(1)}, u32[]{:S(2)}, u32[]{:S(2)}) collective-permute-start(f32[1,3,32,128]{3,2,1,0:T(8,128)S(1)} %slice_add_fusion.34), channel_id=1, source_target_pairs={{0,16},{1,9},{2,18},{3,11},{4,20},{5,13},{6,22},{7,15},{8,24},{9,1... | collective-permute-start | bytes 147464 | tf_op jit(solution)/shard_map/ppermute | solution.py:284
  48.4 5.4 %collective-permute-start.8 = (f32[2,5,32,128]{3,2,1,0:T(8,128)S(1)}, f32[2,5,32,128]{3,2,1,0:T(8,128)S(1)}, u32[]{:S(2)}, u32[]{:S(2)}) collective-permute-start(f32[2,5,32,128]{3,2,1,0:T(8,128)S(1)} %slice_add_fusion.12), channel_id=1, source_target_pairs={{0,2},{1,5},{2,0},{3,7},{4,6},{5,1},{6,4},{7,3},{8,10},{9,13},{10,... | collective-permute-start | bytes 491528 | tf_op jit(solution)/shard_map/ppermute | solution.py:284
  53.9 4.5 %collective-permute-start.9 = (f32[1,5,32,128]{3,2,1,0:T(8,128)S(1)}, f32[1,5,32,128]{3,2,1,0:T(8,128)S(1)}, u32[]{:S(2)}, u32[]{:S(2)}) collective-permute-start(f32[1,5,32,128]{3,2,1,0:T(8,128)S(1)} %slice_add_fusion.26), channel_id=1, source_target_pairs={{0,4},{1,3},{2,6},{3,1},{4,0},{5,7},{6,2},{7,5},{8,12},{9,11},{10,... | collective-permute-start | bytes 245768 | tf_op jit(solution)/shard_map/ppermute | solution.py:284
  54.9 9.8 %collective-permute-start.13 = (f32[2,9,32,128]{3,2,1,0:T(8,128)S(1)}, f32[2,9,32,128]{3,2,1,0:T(8,128)S(1)}, u32[]{:S(2)}, u32[]{:S(2)}) collective-permute-start(f32[2,9,32,128]{3,2,1,0:T(8,128)S(1)} %slice_add_fusion.7), channel_id=1, source_target_pairs={{0,8},{1,17},{2,10},{3,19},{4,12},{5,21},{6,14},{7,23},{8,0},{9,25... | collective-permute-start | bytes 884744 | tf_op jit(solution)/shard_map/ppermute | solution.py:284
  58.4 30.9 %copy-start = (s32[16]{0:T(128)S(1)}, s32[16]{0:T(128)}, u32[]{:S(2)}) copy-start(s32[16]{0:T(128)} %owner_ref.1) | copy-start | bytes 196
  64.8 8.4 %collective-permute-start.14 = (f32[1,9,32,128]{3,2,1,0:T(8,128)S(1)}, f32[1,9,32,128]{3,2,1,0:T(8,128)S(1)}, u32[]{:S(2)}, u32[]{:S(2)}) collective-permute-start(f32[1,9,32,128]{3,2,1,0:T(8,128)S(1)} %slice_add_fusion.15), channel_id=1, source_target_pairs={{0,16},{1,9},{2,18},{3,11},{4,20},{5,13},{6,22},{7,15},{8,24},{9,1... | collective-permute-start | bytes 442376 | tf_op jit(solution)/shard_map/ppermute | solution.py:284
  73.3 13.9 %collective-permute-start.18 = (f32[4,32,128]{2,1,0:T(8,128)S(1)}, f32[4,32,128]{2,1,0:T(8,128)S(1)}, u32[]{:S(2)}, u32[]{:S(2)}) collective-permute-start(f32[4,32,128]{2,1,0:T(8,128)S(1)} %pad_maximum_fusion.4), channel_id=1, source_target_pairs={{0,8},{2,10},{4,12},{6,14},{8,0},{10,2},{12,4},{14,6},{16,24},{18,... | collective-permute-start | bytes 196616 | tf_op jit(solution)/shard_map/ppermute | solution.py:237
  73.4 13.9 %collective-permute-start.19 = (f32[4,32,128]{2,1,0:T(8,128)S(1)}, f32[4,32,128]{2,1,0:T(8,128)S(1)}, u32[]{:S(2)}, u32[]{:S(2)}) collective-permute-start(f32[4,32,128]{2,1,0:T(8,128)S(1)} %pad_maximum_fusion.5), channel_id=1, source_target_pairs={{0,16},{2,18},{4,20},{6,22},{8,24},{10,26},{12,28},{14,30},{16,0},... | collective-permute-start | bytes 196616 | tf_op jit(solution)/shard_map/ppermute | solution.py:237
  75.6 11.7 %collective-permute-start.20 = (f32[4,32,128]{2,1,0:T(8,128)S(1)}, f32[4,32,128]{2,1,0:T(8,128)S(1)}, u32[]{:S(2)}, u32[]{:S(2)}) collective-permute-start(f32[4,32,128]{2,1,0:T(8,128)S(1)} %pad_maximum_fusion.6), channel_id=1, source_target_pairs={{0,24},{2,26},{4,28},{6,30},{8,16},{10,18},{12,20},{14,22},{16,8},... | collective-permute-start | bytes 196616 | tf_op jit(solution)/shard_map/ppermute | solution.py:237
  77.8 4.3 %collective-permute-start.15 = (f32[4,32,128]{2,1,0:T(8,128)S(1)}, f32[4,32,128]{2,1,0:T(8,128)S(1)}, u32[]{:S(2)}, u32[]{:S(2)}) collective-permute-start(f32[4,32,128]{2,1,0:T(8,128)S(1)} %pad_maximum_fusion.1), channel_id=1, source_target_pairs={{0,2},{2,0},{4,6},{6,4},{8,10},{10,8},{12,14},{14,12},{16,18},{18,... | collective-permute-start | bytes 196616 | tf_op jit(solution)/shard_map/ppermute | solution.py:237
  79.8 4.3 %collective-permute-start.16 = (f32[4,32,128]{2,1,0:T(8,128)S(1)}, f32[4,32,128]{2,1,0:T(8,128)S(1)}, u32[]{:S(2)}, u32[]{:S(2)}) collective-permute-start(f32[4,32,128]{2,1,0:T(8,128)S(1)} %pad_maximum_fusion.2), channel_id=1, source_target_pairs={{0,4},{2,6},{4,0},{6,2},{8,12},{10,14},{12,8},{14,10},{16,20},{18,... | collective-permute-start | bytes 196616 | tf_op jit(solution)/shard_map/ppermute | solution.py:237
  82.1 5.2 %collective-permute-start.17 = (f32[4,32,128]{2,1,0:T(8,128)S(1)}, f32[4,32,128]{2,1,0:T(8,128)S(1)}, u32[]{:S(2)}, u32[]{:S(2)}) collective-permute-start(f32[4,32,128]{2,1,0:T(8,128)S(1)} %pad_maximum_fusion.3), channel_id=1, source_target_pairs={{0,6},{2,4},{4,2},{6,0},{8,14},{10,12},{12,10},{14,8},{16,22},{18,... | collective-permute-start | bytes 196616 | tf_op jit(solution)/shard_map/ppermute | solution.py:237
  87.3 2.0 %collective-permute-start.22 = (f32[24,32,128]{2,1,0:T(8,128)S(1)}, f32[24,32,128]{2,1,0:T(8,128)S(1)}, u32[]{:S(2)}, u32[]{:S(2)}) collective-permute-start(f32[24,32,128]{2,1,0:T(8,128)S(1)} %constant_dynamic-update-slice_fusion.refs_1_), channel_id=1, source_target_pairs={{0,1},{1,0},{2,3},{3,2},{4,5},{5,4},{6,7},{7,6},{8,9},{9,8},{10,11... | collective-permute-start | bytes 1179656 | tf_op jit(solution)/shard_map/ppermute | solution.py:238
  87.4 1.9 %collective-permute-start.21 = (f32[8,32,128]{2,1,0:T(8,128)S(1)}, f32[8,32,128]{2,1,0:T(8,128)S(1)}, u32[]{:S(2)}, u32[]{:S(2)}) collective-permute-start(f32[8,32,128]{2,1,0:T(8,128)S(1)} %pad_maximum_fusion.refs_0_), channel_id=1, source_target_pairs={{0,1},{1,0},{2,3},{3,2},{4,5},{5,4},{6,7},{7,6},{8,9},{9,8},{10,11... | collective-permute-start | bytes 393224 | tf_op jit(solution)/shard_map/ppermute | solution.py:238

commit v3 on v2

--- a/solution.py
+++ b/solution.py
@@ -39,13 +39,14 @@
         for j in range(self.chips):
             for unit in range(self.chips + 1):
                 dz, dp = (unit // PLANE, unit % PLANE) if unit < self.chips else (-1, 0)
-                if dp == 0:
-                    name, i = "line", 1 + dz
-                elif dz == 0:
-                    name, i = "plane", dp - 1
-                else:
-                    name, i = "cross", (dp - 1) * (self.lines - 1) + dz - 1
                 for parity in range(2):
+                    i = dp - 1 if dp == 3 else (dp - 1) ^ parity
+                    if dp == 0:
+                        name, i = "line", 1 + dz
+                    elif dz == 0:
+                        name = "plane"
+                    else:
+                        name, i = "cross", i * (self.lines - 1) + dz - 1
                     place = 0
                     at = j ^ dp if name == "cross" else j
                     for bit in self.order(name, parity):
@@ -194,20 +195,22 @@
     for o in range(sz.cores):
         own, far = refs[2 * o:2 * o + 2]
         shift = (o ^ core) * sz.rows
+        parity = (o ^ core) & 1
         for d in range(sz.chips):
             dp, dz = d % PLANE, d // PLANE
+            i = dp - 1 if dp == 3 else (dp - 1) ^ parity
             if dp == 0:
                 mine = own[n_plane + 1 + dz]
             elif dz == 0:
-                mine = own[dp - 1]
+                mine = own[i]
             else:
-                mine = far[(dp - 1) * sz.lines + dz]
+                mine = far[i * sz.lines + dz]
             if d == 0:
                 other = own[n_plane]
             elif dz == 0:
-                other = far[(dp - 1) * sz.lines]
+                other = far[i * sz.lines]
             else:
-                other = far[n_plane * sz.lines + (dz - 1) * PLANE + dp]
+                other = far[n_plane * sz.lines + (dz - 1) * PLANE + (1 + i if dp else 0)]
             top = (me >> (d.bit_length() - 1)) & 1 if d else 0
             tiles[d, pl.ds(pl.multiple_of(top * half + shift, sz.rows), sz.rows), :] = mine
             tiles[d, pl.ds(pl.multiple_of((1 - top) * half + shift, sz.rows), sz.rows), :] = other
@@ -274,7 +277,15 @@
 
     first = sz.at["cross", "s"][1]
     cuts = [(0, first), (first, sz.sent), (sz.sent, sz.total)]
-    got = [[go(send[e - 1, lo:hi], core=e) for e in range(1, cores)] for lo, hi in cuts]
+    got = []
+    for lo, hi in cuts:
+        moved = []
+        for e in range(1, cores):
+            x = send[e - 1, lo:hi]
+            if got:
+                x = x + 0 * got[0][e - 1][:1]
+            moved.append(go(x, core=e))
+        got.append(moved)
 
     def step(x, name, k):
         pairs = []
@@ -293,7 +304,7 @@
         off = cuts[cut][0]
         return [x.reshape(shape) for x in [keep[lo:hi]] + [g[lo - off:hi - off] for g in got[cut]]]
 
-    parts, tail = {}, {}
+    parts, before = {}, None
     for k in range(sz.bits):
         for name in ("cross", "line", "plane"):
             if k:
@@ -302,18 +313,24 @@
             else:
                 sent, parts[name] = terms(name, "s"), terms(name, "k")
             sent = total(sent)
+            if before is not None:
+                sent = sent + 0 * before[:sent.shape[0], :1]
+            before = sent
             come = step(sent, name, k)
-            tail[name, k] = come[-1:, -1:, -1:, -1:]
             parts[name].append(come)
-    cross, line, plane = [total(parts[name])[0] for name in ("cross", "line", "plane")]
+    cross = total(parts["cross"])[0]
+    line = total(parts["line"])[0] + 0 * cross[:1]
+    plane = total(parts["plane"])[0] + 0 * line[:1]
     cross = cross.reshape(PLANE - 1, lines - 1, rows, tile)
-    near = [
-        go(jnp.concatenate([plane[dp - 1:dp], cross[dp - 1]]), chip=dp) for dp in range(1, PLANE)
+    near = [jnp.concatenate([plane[i:i + 1], cross[i]]) for i in range(PLANE - 1)]
+    far = [
+        jnp.concatenate([line[1 + dz:2 + dz], cross[:, dz - 1]]) for dz in range(1, lines)
     ]
-    far = [
-        go(jnp.concatenate([line[1 + dz:2 + dz], cross[:, dz - 1]]), chip=dz * PLANE)
-        for dz in range(1, lines)
-    ]
+    sent = jnp.stack([near[0], near[2]])
+    far = [go(x, chip=dz * PLANE) for dz, x in enumerate(far, 1)]
+    come = step(sent, "plane", 0)
+    last = step(jnp.stack([near[1], come[1]]), "plane", 1)
+    near = [come[0], last[0], last[1]]
     own = jnp.concatenate([plane, line])
     far = jnp.concatenate(near + far)
     every = [own, far]

time: 91 us -> 79.8 us (0.88)
  waiting for transfers between devices: 46.6 us -> 30.2 us
  starting transfers between devices: 30.3 us -> 35 us
    ppermute x12 -> x14, waiting for transfers between devices: 37 us -> 26.4 us  [step(): return lax.ppermute(x, ('aux', 'occ'), pairs)]
    ppermute x6 -> x3, waiting for transfers between devices: 6.64 us -> 0.01 us  [go(): return lax.ppermute(x, 'aux', [(j, j ^ chip) for j in range(chips)])]
    ppermute x12 -> x14, starting transfers between devices: 21.3 us -> 27.9 us  [step(): return lax.ppermute(x, ('aux', 'occ'), pairs)]
    ppermute x6 -> x3, starting transfers between devices: 7.22 us -> 5.32 us  [go(): return lax.ppermute(x, 'aux', [(j, j ^ chip) for j in range(chips)])]
    add x0 -> x27, other arithmetic: none -> 0.93 us  [the longest x22 0.65 us: local(): sent = sent + 0 * before[:sent.shape[0], :1]]
  transfers between devices with their start and end apart: 23 -> 22, of which waited for: 14 -> 12; matrix products, arithmetic and copies ran while one was open for 1% -> 2% of each run, Pallas kernels for 0% -> 0%
where the time goes in v3:
time: 79.8 us; the launch traced here: 79.6 us
  starting transfers between devices  35 us (44%)
  waiting for transfers between devices  30.2 us (38%)
  Pallas kernels  12.3 us (15%)
  other arithmetic  1.57 us (2%)
    ppermute x14, starting transfers between devices, step(): return lax.ppermute(x, ('aux', 'occ'), pairs)  27.9 us
    ppermute x14, waiting for transfers between devices, step(): return lax.ppermute(x, ('aux', 'occ'), pairs)  26.4 us
    pallas_call x1, Pallas kernels, local(): pl.pallas_call(functools.partial(pair_kernel, sz), out_shape=[space((sz.t...  10.7 us
    ppermute x3, starting transfers between devices, go(): return lax.ppermute(x, 'aux', [(j, j ^ chip) for j in range(chips)])  5.32 us
    ppermute x5, waiting for transfers between devices, go(): return lax.ppermute(x, 'occ', [(j, j ^ core) for j in range(cores)])  3.8 us
    ppermute x5, starting transfers between devices, go(): return lax.ppermute(x, 'occ', [(j, j ^ core) for j in range(cores)])  1.78 us
  transfers between devices with their start and end apart: 22, of which 12 were waited for; matrix products, arithmetic and copies ran while one was open for 2% of the time, Pallas kernels for 0%

profile of v3, /device:TPU:0, one launch (start us, length us, event | category | flops | bytes accessed | tf_op | source)
XLA Modules:
  0.0 79.6 jit_solution(5268100944787681440)
XLA Ops:
  0.0 10.7 %pairs.1 = (f32[8704,128]{1,0:T(8,128)S(1)}, f32[1,8704,128]{2,1,0:T(8,128)S(1)}) custom-call(s32[1,4,6]{2,1,0:T(4,128)} %slots_hbm.1, s32[16]{0:T(128)} %owner_ref.1, s32[544]{0:T(1024)} %constant.3.clone.table_hbm, bf16[1,4,6,128,1024]{4,3,2,1,0:T(8,128)(2,1)} %x_ref.1, bf16[4,128,128]{2,1,0:T(8,128)(2,1)} %fit_hbm.1), custom_call_target="tpu_custom_call" | custom-call | tf_op jit(solution)/shard_map/pairs/pallas_call | solution.py:248
  11.3 2.5 %collective-permute-done = f32[2304,128]{1,0:T(8,128)S(1)} collective-permute-done((f32[2304,128]{1,0:T(8,128)S(1)}, f32[2304,128]{1,0:T(8,128)S(1)}, u32[]{:S(2)}, u32[]{:S(2)}) %collective-permute-start) | collective-permute-done | bytes 1179680 | tf_op jit(solution)/shard_map/ppermute | solution.py:241
  14.8 2.9 %collective-permute-start.5 = (f32[8,9,32,128]{3,2,1,0:T(8,128)S(1)}, f32[8,9,32,128]{3,2,1,0:T(8,128)S(1)}, u32[]{:S(2)}, u32[]{:S(2)}) collective-permute-start(f32[8,9,32,128]{3,2,1,0:T(8,128)S(1)} %bitcast.98), channel_id=1, source_target_pairs={{0,2},{1,5},{2,0},{3,7},{4,6},{5,1},{6,4},{7,3},{8,10},{9,13},{10,... | collective-permute-start | bytes 3538952 | tf_op jit(solution)/shard_map/ppermute | solution.py:295
  17.9 1.9 %collective-permute-start.4 = (f32[8,5,32,128]{3,2,1,0:T(8,128)S(1)}, f32[8,5,32,128]{3,2,1,0:T(8,128)S(1)}, u32[]{:S(2)}, u32[]{:S(2)}) collective-permute-start(f32[8,5,32,128]{3,2,1,0:T(8,128)S(1)} %broadcast_add_fusion), channel_id=1, source_target_pairs={{0,8},{1,17},{2,10},{3,19},{4,12},{5,21},{6,14},{7,23},{8,0},{9,25... | collective-permute-start | bytes 1966088 | tf_op jit(solution)/shard_map/ppermute | solution.py:295
  19.8 1.6 %collective-permute-start.3 = (f32[8,3,32,128]{3,2,1,0:T(8,128)S(1)}, f32[8,3,32,128]{3,2,1,0:T(8,128)S(1)}, u32[]{:S(2)}, u32[]{:S(2)}) collective-permute-start(f32[8,3,32,128]{3,2,1,0:T(8,128)S(1)} %broadcast_add_fusion.1), channel_id=1, source_target_pairs={{0,2},{1,5},{2,0},{3,7},{4,6},{5,1},{6,4},{7,3},{8,10},{9,13},{10,... | collective-permute-start | bytes 1179656 | tf_op jit(solution)/shard_map/ppermute | solution.py:295
  21.5 10.4 %collective-permute-done.5 = f32[8,9,32,128]{3,2,1,0:T(8,128)S(1)} collective-permute-done((f32[8,9,32,128]{3,2,1,0:T(8,128)S(1)}, f32[8,9,32,128]{3,2,1,0:T(8,128)S(1)}, u32[]{:S(2)}, u32[]{:S(2)}) %collective-permute-start.5) | collective-permute-done | bytes 1179680 | tf_op jit(solution)/shard_map/ppermute | solution.py:295
  32.0 2.1 %collective-permute-start.8 = (f32[4,9,32,128]{3,2,1,0:T(8,128)S(1)}, f32[4,9,32,128]{3,2,1,0:T(8,128)S(1)}, u32[]{:S(2)}, u32[]{:S(2)}) collective-permute-start(f32[4,9,32,128]{3,2,1,0:T(8,128)S(1)} %fusion), channel_id=1, source_target_pairs={{0,4},{1,3},{2,6},{3,1},{4,0},{5,7},{6,2},{7,5},{8,12},{9,11},{10,... | collective-permute-start | bytes 1769480 | tf_op jit(solution)/shard_map/ppermute | solution.py:295
  35.4 2.1 %collective-permute-start.7 = (f32[4,5,32,128]{3,2,1,0:T(8,128)S(1)}, f32[4,5,32,128]{3,2,1,0:T(8,128)S(1)}, u32[]{:S(2)}, u32[]{:S(2)}) collective-permute-start(f32[4,5,32,128]{3,2,1,0:T(8,128)S(1)} %fusion.1), channel_id=1, source_target_pairs={{0,16},{1,9},{2,18},{3,11},{4,20},{5,13},{6,22},{7,15},{8,24},{9,1... | collective-permute-start | bytes 983048 | tf_op jit(solution)/shard_map/ppermute | solution.py:295
  37.9 2.4 %collective-permute-start.6 = (f32[4,3,32,128]{3,2,1,0:T(8,128)S(1)}, f32[4,3,32,128]{3,2,1,0:T(8,128)S(1)}, u32[]{:S(2)}, u32[]{:S(2)}) collective-permute-start(f32[4,3,32,128]{3,2,1,0:T(8,128)S(1)} %fusion.3), channel_id=1, source_target_pairs={{0,4},{1,3},{2,6},{3,1},{4,0},{5,7},{6,2},{7,5},{8,12},{9,11},{10,... | collective-permute-start | bytes 589832 | tf_op jit(solution)/shard_map/ppermute | solution.py:295
  40.5 1.5 %collective-permute-done.8 = f32[4,9,32,128]{3,2,1,0:T(8,128)S(1)} collective-permute-done((f32[4,9,32,128]{3,2,1,0:T(8,128)S(1)}, f32[4,9,32,128]{3,2,1,0:T(8,128)S(1)}, u32[]{:S(2)}, u32[]{:S(2)}) %collective-permute-start.8) | collective-permute-done | bytes 589856 | tf_op jit(solution)/shard_map/ppermute | solution.py:295
  42.0 2.1 %collective-permute-start.11 = (f32[2,9,32,128]{3,2,1,0:T(8,128)S(1)}, f32[2,9,32,128]{3,2,1,0:T(8,128)S(1)}, u32[]{:S(2)}, u32[]{:S(2)}) collective-permute-start(f32[2,9,32,128]{3,2,1,0:T(8,128)S(1)} %fusion.2), channel_id=1, source_target_pairs={{0,8},{1,17},{2,10},{3,19},{4,12},{5,21},{6,14},{7,23},{8,0},{9,25... | collective-permute-start | bytes 884744 | tf_op jit(solution)/shard_map/ppermute | solution.py:295
  44.2 1.6 %collective-permute-done.7 = f32[4,5,32,128]{3,2,1,0:T(8,128)S(1)} collective-permute-done((f32[4,5,32,128]{3,2,1,0:T(8,128)S(1)}, f32[4,5,32,128]{3,2,1,0:T(8,128)S(1)}, u32[]{:S(2)}, u32[]{:S(2)}) %collective-permute-start.7) | collective-permute-done | bytes 327712 | tf_op jit(solution)/shard_map/ppermute | solution.py:295
  45.9 2.2 %collective-permute-start.10 = (f32[2,5,32,128]{3,2,1,0:T(8,128)S(1)}, f32[2,5,32,128]{3,2,1,0:T(8,128)S(1)}, u32[]{:S(2)}, u32[]{:S(2)}) collective-permute-start(f32[2,5,32,128]{3,2,1,0:T(8,128)S(1)} %fusion.4), channel_id=1, source_target_pairs={{0,2},{1,5},{2,0},{3,7},{4,6},{5,1},{6,4},{7,3},{8,10},{9,13},{10,... | collective-permute-start | bytes 491528 | tf_op jit(solution)/shard_map/ppermute | solution.py:295
  48.1 1.5 %collective-permute-start.9 = (f32[2,3,32,128]{3,2,1,0:T(8,128)S(1)}, f32[2,3,32,128]{3,2,1,0:T(8,128)S(1)}, u32[]{:S(2)}, u32[]{:S(2)}) collective-permute-start(f32[2,3,32,128]{3,2,1,0:T(8,128)S(1)} %fusion.9), channel_id=1, source_target_pairs={{0,8},{1,17},{2,10},{3,19},{4,12},{5,21},{6,14},{7,23},{8,0},{9,25... | collective-permute-start | bytes 294920 | tf_op jit(solution)/shard_map/ppermute | solution.py:295
  49.6 1.4 %collective-permute-done.11 = f32[2,9,32,128]{3,2,1,0:T(8,128)S(1)} collective-permute-done((f32[2,9,32,128]{3,2,1,0:T(8,128)S(1)}, f32[2,9,32,128]{3,2,1,0:T(8,128)S(1)}, u32[]{:S(2)}, u32[]{:S(2)}) %collective-permute-start.11) | collective-permute-done | bytes 294944 | tf_op jit(solution)/shard_map/ppermute | solution.py:295
  51.1 4.1 %collective-permute-start.14 = (f32[1,9,32,128]{3,2,1,0:T(8,128)S(1)}, f32[1,9,32,128]{3,2,1,0:T(8,128)S(1)}, u32[]{:S(2)}, u32[]{:S(2)}) collective-permute-start(f32[1,9,32,128]{3,2,1,0:T(8,128)S(1)} %fusion.6), channel_id=1, source_target_pairs={{0,16},{1,9},{2,18},{3,11},{4,20},{5,13},{6,22},{7,15},{8,24},{9,1... | collective-permute-start | bytes 442376 | tf_op jit(solution)/shard_map/ppermute | solution.py:295
  55.2 1.6 %collective-permute-start.13 = (f32[1,5,32,128]{3,2,1,0:T(8,128)S(1)}, f32[1,5,32,128]{3,2,1,0:T(8,128)S(1)}, u32[]{:S(2)}, u32[]{:S(2)}) collective-permute-start(f32[1,5,32,128]{3,2,1,0:T(8,128)S(1)} %fusion.13), channel_id=1, source_target_pairs={{0,4},{1,3},{2,6},{3,1},{4,0},{5,7},{6,2},{7,5},{8,12},{9,11},{10,... | collective-permute-start | bytes 245768 | tf_op jit(solution)/shard_map/ppermute | solution.py:295
  56.9 1.6 %collective-permute-done.14 = f32[1,9,32,128]{3,2,1,0:T(8,128)S(1)} collective-permute-done((f32[1,9,32,128]{3,2,1,0:T(8,128)S(1)}, f32[1,9,32,128]{3,2,1,0:T(8,128)S(1)}, u32[]{:S(2)}, u32[]{:S(2)}) %collective-permute-start.14) | collective-permute-done | bytes 147488 | tf_op jit(solution)/shard_map/ppermute | solution.py:295
  59.8 4.7 %collective-permute-start.19 = (f32[4,32,128]{2,1,0:T(8,128)S(1)}, f32[4,32,128]{2,1,0:T(8,128)S(1)}, u32[]{:S(2)}, u32[]{:S(2)}) collective-permute-start(f32[4,32,128]{2,1,0:T(8,128)S(1)} %pad_maximum_fusion.5), channel_id=1, source_target_pairs={{0,24},{2,26},{4,28},{6,30},{8,16},{10,18},{12,20},{14,22},{16,8},... | collective-permute-start | bytes 196616 | tf_op jit(solution)/shard_map/ppermute | solution.py:240
  64.6 1.8 %collective-permute-start.15 = (f32[2,4,32,128]{3,2,1,0:T(8,128)S(1)}, f32[2,4,32,128]{3,2,1,0:T(8,128)S(1)}, u32[]{:S(2)}, u32[]{:S(2)}) collective-permute-start(f32[2,4,32,128]{3,2,1,0:T(8,128)S(1)} %pad_maximum_fusion.1), channel_id=1, source_target_pairs={{0,2},{1,5},{2,0},{3,7},{4,6},{5,1},{6,4},{7,3},{8,10},{9,13},{10,... | collective-permute-start | bytes 393224 | tf_op jit(solution)/shard_map/ppermute | solution.py:295
  67.0 3.9 %collective-permute-done.15 = f32[2,4,32,128]{3,2,1,0:T(8,128)S(1)} collective-permute-done((f32[2,4,32,128]{3,2,1,0:T(8,128)S(1)}, f32[2,4,32,128]{3,2,1,0:T(8,128)S(1)}, u32[]{:S(2)}, u32[]{:S(2)}) %collective-permute-start.15) | collective-permute-done | bytes 131104 | tf_op jit(solution)/shard_map/ppermute | solution.py:295
  70.9 1.6 %collective-permute-start.16 = (f32[2,4,32,128]{3,2,1,0:T(8,128)S(1)}, f32[2,4,32,128]{3,2,1,0:T(8,128)S(1)}, u32[]{:S(2)}, u32[]{:S(2)}) collective-permute-start(f32[2,4,32,128]{3,2,1,0:T(8,128)S(1)} %pad_maximum_fusion.2), channel_id=1, source_target_pairs={{0,4},{1,3},{2,6},{3,1},{4,0},{5,7},{6,2},{7,5},{8,12},{9,11},{10,... | collective-permute-start | bytes 393224 | tf_op jit(solution)/shard_map/ppermute | solution.py:295
  72.5 3.4 %collective-permute-done.16 = f32[2,4,32,128]{3,2,1,0:T(8,128)S(1)} collective-permute-done((f32[2,4,32,128]{3,2,1,0:T(8,128)S(1)}, f32[2,4,32,128]{3,2,1,0:T(8,128)S(1)}, u32[]{:S(2)}, u32[]{:S(2)}) %collective-permute-start.16) | collective-permute-done | bytes 131104 | tf_op jit(solution)/shard_map/ppermute | solution.py:295
  78.0 1.6 %place.1 = f32[128,1024]{1,0:T(8,128)} custom-call(s32[16]{0:T(128)S(1)} %copy-done, f32[8,32,128]{2,1,0:T(8,128)S(1)} %pad_maximum_fusion.refs_0_, f32[24,32,128]{2,1,0:T(8,128)S(1)} %constant_dynamic-update-slice_fusion.refs_1_, f32[8,32,128]{2,1,0:T(8,128)S(1)} %collective-permute-done.20.refs_2_, f32[24,32,128]{2,1,0:T(8,128)S(1)} %collective-permute-done.21.refs_3_), custom_call_target="tpu_custom_call" | custom-call | tf_op jit(solution)/shard_map/place/pallas_call | solution.py:340
  (85 shorter events, 8.1 us)
Async XLA Ops:
  10.8 3.0 %collective-permute-start = (f32[2304,128]{1,0:T(8,128)S(1)}, f32[2304,128]{1,0:T(8,128)S(1)}, u32[]{:S(2)}, u32[]{:S(2)}) collective-permute-start(f32[2304,128]{1,0:T(8,128)S(1)} %slice_bitcast_fusion), channel_id=1, source_target_pairs={{0,1},{1,0},{2,3},{3,2},{4,5},{5,4},{6,7},{7,6},{8,9},{9,8},{10,11... | collective-permute-start | bytes 3538952 | tf_op jit(solution)/shard_map/ppermute | solution.py:241
  13.8 3.9 %collective-permute-start.2 = (f32[2048,128]{1,0:T(8,128)S(1)}, f32[2048,128]{1,0:T(8,128)S(1)}, u32[]{:S(2)}, u32[]{:S(2)}) collective-permute-start(f32[2048,128]{1,0:T(8,128)S(1)} %bitcast_add_fusion.1), channel_id=1, source_target_pairs={{0,1},{1,0},{2,3},{3,2},{4,5},{5,4},{6,7},{7,6},{8,9},{9,8},{10,11... | collective-permute-start | bytes 3145736 | tf_op jit(solution)/shard_map/ppermute | solution.py:241
  14.4 7.0 %collective-permute-start.1 = (f32[4352,128]{1,0:T(8,128)S(1)}, f32[4352,128]{1,0:T(8,128)S(1)}, u32[]{:S(2)}, u32[]{:S(2)}) collective-permute-start(f32[4352,128]{1,0:T(8,128)S(1)} %bitcast_add_fusion), channel_id=1, source_target_pairs={{0,1},{1,0},{2,3},{3,2},{4,5},{5,4},{6,7},{7,6},{8,9},{9,8},{10,11... | collective-permute-start | bytes 6684680 | tf_op jit(solution)/shard_map/ppermute | solution.py:241
  14.8 17.1 %collective-permute-start.5 = (f32[8,9,32,128]{3,2,1,0:T(8,128)S(1)}, f32[8,9,32,128]{3,2,1,0:T(8,128)S(1)}, u32[]{:S(2)}, u32[]{:S(2)}) collective-permute-start(f32[8,9,32,128]{3,2,1,0:T(8,128)S(1)} %bitcast.98), channel_id=1, source_target_pairs={{0,2},{1,5},{2,0},{3,7},{4,6},{5,1},{6,4},{7,3},{8,10},{9,13},{10,... | collective-permute-start | bytes 3538952 | tf_op jit(solution)/shard_map/ppermute | solution.py:295
  17.9 17.5 %collective-permute-start.4 = (f32[8,5,32,128]{3,2,1,0:T(8,128)S(1)}, f32[8,5,32,128]{3,2,1,0:T(8,128)S(1)}, u32[]{:S(2)}, u32[]{:S(2)}) collective-permute-start(f32[8,5,32,128]{3,2,1,0:T(8,128)S(1)} %broadcast_add_fusion), channel_id=1, source_target_pairs={{0,8},{1,17},{2,10},{3,19},{4,12},{5,21},{6,14},{7,23},{8,0},{9,25... | collective-permute-start | bytes 1966088 | tf_op jit(solution)/shard_map/ppermute | solution.py:295
  19.8 18.0 %collective-permute-start.3 = (f32[8,3,32,128]{3,2,1,0:T(8,128)S(1)}, f32[8,3,32,128]{3,2,1,0:T(8,128)S(1)}, u32[]{:S(2)}, u32[]{:S(2)}) collective-permute-start(f32[8,3,32,128]{3,2,1,0:T(8,128)S(1)} %broadcast_add_fusion.1), channel_id=1, source_target_pairs={{0,2},{1,5},{2,0},{3,7},{4,6},{5,1},{6,4},{7,3},{8,10},{9,13},{10,... | collective-permute-start | bytes 1179656 | tf_op jit(solution)/shard_map/ppermute | solution.py:295
  32.0 10.0 %collective-permute-start.8 = (f32[4,9,32,128]{3,2,1,0:T(8,128)S(1)}, f32[4,9,32,128]{3,2,1,0:T(8,128)S(1)}, u32[]{:S(2)}, u32[]{:S(2)}) collective-permute-start(f32[4,9,32,128]{3,2,1,0:T(8,128)S(1)} %fusion), channel_id=1, source_target_pairs={{0,4},{1,3},{2,6},{3,1},{4,0},{5,7},{6,2},{7,5},{8,12},{9,11},{10,... | collective-permute-start | bytes 1769480 | tf_op jit(solution)/shard_map/ppermute | solution.py:295
  35.4 10.4 %collective-permute-start.7 = (f32[4,5,32,128]{3,2,1,0:T(8,128)S(1)}, f32[4,5,32,128]{3,2,1,0:T(8,128)S(1)}, u32[]{:S(2)}, u32[]{:S(2)}) collective-permute-start(f32[4,5,32,128]{3,2,1,0:T(8,128)S(1)} %fusion.1), channel_id=1, source_target_pairs={{0,16},{1,9},{2,18},{3,11},{4,20},{5,13},{6,22},{7,15},{8,24},{9,1... | collective-permute-start | bytes 983048 | tf_op jit(solution)/shard_map/ppermute | solution.py:295
  37.9 10.1 %collective-permute-start.6 = (f32[4,3,32,128]{3,2,1,0:T(8,128)S(1)}, f32[4,3,32,128]{3,2,1,0:T(8,128)S(1)}, u32[]{:S(2)}, u32[]{:S(2)}) collective-permute-start(f32[4,3,32,128]{3,2,1,0:T(8,128)S(1)} %fusion.3), channel_id=1, source_target_pairs={{0,4},{1,3},{2,6},{3,1},{4,0},{5,7},{6,2},{7,5},{8,12},{9,11},{10,... | collective-permute-start | bytes 589832 | tf_op jit(solution)/shard_map/ppermute | solution.py:295
  42.0 9.0 %collective-permute-start.11 = (f32[2,9,32,128]{3,2,1,0:T(8,128)S(1)}, f32[2,9,32,128]{3,2,1,0:T(8,128)S(1)}, u32[]{:S(2)}, u32[]{:S(2)}) collective-permute-start(f32[2,9,32,128]{3,2,1,0:T(8,128)S(1)} %fusion.2), channel_id=1, source_target_pairs={{0,8},{1,17},{2,10},{3,19},{4,12},{5,21},{6,14},{7,23},{8,0},{9,25... | collective-permute-start | bytes 884744 | tf_op jit(solution)/shard_map/ppermute | solution.py:295
  45.9 9.3 %collective-permute-start.10 = (f32[2,5,32,128]{3,2,1,0:T(8,128)S(1)}, f32[2,5,32,128]{3,2,1,0:T(8,128)S(1)}, u32[]{:S(2)}, u32[]{:S(2)}) collective-permute-start(f32[2,5,32,128]{3,2,1,0:T(8,128)S(1)} %fusion.4), channel_id=1, source_target_pairs={{0,2},{1,5},{2,0},{3,7},{4,6},{5,1},{6,4},{7,3},{8,10},{9,13},{10,... | collective-permute-start | bytes 491528 | tf_op jit(solution)/shard_map/ppermute | solution.py:295
  48.1 8.7 %collective-permute-start.9 = (f32[2,3,32,128]{3,2,1,0:T(8,128)S(1)}, f32[2,3,32,128]{3,2,1,0:T(8,128)S(1)}, u32[]{:S(2)}, u32[]{:S(2)}) collective-permute-start(f32[2,3,32,128]{3,2,1,0:T(8,128)S(1)} %fusion.9), channel_id=1, source_target_pairs={{0,8},{1,17},{2,10},{3,19},{4,12},{5,21},{6,14},{7,23},{8,0},{9,25... | collective-permute-start | bytes 294920 | tf_op jit(solution)/shard_map/ppermute | solution.py:295
  51.1 7.4 %collective-permute-start.14 = (f32[1,9,32,128]{3,2,1,0:T(8,128)S(1)}, f32[1,9,32,128]{3,2,1,0:T(8,128)S(1)}, u32[]{:S(2)}, u32[]{:S(2)}) collective-permute-start(f32[1,9,32,128]{3,2,1,0:T(8,128)S(1)} %fusion.6), channel_id=1, source_target_pairs={{0,16},{1,9},{2,18},{3,11},{4,20},{5,13},{6,22},{7,15},{8,24},{9,1... | collective-permute-start | bytes 442376 | tf_op jit(solution)/shard_map/ppermute | solution.py:295
  55.2 4.5 %collective-permute-start.13 = (f32[1,5,32,128]{3,2,1,0:T(8,128)S(1)}, f32[1,5,32,128]{3,2,1,0:T(8,128)S(1)}, u32[]{:S(2)}, u32[]{:S(2)}) collective-permute-start(f32[1,5,32,128]{3,2,1,0:T(8,128)S(1)} %fusion.13), channel_id=1, source_target_pairs={{0,4},{1,3},{2,6},{3,1},{4,0},{5,7},{6,2},{7,5},{8,12},{9,11},{10,... | collective-permute-start | bytes 245768 | tf_op jit(solution)/shard_map/ppermute | solution.py:295
  56.8 7.7 %collective-permute-start.12 = (f32[1,3,32,128]{3,2,1,0:T(8,128)S(1)}, f32[1,3,32,128]{3,2,1,0:T(8,128)S(1)}, u32[]{:S(2)}, u32[]{:S(2)}) collective-permute-start(f32[1,3,32,128]{3,2,1,0:T(8,128)S(1)} %fusion.20), channel_id=1, source_target_pairs={{0,16},{1,9},{2,18},{3,11},{4,20},{5,13},{6,22},{7,15},{8,24},{9,1... | collective-permute-start | bytes 147464 | tf_op jit(solution)/shard_map/ppermute | solution.py:295
  58.6 19.4 %copy-start = (s32[16]{0:T(128)S(1)}, s32[16]{0:T(128)}, u32[]{:S(2)}) copy-start(s32[16]{0:T(128)} %owner_ref.1) | copy-start | bytes 196
  59.8 16.2 %collective-permute-start.19 = (f32[4,32,128]{2,1,0:T(8,128)S(1)}, f32[4,32,128]{2,1,0:T(8,128)S(1)}, u32[]{:S(2)}, u32[]{:S(2)}) collective-permute-start(f32[4,32,128]{2,1,0:T(8,128)S(1)} %pad_maximum_fusion.5), channel_id=1, source_target_pairs={{0,24},{2,26},{4,28},{6,30},{8,16},{10,18},{12,20},{14,22},{16,8},... | collective-permute-start | bytes 196616 | tf_op jit(solution)/shard_map/ppermute | solution.py:240
  64.5 11.5 %collective-permute-start.18 = (f32[4,32,128]{2,1,0:T(8,128)S(1)}, f32[4,32,128]{2,1,0:T(8,128)S(1)}, u32[]{:S(2)}, u32[]{:S(2)}) collective-permute-start(f32[4,32,128]{2,1,0:T(8,128)S(1)} %pad_maximum_fusion.4), channel_id=1, source_target_pairs={{0,16},{2,18},{4,20},{6,22},{8,24},{10,26},{12,28},{14,30},{16,0},... | collective-permute-start | bytes 196616 | tf_op jit(solution)/shard_map/ppermute | solution.py:240
  64.6 6.3 %collective-permute-start.15 = (f32[2,4,32,128]{3,2,1,0:T(8,128)S(1)}, f32[2,4,32,128]{3,2,1,0:T(8,128)S(1)}, u32[]{:S(2)}, u32[]{:S(2)}) collective-permute-start(f32[2,4,32,128]{3,2,1,0:T(8,128)S(1)} %pad_maximum_fusion.1), channel_id=1, source_target_pairs={{0,2},{1,5},{2,0},{3,7},{4,6},{5,1},{6,4},{7,3},{8,10},{9,13},{10,... | collective-permute-start | bytes 393224 | tf_op jit(solution)/shard_map/ppermute | solution.py:295
  66.3 9.6 %collective-permute-start.17 = (f32[4,32,128]{2,1,0:T(8,128)S(1)}, f32[4,32,128]{2,1,0:T(8,128)S(1)}, u32[]{:S(2)}, u32[]{:S(2)}) collective-permute-start(f32[4,32,128]{2,1,0:T(8,128)S(1)} %pad_maximum_fusion.3), channel_id=1, source_target_pairs={{0,8},{2,10},{4,12},{6,14},{8,0},{10,2},{12,4},{14,6},{16,24},{18,... | collective-permute-start | bytes 196616 | tf_op jit(solution)/shard_map/ppermute | solution.py:240
  70.9 5.0 %collective-permute-start.16 = (f32[2,4,32,128]{3,2,1,0:T(8,128)S(1)}, f32[2,4,32,128]{3,2,1,0:T(8,128)S(1)}, u32[]{:S(2)}, u32[]{:S(2)}) collective-permute-start(f32[2,4,32,128]{3,2,1,0:T(8,128)S(1)} %pad_maximum_fusion.2), channel_id=1, source_target_pairs={{0,4},{1,3},{2,6},{3,1},{4,0},{5,7},{6,2},{7,5},{8,12},{9,11},{10,... | collective-permute-start | bytes 393224 | tf_op jit(solution)/shard_map/ppermute | solution.py:295
  76.0 2.0 %collective-permute-start.21 = (f32[24,32,128]{2,1,0:T(8,128)S(1)}, f32[24,32,128]{2,1,0:T(8,128)S(1)}, u32[]{:S(2)}, u32[]{:S(2)}) collective-permute-start(f32[24,32,128]{2,1,0:T(8,128)S(1)} %constant_dynamic-update-slice_fusion.refs_1_), channel_id=1, source_target_pairs={{0,1},{1,0},{2,3},{3,2},{4,5},{5,4},{6,7},{7,6},{8,9},{9,8},{10,11... | collective-permute-start | bytes 1179656 | tf_op jit(solution)/shard_map/ppermute | solution.py:241
  76.1 1.9 %collective-permute-start.20 = (f32[8,32,128]{2,1,0:T(8,128)S(1)}, f32[8,32,128]{2,1,0:T(8,128)S(1)}, u32[]{:S(2)}, u32[]{:S(2)}) collective-permute-start(f32[8,32,128]{2,1,0:T(8,128)S(1)} %pad_maximum_fusion.refs_0_), channel_id=1, source_target_pairs={{0,1},{1,0},{2,3},{3,2},{4,5},{5,4},{6,7},{7,6},{8,9},{9,8},{10,11... | collective-permute-start | bytes 393224 | tf_op jit(solution)/shard_map/ppermute | solution.py:241

commit v4 on v3

--- a/solution.py
+++ b/solution.py
@@ -34,27 +34,32 @@
             low, high = low[::-1], high[::-1]
         return high + low if name == "line" else low + high
 
+    def place(self, d, bits, parity):
+        if parity and d >= 0:
+            return sum((d >> b & 1) << (bits - 1 - b) for b in range(bits))
+        return d
+
     def table(self):
         out = np.zeros((self.chips, self.chips + 1, 2), np.int32)
         for j in range(self.chips):
             for unit in range(self.chips + 1):
                 dz, dp = (unit // PLANE, unit % PLANE) if unit < self.chips else (-1, 0)
                 for parity in range(2):
-                    i = dp - 1 if dp == 3 else (dp - 1) ^ parity
+                    p, q = self.place(dp, 2, parity), self.place(dz, self.bits - 2, parity)
                     if dp == 0:
-                        name, i = "line", 1 + dz
+                        name, i = "line", 1 + q
                     elif dz == 0:
-                        name = "plane"
+                        name, i = "plane", p - 1
                     else:
-                        name, i = "cross", i * (self.lines - 1) + dz - 1
-                    place = 0
+                        name, i = "cross", (p - 1) * (self.lines - 1) + q - 1
+                    row = 0
                     at = j ^ dp if name == "cross" else j
                     for bit in self.order(name, parity):
-                        place = 2 * place + (at >> bit & 1)
+                        row = 2 * row + (at >> bit & 1)
                     half = self.chips // 2
-                    base = self.at[name, "s" if place >= half else "k"][0]
-                    place = (place % half) * self.count[name] + i
-                    out[j, unit, parity] = base + place * self.rows
+                    base = self.at[name, "s" if row >= half else "k"][0]
+                    row = (row % half) * self.count[name] + i
+                    out[j, unit, parity] = base + row * self.rows
         return out.reshape(-1)
 
 
@@ -198,19 +203,22 @@
         parity = (o ^ core) & 1
         for d in range(sz.chips):
             dp, dz = d % PLANE, d // PLANE
-            i = dp - 1 if dp == 3 else (dp - 1) ^ parity
+            p, q = [
+                jnp.where(parity == 0, sz.place(x, bits, 0), sz.place(x, bits, 1))
+                for x, bits in ((dp, 2), (dz, sz.bits - 2))
+            ]
             if dp == 0:
-                mine = own[n_plane + 1 + dz]
+                mine = own[n_plane + 1 + q]
             elif dz == 0:
-                mine = own[i]
+                mine = own[p - 1]
             else:
-                mine = far[i * sz.lines + dz]
+                mine = far[(p - 1) * sz.lines + q]
             if d == 0:
                 other = own[n_plane]
             elif dz == 0:
-                other = far[i * sz.lines]
+                other = far[(p - 1) * sz.lines]
             else:
-                other = far[n_plane * sz.lines + (dz - 1) * PLANE + (1 + i if dp else 0)]
+                other = far[n_plane * sz.lines + (q - 1) * PLANE + p]
             top = (me >> (d.bit_length() - 1)) & 1 if d else 0
             tiles[d, pl.ds(pl.multiple_of(top * half + shift, sz.rows), sz.rows), :] = mine
             tiles[d, pl.ds(pl.multiple_of((1 - top) * half + shift, sz.rows), sz.rows), :] = other
@@ -322,15 +330,17 @@
     line = total(parts["line"])[0] + 0 * cross[:1]
     plane = total(parts["plane"])[0] + 0 * line[:1]
     cross = cross.reshape(PLANE - 1, lines - 1, rows, tile)
-    near = [jnp.concatenate([plane[i:i + 1], cross[i]]) for i in range(PLANE - 1)]
-    far = [
-        jnp.concatenate([line[1 + dz:2 + dz], cross[:, dz - 1]]) for dz in range(1, lines)
-    ]
-    sent = jnp.stack([near[0], near[2]])
-    far = [go(x, chip=dz * PLANE) for dz, x in enumerate(far, 1)]
-    come = step(sent, "plane", 0)
-    last = step(jnp.stack([near[1], come[1]]), "plane", 1)
-    near = [come[0], last[0], last[1]]
+    def across(blocks, name):
+        for k in range(len(blocks).bit_length() - 1):
+            moved = [q for q in range(len(blocks)) if q >> k & 1]
+            come = step(jnp.stack([blocks[q] for q in moved]), name, k)
+            for i, q in enumerate(moved):
+                blocks[q] = come[i]
+        return blocks[1:]
+
+    far = [jnp.concatenate([line[1 + q:2 + q], cross[:, q - 1]]) for q in range(1, lines)]
+    near = [jnp.concatenate([plane[q - 1:q], cross[q - 1]]) for q in range(1, PLANE)]
+    far, near = across([None] + far, "line"), across([None] + near, "plane")
     own = jnp.concatenate([plane, line])
     far = jnp.concatenate(near + far)
     every = [own, far]

time: 79.8 us -> 77.5 us (0.971)
  starting transfers between devices: 35 us -> 33.6 us
  waiting for transfers between devices: 30.2 us -> 29.4 us
    ppermute x3 -> x0, starting transfers between devices: 5.32 us -> none  [go(): return lax.ppermute(x, 'aux', [(j, j ^ chip) for j in range(chips)])]
    ppermute x14 -> x16, starting transfers between devices: 27.9 us -> 31.8 us  [step(): return lax.ppermute(x, ('aux', 'occ'), pairs)]
    ppermute x14 -> x16, waiting for transfers between devices: 26.4 us -> 25.6 us  [step(): return lax.ppermute(x, ('aux', 'occ'), pairs)]
  transfers between devices with their start and end apart: 22 -> 21, of which waited for: 12 -> 13; matrix products, arithmetic and copies ran while one was open for 2% -> 2% of each run, Pallas kernels for 0% -> 0%
where the time goes in v4:
time: 77.5 us; the launch traced here: 77.3 us
  starting transfers between devices  33.6 us (43%)
  waiting for transfers between devices  29.4 us (38%)
  Pallas kernels  12.3 us (16%)
  other arithmetic  1.58 us (2%)
    ppermute x16, starting transfers between devices, step(): return lax.ppermute(x, ('aux', 'occ'), pairs)  31.8 us
    ppermute x16, waiting for transfers between devices, step(): return lax.ppermute(x, ('aux', 'occ'), pairs)  25.6 us
    pallas_call x1, Pallas kernels, local(): pl.pallas_call(functools.partial(pair_kernel, sz), out_shape=[space((sz.t...  10.7 us
    ppermute x5, waiting for transfers between devices, go(): return lax.ppermute(x, 'occ', [(j, j ^ core) for j in range(cores)])  3.8 us
    ppermute x5, starting transfers between devices, go(): return lax.ppermute(x, 'occ', [(j, j ^ core) for j in range(cores)])  1.79 us
    pallas_call x1, Pallas kernels, local(): pl.pallas_call(functools.partial(place_kernel, sz), out_shape=jax.ShapeDt...  1.6 us
  transfers between devices with their start and end apart: 21, of which 13 were waited for; matrix products, arithmetic and copies ran while one was open for 2% of the time, Pallas kernels for 0%

profile of v4, /device:TPU:0, one launch (start us, length us, event | category | flops | bytes accessed | tf_op | source)
XLA Modules:
  0.0 77.3 jit_solution(4771359172216674097)
XLA Ops:
  0.0 10.7 %pairs.1 = (f32[8704,128]{1,0:T(8,128)S(1)}, f32[1,8704,128]{2,1,0:T(8,128)S(1)}) custom-call(s32[1,4,6]{2,1,0:T(4,128)} %slots_hbm.1, s32[16]{0:T(128)} %owner_ref.1, s32[544]{0:T(1024)} %constant.3.clone.table_hbm, bf16[1,4,6,128,1024]{4,3,2,1,0:T(8,128)(2,1)} %x_ref.1, bf16[4,128,128]{2,1,0:T(8,128)(2,1)} %fit_hbm.1), custom_call_target="tpu_custom_call" | custom-call | tf_op jit(solution)/shard_map/pairs/pallas_call | solution.py:256
  11.3 2.5 %collective-permute-done = f32[2304,128]{1,0:T(8,128)S(1)} collective-permute-done((f32[2304,128]{1,0:T(8,128)S(1)}, f32[2304,128]{1,0:T(8,128)S(1)}, u32[]{:S(2)}, u32[]{:S(2)}) %collective-permute-start) | collective-permute-done | bytes 1179680 | tf_op jit(solution)/shard_map/ppermute | solution.py:249
  14.8 2.9 %collective-permute-start.5 = (f32[8,9,32,128]{3,2,1,0:T(8,128)S(1)}, f32[8,9,32,128]{3,2,1,0:T(8,128)S(1)}, u32[]{:S(2)}, u32[]{:S(2)}) collective-permute-start(f32[8,9,32,128]{3,2,1,0:T(8,128)S(1)} %bitcast.116), channel_id=1, source_target_pairs={{0,2},{1,5},{2,0},{3,7},{4,6},{5,1},{6,4},{7,3},{8,10},{9,13},{10,... | collective-permute-start | bytes 3538952 | tf_op jit(solution)/shard_map/ppermute | solution.py:303
  17.9 1.9 %collective-permute-start.4 = (f32[8,5,32,128]{3,2,1,0:T(8,128)S(1)}, f32[8,5,32,128]{3,2,1,0:T(8,128)S(1)}, u32[]{:S(2)}, u32[]{:S(2)}) collective-permute-start(f32[8,5,32,128]{3,2,1,0:T(8,128)S(1)} %broadcast_add_fusion), channel_id=1, source_target_pairs={{0,8},{1,17},{2,10},{3,19},{4,12},{5,21},{6,14},{7,23},{8,0},{9,25... | collective-permute-start | bytes 1966088 | tf_op jit(solution)/shard_map/ppermute | solution.py:303
  19.8 1.6 %collective-permute-start.3 = (f32[8,3,32,128]{3,2,1,0:T(8,128)S(1)}, f32[8,3,32,128]{3,2,1,0:T(8,128)S(1)}, u32[]{:S(2)}, u32[]{:S(2)}) collective-permute-start(f32[8,3,32,128]{3,2,1,0:T(8,128)S(1)} %broadcast_add_fusion.1), channel_id=1, source_target_pairs={{0,2},{1,5},{2,0},{3,7},{4,6},{5,1},{6,4},{7,3},{8,10},{9,13},{10,... | collective-permute-start | bytes 1179656 | tf_op jit(solution)/shard_map/ppermute | solution.py:303
  21.5 10.4 %collective-permute-done.5 = f32[8,9,32,128]{3,2,1,0:T(8,128)S(1)} collective-permute-done((f32[8,9,32,128]{3,2,1,0:T(8,128)S(1)}, f32[8,9,32,128]{3,2,1,0:T(8,128)S(1)}, u32[]{:S(2)}, u32[]{:S(2)}) %collective-permute-start.5) | collective-permute-done | bytes 1179680 | tf_op jit(solution)/shard_map/ppermute | solution.py:303
  32.0 2.1 %collective-permute-start.8 = (f32[4,9,32,128]{3,2,1,0:T(8,128)S(1)}, f32[4,9,32,128]{3,2,1,0:T(8,128)S(1)}, u32[]{:S(2)}, u32[]{:S(2)}) collective-permute-start(f32[4,9,32,128]{3,2,1,0:T(8,128)S(1)} %fusion), channel_id=1, source_target_pairs={{0,4},{1,3},{2,6},{3,1},{4,0},{5,7},{6,2},{7,5},{8,12},{9,11},{10,... | collective-permute-start | bytes 1769480 | tf_op jit(solution)/shard_map/ppermute | solution.py:303
  35.4 2.2 %collective-permute-start.7 = (f32[4,5,32,128]{3,2,1,0:T(8,128)S(1)}, f32[4,5,32,128]{3,2,1,0:T(8,128)S(1)}, u32[]{:S(2)}, u32[]{:S(2)}) collective-permute-start(f32[4,5,32,128]{3,2,1,0:T(8,128)S(1)} %fusion.1), channel_id=1, source_target_pairs={{0,16},{1,9},{2,18},{3,11},{4,20},{5,13},{6,22},{7,15},{8,24},{9,1... | collective-permute-start | bytes 983048 | tf_op jit(solution)/shard_map/ppermute | solution.py:303
  37.9 2.4 %collective-permute-start.6 = (f32[4,3,32,128]{3,2,1,0:T(8,128)S(1)}, f32[4,3,32,128]{3,2,1,0:T(8,128)S(1)}, u32[]{:S(2)}, u32[]{:S(2)}) collective-permute-start(f32[4,3,32,128]{3,2,1,0:T(8,128)S(1)} %fusion.3), channel_id=1, source_target_pairs={{0,4},{1,3},{2,6},{3,1},{4,0},{5,7},{6,2},{7,5},{8,12},{9,11},{10,... | collective-permute-start | bytes 589832 | tf_op jit(solution)/shard_map/ppermute | solution.py:303
  40.5 1.5 %collective-permute-done.8 = f32[4,9,32,128]{3,2,1,0:T(8,128)S(1)} collective-permute-done((f32[4,9,32,128]{3,2,1,0:T(8,128)S(1)}, f32[4,9,32,128]{3,2,1,0:T(8,128)S(1)}, u32[]{:S(2)}, u32[]{:S(2)}) %collective-permute-start.8) | collective-permute-done | bytes 589856 | tf_op jit(solution)/shard_map/ppermute | solution.py:303
  42.0 2.1 %collective-permute-start.11 = (f32[2,9,32,128]{3,2,1,0:T(8,128)S(1)}, f32[2,9,32,128]{3,2,1,0:T(8,128)S(1)}, u32[]{:S(2)}, u32[]{:S(2)}) collective-permute-start(f32[2,9,32,128]{3,2,1,0:T(8,128)S(1)} %fusion.2), channel_id=1, source_target_pairs={{0,8},{1,17},{2,10},{3,19},{4,12},{5,21},{6,14},{7,23},{8,0},{9,25... | collective-permute-start | bytes 884744 | tf_op jit(solution)/shard_map/ppermute | solution.py:303
  44.2 1.6 %collective-permute-done.7 = f32[4,5,32,128]{3,2,1,0:T(8,128)S(1)} collective-permute-done((f32[4,5,32,128]{3,2,1,0:T(8,128)S(1)}, f32[4,5,32,128]{3,2,1,0:T(8,128)S(1)}, u32[]{:S(2)}, u32[]{:S(2)}) %collective-permute-start.7) | collective-permute-done | bytes 327712 | tf_op jit(solution)/shard_map/ppermute | solution.py:303
  45.8 2.2 %collective-permute-start.10 = (f32[2,5,32,128]{3,2,1,0:T(8,128)S(1)}, f32[2,5,32,128]{3,2,1,0:T(8,128)S(1)}, u32[]{:S(2)}, u32[]{:S(2)}) collective-permute-start(f32[2,5,32,128]{3,2,1,0:T(8,128)S(1)} %fusion.4), channel_id=1, source_target_pairs={{0,2},{1,5},{2,0},{3,7},{4,6},{5,1},{6,4},{7,3},{8,10},{9,13},{10,... | collective-permute-start | bytes 491528 | tf_op jit(solution)/shard_map/ppermute | solution.py:303
  48.1 1.5 %collective-permute-start.9 = (f32[2,3,32,128]{3,2,1,0:T(8,128)S(1)}, f32[2,3,32,128]{3,2,1,0:T(8,128)S(1)}, u32[]{:S(2)}, u32[]{:S(2)}) collective-permute-start(f32[2,3,32,128]{3,2,1,0:T(8,128)S(1)} %fusion.9), channel_id=1, source_target_pairs={{0,8},{1,17},{2,10},{3,19},{4,12},{5,21},{6,14},{7,23},{8,0},{9,25... | collective-permute-start | bytes 294920 | tf_op jit(solution)/shard_map/ppermute | solution.py:303
  51.1 4.1 %collective-permute-start.14 = (f32[1,9,32,128]{3,2,1,0:T(8,128)S(1)}, f32[1,9,32,128]{3,2,1,0:T(8,128)S(1)}, u32[]{:S(2)}, u32[]{:S(2)}) collective-permute-start(f32[1,9,32,128]{3,2,1,0:T(8,128)S(1)} %fusion.6), channel_id=1, source_target_pairs={{0,16},{1,9},{2,18},{3,11},{4,20},{5,13},{6,22},{7,15},{8,24},{9,1... | collective-permute-start | bytes 442376 | tf_op jit(solution)/shard_map/ppermute | solution.py:303
  55.2 1.6 %collective-permute-start.13 = (f32[1,5,32,128]{3,2,1,0:T(8,128)S(1)}, f32[1,5,32,128]{3,2,1,0:T(8,128)S(1)}, u32[]{:S(2)}, u32[]{:S(2)}) collective-permute-start(f32[1,5,32,128]{3,2,1,0:T(8,128)S(1)} %fusion.13), channel_id=1, source_target_pairs={{0,4},{1,3},{2,6},{3,1},{4,0},{5,7},{6,2},{7,5},{8,12},{9,11},{10,... | collective-permute-start | bytes 245768 | tf_op jit(solution)/shard_map/ppermute | solution.py:303
  56.9 1.6 %collective-permute-done.14 = f32[1,9,32,128]{3,2,1,0:T(8,128)S(1)} collective-permute-done((f32[1,9,32,128]{3,2,1,0:T(8,128)S(1)}, f32[1,9,32,128]{3,2,1,0:T(8,128)S(1)}, u32[]{:S(2)}, u32[]{:S(2)}) %collective-permute-start.14) | collective-permute-done | bytes 147488 | tf_op jit(solution)/shard_map/ppermute | solution.py:303
  59.8 2.2 %collective-permute-start.17 = (f32[2,4,32,128]{3,2,1,0:T(8,128)S(1)}, f32[2,4,32,128]{3,2,1,0:T(8,128)S(1)}, u32[]{:S(2)}, u32[]{:S(2)}) collective-permute-start(f32[2,4,32,128]{3,2,1,0:T(8,128)S(1)} %pad_maximum_fusion.3), channel_id=1, source_target_pairs={{0,8},{1,17},{2,10},{3,19},{4,12},{5,21},{6,14},{7,23},{8,0},{9,25... | collective-permute-start | bytes 393224 | tf_op jit(solution)/shard_map/ppermute | solution.py:303
  62.1 1.7 %collective-permute-start.15 = (f32[2,4,32,128]{3,2,1,0:T(8,128)S(1)}, f32[2,4,32,128]{3,2,1,0:T(8,128)S(1)}, u32[]{:S(2)}, u32[]{:S(2)}) collective-permute-start(f32[2,4,32,128]{3,2,1,0:T(8,128)S(1)} %pad_maximum_fusion.1), channel_id=1, source_target_pairs={{0,2},{1,5},{2,0},{3,7},{4,6},{5,1},{6,4},{7,3},{8,10},{9,13},{10,... | collective-permute-start | bytes 393224 | tf_op jit(solution)/shard_map/ppermute | solution.py:303
  63.8 2.6 %collective-permute-done.17 = f32[2,4,32,128]{3,2,1,0:T(8,128)S(1)} collective-permute-done((f32[2,4,32,128]{3,2,1,0:T(8,128)S(1)}, f32[2,4,32,128]{3,2,1,0:T(8,128)S(1)}, u32[]{:S(2)}, u32[]{:S(2)}) %collective-permute-start.17) | collective-permute-done | bytes 131104 | tf_op jit(solution)/shard_map/ppermute | solution.py:303
  66.4 1.7 %collective-permute-start.18 = (f32[2,4,32,128]{3,2,1,0:T(8,128)S(1)}, f32[2,4,32,128]{3,2,1,0:T(8,128)S(1)}, u32[]{:S(2)}, u32[]{:S(2)}) collective-permute-start(f32[2,4,32,128]{3,2,1,0:T(8,128)S(1)} %pad_maximum_fusion.4), channel_id=1, source_target_pairs={{0,16},{1,9},{2,18},{3,11},{4,20},{5,13},{6,22},{7,15},{8,24},{9,1... | collective-permute-start | bytes 393224 | tf_op jit(solution)/shard_map/ppermute | solution.py:303
  68.1 1.6 %collective-permute-start.16 = (f32[2,4,32,128]{3,2,1,0:T(8,128)S(1)}, f32[2,4,32,128]{3,2,1,0:T(8,128)S(1)}, u32[]{:S(2)}, u32[]{:S(2)}) collective-permute-start(f32[2,4,32,128]{3,2,1,0:T(8,128)S(1)} %pad_maximum_fusion.2), channel_id=1, source_target_pairs={{0,4},{1,3},{2,6},{3,1},{4,0},{5,7},{6,2},{7,5},{8,12},{9,11},{10,... | collective-permute-start | bytes 393224 | tf_op jit(solution)/shard_map/ppermute | solution.py:303
  69.7 3.5 %collective-permute-done.16 = f32[2,4,32,128]{3,2,1,0:T(8,128)S(1)} collective-permute-done((f32[2,4,32,128]{3,2,1,0:T(8,128)S(1)}, f32[2,4,32,128]{3,2,1,0:T(8,128)S(1)}, u32[]{:S(2)}, u32[]{:S(2)}) %collective-permute-start.16) | collective-permute-done | bytes 131104 | tf_op jit(solution)/shard_map/ppermute | solution.py:303
  75.7 1.6 %place.1 = f32[128,1024]{1,0:T(8,128)} custom-call(s32[16]{0:T(128)S(1)} %copy-done, f32[8,32,128]{2,1,0:T(8,128)S(1)} %pad_maximum_fusion.refs_0_, f32[24,32,128]{2,1,0:T(8,128)S(1)} %fusion.14.refs_1_, f32[8,32,128]{2,1,0:T(8,128)S(1)} %collective-permute-done.19.refs_2_, f32[24,32,128]{2,1,0:T(8,128)S(1)} %collective-permute-done.20.refs_3_), custom_call_target="tpu_custom_call" | custom-call | tf_op jit(solution)/shard_map/place/pallas_call | solution.py:350
  (85 shorter events, 9.4 us)
Async XLA Ops:
  10.8 3.0 %collective-permute-start = (f32[2304,128]{1,0:T(8,128)S(1)}, f32[2304,128]{1,0:T(8,128)S(1)}, u32[]{:S(2)}, u32[]{:S(2)}) collective-permute-start(f32[2304,128]{1,0:T(8,128)S(1)} %slice_bitcast_fusion), channel_id=1, source_target_pairs={{0,1},{1,0},{2,3},{3,2},{4,5},{5,4},{6,7},{7,6},{8,9},{9,8},{10,11... | collective-permute-start | bytes 3538952 | tf_op jit(solution)/shard_map/ppermute | solution.py:249
  13.8 3.9 %collective-permute-start.2 = (f32[2048,128]{1,0:T(8,128)S(1)}, f32[2048,128]{1,0:T(8,128)S(1)}, u32[]{:S(2)}, u32[]{:S(2)}) collective-permute-start(f32[2048,128]{1,0:T(8,128)S(1)} %bitcast_add_fusion.1), channel_id=1, source_target_pairs={{0,1},{1,0},{2,3},{3,2},{4,5},{5,4},{6,7},{7,6},{8,9},{9,8},{10,11... | collective-permute-start | bytes 3145736 | tf_op jit(solution)/shard_map/ppermute | solution.py:249
  14.4 7.0 %collective-permute-start.1 = (f32[4352,128]{1,0:T(8,128)S(1)}, f32[4352,128]{1,0:T(8,128)S(1)}, u32[]{:S(2)}, u32[]{:S(2)}) collective-permute-start(f32[4352,128]{1,0:T(8,128)S(1)} %bitcast_add_fusion), channel_id=1, source_target_pairs={{0,1},{1,0},{2,3},{3,2},{4,5},{5,4},{6,7},{7,6},{8,9},{9,8},{10,11... | collective-permute-start | bytes 6684680 | tf_op jit(solution)/shard_map/ppermute | solution.py:249
  14.8 17.1 %collective-permute-start.5 = (f32[8,9,32,128]{3,2,1,0:T(8,128)S(1)}, f32[8,9,32,128]{3,2,1,0:T(8,128)S(1)}, u32[]{:S(2)}, u32[]{:S(2)}) collective-permute-start(f32[8,9,32,128]{3,2,1,0:T(8,128)S(1)} %bitcast.116), channel_id=1, source_target_pairs={{0,2},{1,5},{2,0},{3,7},{4,6},{5,1},{6,4},{7,3},{8,10},{9,13},{10,... | collective-permute-start | bytes 3538952 | tf_op jit(solution)/shard_map/ppermute | solution.py:303
  17.9 17.5 %collective-permute-start.4 = (f32[8,5,32,128]{3,2,1,0:T(8,128)S(1)}, f32[8,5,32,128]{3,2,1,0:T(8,128)S(1)}, u32[]{:S(2)}, u32[]{:S(2)}) collective-permute-start(f32[8,5,32,128]{3,2,1,0:T(8,128)S(1)} %broadcast_add_fusion), channel_id=1, source_target_pairs={{0,8},{1,17},{2,10},{3,19},{4,12},{5,21},{6,14},{7,23},{8,0},{9,25... | collective-permute-start | bytes 1966088 | tf_op jit(solution)/shard_map/ppermute | solution.py:303
  19.8 18.0 %collective-permute-start.3 = (f32[8,3,32,128]{3,2,1,0:T(8,128)S(1)}, f32[8,3,32,128]{3,2,1,0:T(8,128)S(1)}, u32[]{:S(2)}, u32[]{:S(2)}) collective-permute-start(f32[8,3,32,128]{3,2,1,0:T(8,128)S(1)} %broadcast_add_fusion.1), channel_id=1, source_target_pairs={{0,2},{1,5},{2,0},{3,7},{4,6},{5,1},{6,4},{7,3},{8,10},{9,13},{10,... | collective-permute-start | bytes 1179656 | tf_op jit(solution)/shard_map/ppermute | solution.py:303
  32.0 10.0 %collective-permute-start.8 = (f32[4,9,32,128]{3,2,1,0:T(8,128)S(1)}, f32[4,9,32,128]{3,2,1,0:T(8,128)S(1)}, u32[]{:S(2)}, u32[]{:S(2)}) collective-permute-start(f32[4,9,32,128]{3,2,1,0:T(8,128)S(1)} %fusion), channel_id=1, source_target_pairs={{0,4},{1,3},{2,6},{3,1},{4,0},{5,7},{6,2},{7,5},{8,12},{9,11},{10,... | collective-permute-start | bytes 1769480 | tf_op jit(solution)/shard_map/ppermute | solution.py:303
  35.4 10.4 %collective-permute-start.7 = (f32[4,5,32,128]{3,2,1,0:T(8,128)S(1)}, f32[4,5,32,128]{3,2,1,0:T(8,128)S(1)}, u32[]{:S(2)}, u32[]{:S(2)}) collective-permute-start(f32[4,5,32,128]{3,2,1,0:T(8,128)S(1)} %fusion.1), channel_id=1, source_target_pairs={{0,16},{1,9},{2,18},{3,11},{4,20},{5,13},{6,22},{7,15},{8,24},{9,1... | collective-permute-start | bytes 983048 | tf_op jit(solution)/shard_map/ppermute | solution.py:303
  37.9 10.1 %collective-permute-start.6 = (f32[4,3,32,128]{3,2,1,0:T(8,128)S(1)}, f32[4,3,32,128]{3,2,1,0:T(8,128)S(1)}, u32[]{:S(2)}, u32[]{:S(2)}) collective-permute-start(f32[4,3,32,128]{3,2,1,0:T(8,128)S(1)} %fusion.3), channel_id=1, source_target_pairs={{0,4},{1,3},{2,6},{3,1},{4,0},{5,7},{6,2},{7,5},{8,12},{9,11},{10,... | collective-permute-start | bytes 589832 | tf_op jit(solution)/shard_map/ppermute | solution.py:303
  42.0 9.0 %collective-permute-start.11 = (f32[2,9,32,128]{3,2,1,0:T(8,128)S(1)}, f32[2,9,32,128]{3,2,1,0:T(8,128)S(1)}, u32[]{:S(2)}, u32[]{:S(2)}) collective-permute-start(f32[2,9,32,128]{3,2,1,0:T(8,128)S(1)} %fusion.2), channel_id=1, source_target_pairs={{0,8},{1,17},{2,10},{3,19},{4,12},{5,21},{6,14},{7,23},{8,0},{9,25... | collective-permute-start | bytes 884744 | tf_op jit(solution)/shard_map/ppermute | solution.py:303
  45.8 9.3 %collective-permute-start.10 = (f32[2,5,32,128]{3,2,1,0:T(8,128)S(1)}, f32[2,5,32,128]{3,2,1,0:T(8,128)S(1)}, u32[]{:S(2)}, u32[]{:S(2)}) collective-permute-start(f32[2,5,32,128]{3,2,1,0:T(8,128)S(1)} %fusion.4), channel_id=1, source_target_pairs={{0,2},{1,5},{2,0},{3,7},{4,6},{5,1},{6,4},{7,3},{8,10},{9,13},{10,... | collective-permute-start | bytes 491528 | tf_op jit(solution)/shard_map/ppermute | solution.py:303
  48.1 8.7 %collective-permute-start.9 = (f32[2,3,32,128]{3,2,1,0:T(8,128)S(1)}, f32[2,3,32,128]{3,2,1,0:T(8,128)S(1)}, u32[]{:S(2)}, u32[]{:S(2)}) collective-permute-start(f32[2,3,32,128]{3,2,1,0:T(8,128)S(1)} %fusion.9), channel_id=1, source_target_pairs={{0,8},{1,17},{2,10},{3,19},{4,12},{5,21},{6,14},{7,23},{8,0},{9,25... | collective-permute-start | bytes 294920 | tf_op jit(solution)/shard_map/ppermute | solution.py:303
  51.1 7.4 %collective-permute-start.14 = (f32[1,9,32,128]{3,2,1,0:T(8,128)S(1)}, f32[1,9,32,128]{3,2,1,0:T(8,128)S(1)}, u32[]{:S(2)}, u32[]{:S(2)}) collective-permute-start(f32[1,9,32,128]{3,2,1,0:T(8,128)S(1)} %fusion.6), channel_id=1, source_target_pairs={{0,16},{1,9},{2,18},{3,11},{4,20},{5,13},{6,22},{7,15},{8,24},{9,1... | collective-permute-start | bytes 442376 | tf_op jit(solution)/shard_map/ppermute | solution.py:303
  55.2 4.5 %collective-permute-start.13 = (f32[1,5,32,128]{3,2,1,0:T(8,128)S(1)}, f32[1,5,32,128]{3,2,1,0:T(8,128)S(1)}, u32[]{:S(2)}, u32[]{:S(2)}) collective-permute-start(f32[1,5,32,128]{3,2,1,0:T(8,128)S(1)} %fusion.13), channel_id=1, source_target_pairs={{0,4},{1,3},{2,6},{3,1},{4,0},{5,7},{6,2},{7,5},{8,12},{9,11},{10,... | collective-permute-start | bytes 245768 | tf_op jit(solution)/shard_map/ppermute | solution.py:303
  56.8 5.2 %collective-permute-start.12 = (f32[1,3,32,128]{3,2,1,0:T(8,128)S(1)}, f32[1,3,32,128]{3,2,1,0:T(8,128)S(1)}, u32[]{:S(2)}, u32[]{:S(2)}) collective-permute-start(f32[1,3,32,128]{3,2,1,0:T(8,128)S(1)} %fusion.23), channel_id=1, source_target_pairs={{0,16},{1,9},{2,18},{3,11},{4,20},{5,13},{6,22},{7,15},{8,24},{9,1... | collective-permute-start | bytes 147464 | tf_op jit(solution)/shard_map/ppermute | solution.py:303
  59.7 16.0 %copy-start = (s32[16]{0:T(128)S(1)}, s32[16]{0:T(128)}, u32[]{:S(2)}) copy-start(s32[16]{0:T(128)} %owner_ref.1) | copy-start | bytes 196
  59.8 6.5 %collective-permute-start.17 = (f32[2,4,32,128]{3,2,1,0:T(8,128)S(1)}, f32[2,4,32,128]{3,2,1,0:T(8,128)S(1)}, u32[]{:S(2)}, u32[]{:S(2)}) collective-permute-start(f32[2,4,32,128]{3,2,1,0:T(8,128)S(1)} %pad_maximum_fusion.3), channel_id=1, source_target_pairs={{0,8},{1,17},{2,10},{3,19},{4,12},{5,21},{6,14},{7,23},{8,0},{9,25... | collective-permute-start | bytes 393224 | tf_op jit(solution)/shard_map/ppermute | solution.py:303
  62.1 6.0 %collective-permute-start.15 = (f32[2,4,32,128]{3,2,1,0:T(8,128)S(1)}, f32[2,4,32,128]{3,2,1,0:T(8,128)S(1)}, u32[]{:S(2)}, u32[]{:S(2)}) collective-permute-start(f32[2,4,32,128]{3,2,1,0:T(8,128)S(1)} %pad_maximum_fusion.1), channel_id=1, source_target_pairs={{0,2},{1,5},{2,0},{3,7},{4,6},{5,1},{6,4},{7,3},{8,10},{9,13},{10,... | collective-permute-start | bytes 393224 | tf_op jit(solution)/shard_map/ppermute | solution.py:303
  66.4 7.3 %collective-permute-start.18 = (f32[2,4,32,128]{3,2,1,0:T(8,128)S(1)}, f32[2,4,32,128]{3,2,1,0:T(8,128)S(1)}, u32[]{:S(2)}, u32[]{:S(2)}) collective-permute-start(f32[2,4,32,128]{3,2,1,0:T(8,128)S(1)} %pad_maximum_fusion.4), channel_id=1, source_target_pairs={{0,16},{1,9},{2,18},{3,11},{4,20},{5,13},{6,22},{7,15},{8,24},{9,1... | collective-permute-start | bytes 393224 | tf_op jit(solution)/shard_map/ppermute | solution.py:303
  68.1 5.0 %collective-permute-start.16 = (f32[2,4,32,128]{3,2,1,0:T(8,128)S(1)}, f32[2,4,32,128]{3,2,1,0:T(8,128)S(1)}, u32[]{:S(2)}, u32[]{:S(2)}) collective-permute-start(f32[2,4,32,128]{3,2,1,0:T(8,128)S(1)} %pad_maximum_fusion.2), channel_id=1, source_target_pairs={{0,4},{1,3},{2,6},{3,1},{4,0},{5,7},{6,2},{7,5},{8,12},{9,11},{10,... | collective-permute-start | bytes 393224 | tf_op jit(solution)/shard_map/ppermute | solution.py:303
  73.7 2.0 %collective-permute-start.20 = (f32[24,32,128]{2,1,0:T(8,128)S(1)}, f32[24,32,128]{2,1,0:T(8,128)S(1)}, u32[]{:S(2)}, u32[]{:S(2)}) collective-permute-start(f32[24,32,128]{2,1,0:T(8,128)S(1)} %fusion.14.refs_1_), channel_id=1, source_target_pairs={{0,1},{1,0},{2,3},{3,2},{4,5},{5,4},{6,7},{7,6},{8,9},{9,8},{10,11... | collective-permute-start | bytes 1179656 | tf_op jit(solution)/shard_map/ppermute | solution.py:249
  73.8 1.9 %collective-permute-start.19 = (f32[8,32,128]{2,1,0:T(8,128)S(1)}, f32[8,32,128]{2,1,0:T(8,128)S(1)}, u32[]{:S(2)}, u32[]{:S(2)}) collective-permute-start(f32[8,32,128]{2,1,0:T(8,128)S(1)} %pad_maximum_fusion.refs_0_), channel_id=1, source_target_pairs={{0,1},{1,0},{2,3},{3,2},{4,5},{5,4},{6,7},{7,6},{8,9},{9,8},{10,11... | collective-permute-start | bytes 393224 | tf_op jit(solution)/shard_map/ppermute | solution.py:249

commit v5 on v4

--- a/solution.py
+++ b/solution.py
@@ -65,7 +65,7 @@
 
 def pair_kernel(
     sz, slots_hbm, owner_hbm, table_hbm, x_ref, fit_hbm, keep, send,
-    xbuf, both, gbuf, fbuf, res, fit_ref, slots_ref, owner_ref, table_ref, ranked, insem, smallsem,
+    xbuf, both, gbuf, fbuf, res, fit_ref, slots_ref, owner_ref, table_ref, ranked, slot_of, insem, smallsem,
 ):
     _, count_a, count_s, tile, width = x_ref.shape
     orbitals = width // tile
@@ -78,8 +78,24 @@
             (table_hbm, table_ref),
         ])
     ]
-    for c in small:
+    for c in small[:2]:
         c.start()
+
+    def tile_copy(a, p):
+        at = (a * count_s + p) * tile
+        if not isinstance(a, int):
+            at = pl.multiple_of(at, tile)
+        return pltpu.make_async_copy(
+            x_ref.at[0, a, p], xbuf.at[pl.ds(at, tile)], insem.at[a * count_s + p]
+        )
+
+    for p in range(count_s):
+        tile_copy(0, p).start()
+    small[2].start()
+    small[3].start()
+    keep[...] = jnp.zeros_like(keep)
+    send[...] = jnp.zeros_like(send)
+    both[...] = jnp.zeros_like(both)
     small[0].wait()
     small[1].wait()
     for a in range(count_a):
@@ -89,15 +105,8 @@
             for t in range(count_s):
                 if t != s:
                     rank = rank + (own[t] < own[s]).astype(jnp.int32)
-            place = a * count_s + rank
-            ranked[place] = own[s]
-            pltpu.make_async_copy(
-                x_ref.at[0, a, s], xbuf.at[pl.ds(pl.multiple_of(place * tile, tile), tile)],
-                insem.at[place],
-            ).start()
-    keep[...] = jnp.zeros_like(keep)
-    send[...] = jnp.zeros_like(send)
-    both[...] = jnp.zeros_like(both)
+            ranked[a * count_s + rank] = own[s]
+            slot_of[a * count_s + rank] = s
     wide = 2 * tile
     span = wide // orbitals
     to = lax.broadcasted_iota(jnp.int32, (wide, wide), 0)
@@ -113,16 +122,16 @@
         both[:tile, :tile] = fit_ref[a]
         both[tile:, tile:] = fit_ref[a]
         for p in range(count_s):
-            pltpu.make_async_copy(
-                x_ref.at[0, a, p],
-                xbuf.at[pl.ds(pl.multiple_of((base + p) * tile, tile), tile)],
-                insem.at[base + p],
-            ).wait()
+            tile_copy(a, p).wait()
         for g in range(0, count_s, 2):
-            at = pl.multiple_of((base + g) * tile, tile)
+            rows = [
+                pl.ds(pl.multiple_of((base + slot_of[base + g + t]) * tile, tile), tile)
+                for t in range(2)
+            ]
             for b in range(width // wide):
+                two = [xbuf[r, b * wide:(b + 1) * wide] for r in rows]
                 gbuf[g // 2, b * wide:(b + 1) * wide, :] = lax.dot_general(
-                    perm, xbuf[pl.ds(at, wide), b * wide:(b + 1) * wide], nt,
+                    perm, jnp.concatenate(two), nt,
                     preferred_element_type=jnp.float32,
                 ).astype(jnp.bfloat16)
                 yield
@@ -182,8 +191,11 @@
             add(a - 1, *left.pop())
         return carry
 
-    for _ in tiles_of(jnp.int32(0)):
-        pass
+    for i, _ in enumerate(tiles_of(jnp.int32(0))):
+        if i in (0, 8):
+            for a in range(1, 2) if i == 0 else range(2, count_a):
+                for p in range(count_s):
+                    tile_copy(a, p).start()
     lax.fori_loop(1, count_a, both_of, 0)
     for p, q in pairs:
         add(jnp.int32(count_a - 1), p, q)
@@ -271,6 +283,7 @@
             pltpu.SMEM(owner.shape, jnp.int32),
             pltpu.SMEM((chips * (chips + 1) * 2,), jnp.int32),
             pltpu.SMEM((count_a * count_s,), jnp.int32),
+            pltpu.SMEM((count_a * count_s,), jnp.int32),
             pltpu.SemaphoreType.DMA((count_a * count_s,)),
             pltpu.SemaphoreType.DMA((4,)),
         ],

time: 77.5 us -> 76.8 us (level)
  no operation moved by 1% of the time
where the time goes in v5:
time: 76.8 us; the launch traced here: 76.7 us
  starting transfers between devices  33.6 us (44%)
  waiting for transfers between devices  29.4 us (38%)
  Pallas kernels  11.6 us (15%)
  other arithmetic  1.58 us (2%)
    ppermute x16, starting transfers between devices, step(): return lax.ppermute(x, ('aux', 'occ'), pairs)  31.8 us
    ppermute x16, waiting for transfers between devices, step(): return lax.ppermute(x, ('aux', 'occ'), pairs)  25.6 us
    pallas_call x1, Pallas kernels, local(): pl.pallas_call(functools.partial(pair_kernel, sz), out_shape=[space((sz.t...  9.99 us
    ppermute x5, waiting for transfers between devices, go(): return lax.ppermute(x, 'occ', [(j, j ^ core) for j in range(cores)])  3.8 us
    ppermute x5, starting transfers between devices, go(): return lax.ppermute(x, 'occ', [(j, j ^ core) for j in range(cores)])  1.79 us
    pallas_call x1, Pallas kernels, local(): pl.pallas_call(functools.partial(place_kernel, sz), out_shape=jax.ShapeDt...  1.6 us
  transfers between devices with their start and end apart: 21, of which 13 were waited for; matrix products, arithmetic and copies ran while one was open for 2% of the time, Pallas kernels for 0%

profile of v5, /device:TPU:0, one launch (start us, length us, event | category | flops | bytes accessed | tf_op | source)
XLA Modules:
  0.0 76.7 jit_solution(10817805704735048895)
XLA Ops:
  0.0 10.0 %pairs.1 = (f32[8704,128]{1,0:T(8,128)S(1)}, f32[1,8704,128]{2,1,0:T(8,128)S(1)}) custom-call(s32[1,4,6]{2,1,0:T(4,128)} %slots_hbm.1, s32[16]{0:T(128)} %owner_ref.1, s32[544]{0:T(1024)} %constant.3.clone.table_hbm, bf16[1,4,6,128,1024]{4,3,2,1,0:T(8,128)(2,1)} %x_ref.1, bf16[4,128,128]{2,1,0:T(8,128)(2,1)} %fit_hbm.1), custom_call_target="tpu_custom_call" | custom-call | tf_op jit(solution)/shard_map/pairs/pallas_call | solution.py:268
  10.6 2.5 %collective-permute-done = f32[2304,128]{1,0:T(8,128)S(1)} collective-permute-done((f32[2304,128]{1,0:T(8,128)S(1)}, f32[2304,128]{1,0:T(8,128)S(1)}, u32[]{:S(2)}, u32[]{:S(2)}) %collective-permute-start) | collective-permute-done | bytes 1179680 | tf_op jit(solution)/shard_map/ppermute | solution.py:261
  14.1 2.9 %collective-permute-start.5 = (f32[8,9,32,128]{3,2,1,0:T(8,128)S(1)}, f32[8,9,32,128]{3,2,1,0:T(8,128)S(1)}, u32[]{:S(2)}, u32[]{:S(2)}) collective-permute-start(f32[8,9,32,128]{3,2,1,0:T(8,128)S(1)} %bitcast.116), channel_id=1, source_target_pairs={{0,2},{1,5},{2,0},{3,7},{4,6},{5,1},{6,4},{7,3},{8,10},{9,13},{10,... | collective-permute-start | bytes 3538952 | tf_op jit(solution)/shard_map/ppermute | solution.py:316
  17.2 1.9 %collective-permute-start.4 = (f32[8,5,32,128]{3,2,1,0:T(8,128)S(1)}, f32[8,5,32,128]{3,2,1,0:T(8,128)S(1)}, u32[]{:S(2)}, u32[]{:S(2)}) collective-permute-start(f32[8,5,32,128]{3,2,1,0:T(8,128)S(1)} %broadcast_add_fusion), channel_id=1, source_target_pairs={{0,8},{1,17},{2,10},{3,19},{4,12},{5,21},{6,14},{7,23},{8,0},{9,25... | collective-permute-start | bytes 1966088 | tf_op jit(solution)/shard_map/ppermute | solution.py:316
  19.2 1.6 %collective-permute-start.3 = (f32[8,3,32,128]{3,2,1,0:T(8,128)S(1)}, f32[8,3,32,128]{3,2,1,0:T(8,128)S(1)}, u32[]{:S(2)}, u32[]{:S(2)}) collective-permute-start(f32[8,3,32,128]{3,2,1,0:T(8,128)S(1)} %broadcast_add_fusion.1), channel_id=1, source_target_pairs={{0,2},{1,5},{2,0},{3,7},{4,6},{5,1},{6,4},{7,3},{8,10},{9,13},{10,... | collective-permute-start | bytes 1179656 | tf_op jit(solution)/shard_map/ppermute | solution.py:316
  20.8 10.4 %collective-permute-done.5 = f32[8,9,32,128]{3,2,1,0:T(8,128)S(1)} collective-permute-done((f32[8,9,32,128]{3,2,1,0:T(8,128)S(1)}, f32[8,9,32,128]{3,2,1,0:T(8,128)S(1)}, u32[]{:S(2)}, u32[]{:S(2)}) %collective-permute-start.5) | collective-permute-done | bytes 1179680 | tf_op jit(solution)/shard_map/ppermute | solution.py:316
  31.3 2.1 %collective-permute-start.8 = (f32[4,9,32,128]{3,2,1,0:T(8,128)S(1)}, f32[4,9,32,128]{3,2,1,0:T(8,128)S(1)}, u32[]{:S(2)}, u32[]{:S(2)}) collective-permute-start(f32[4,9,32,128]{3,2,1,0:T(8,128)S(1)} %fusion), channel_id=1, source_target_pairs={{0,4},{1,3},{2,6},{3,1},{4,0},{5,7},{6,2},{7,5},{8,12},{9,11},{10,... | collective-permute-start | bytes 1769480 | tf_op jit(solution)/shard_map/ppermute | solution.py:316
  34.7 2.1 %collective-permute-start.7 = (f32[4,5,32,128]{3,2,1,0:T(8,128)S(1)}, f32[4,5,32,128]{3,2,1,0:T(8,128)S(1)}, u32[]{:S(2)}, u32[]{:S(2)}) collective-permute-start(f32[4,5,32,128]{3,2,1,0:T(8,128)S(1)} %fusion.1), channel_id=1, source_target_pairs={{0,16},{1,9},{2,18},{3,11},{4,20},{5,13},{6,22},{7,15},{8,24},{9,1... | collective-permute-start | bytes 983048 | tf_op jit(solution)/shard_map/ppermute | solution.py:316
  37.2 2.4 %collective-permute-start.6 = (f32[4,3,32,128]{3,2,1,0:T(8,128)S(1)}, f32[4,3,32,128]{3,2,1,0:T(8,128)S(1)}, u32[]{:S(2)}, u32[]{:S(2)}) collective-permute-start(f32[4,3,32,128]{3,2,1,0:T(8,128)S(1)} %fusion.3), channel_id=1, source_target_pairs={{0,4},{1,3},{2,6},{3,1},{4,0},{5,7},{6,2},{7,5},{8,12},{9,11},{10,... | collective-permute-start | bytes 589832 | tf_op jit(solution)/shard_map/ppermute | solution.py:316
  39.8 1.5 %collective-permute-done.8 = f32[4,9,32,128]{3,2,1,0:T(8,128)S(1)} collective-permute-done((f32[4,9,32,128]{3,2,1,0:T(8,128)S(1)}, f32[4,9,32,128]{3,2,1,0:T(8,128)S(1)}, u32[]{:S(2)}, u32[]{:S(2)}) %collective-permute-start.8) | collective-permute-done | bytes 589856 | tf_op jit(solution)/shard_map/ppermute | solution.py:316
  41.4 2.1 %collective-permute-start.11 = (f32[2,9,32,128]{3,2,1,0:T(8,128)S(1)}, f32[2,9,32,128]{3,2,1,0:T(8,128)S(1)}, u32[]{:S(2)}, u32[]{:S(2)}) collective-permute-start(f32[2,9,32,128]{3,2,1,0:T(8,128)S(1)} %fusion.2), channel_id=1, source_target_pairs={{0,8},{1,17},{2,10},{3,19},{4,12},{5,21},{6,14},{7,23},{8,0},{9,25... | collective-permute-start | bytes 884744 | tf_op jit(solution)/shard_map/ppermute | solution.py:316
  43.5 1.6 %collective-permute-done.7 = f32[4,5,32,128]{3,2,1,0:T(8,128)S(1)} collective-permute-done((f32[4,5,32,128]{3,2,1,0:T(8,128)S(1)}, f32[4,5,32,128]{3,2,1,0:T(8,128)S(1)}, u32[]{:S(2)}, u32[]{:S(2)}) %collective-permute-start.7) | collective-permute-done | bytes 327712 | tf_op jit(solution)/shard_map/ppermute | solution.py:316
  45.2 2.2 %collective-permute-start.10 = (f32[2,5,32,128]{3,2,1,0:T(8,128)S(1)}, f32[2,5,32,128]{3,2,1,0:T(8,128)S(1)}, u32[]{:S(2)}, u32[]{:S(2)}) collective-permute-start(f32[2,5,32,128]{3,2,1,0:T(8,128)S(1)} %fusion.4), channel_id=1, source_target_pairs={{0,2},{1,5},{2,0},{3,7},{4,6},{5,1},{6,4},{7,3},{8,10},{9,13},{10,... | collective-permute-start | bytes 491528 | tf_op jit(solution)/shard_map/ppermute | solution.py:316
  47.4 1.5 %collective-permute-start.9 = (f32[2,3,32,128]{3,2,1,0:T(8,128)S(1)}, f32[2,3,32,128]{3,2,1,0:T(8,128)S(1)}, u32[]{:S(2)}, u32[]{:S(2)}) collective-permute-start(f32[2,3,32,128]{3,2,1,0:T(8,128)S(1)} %fusion.9), channel_id=1, source_target_pairs={{0,8},{1,17},{2,10},{3,19},{4,12},{5,21},{6,14},{7,23},{8,0},{9,25... | collective-permute-start | bytes 294920 | tf_op jit(solution)/shard_map/ppermute | solution.py:316
  50.4 4.1 %collective-permute-start.14 = (f32[1,9,32,128]{3,2,1,0:T(8,128)S(1)}, f32[1,9,32,128]{3,2,1,0:T(8,128)S(1)}, u32[]{:S(2)}, u32[]{:S(2)}) collective-permute-start(f32[1,9,32,128]{3,2,1,0:T(8,128)S(1)} %fusion.6), channel_id=1, source_target_pairs={{0,16},{1,9},{2,18},{3,11},{4,20},{5,13},{6,22},{7,15},{8,24},{9,1... | collective-permute-start | bytes 442376 | tf_op jit(solution)/shard_map/ppermute | solution.py:316
  54.5 1.6 %collective-permute-start.13 = (f32[1,5,32,128]{3,2,1,0:T(8,128)S(1)}, f32[1,5,32,128]{3,2,1,0:T(8,128)S(1)}, u32[]{:S(2)}, u32[]{:S(2)}) collective-permute-start(f32[1,5,32,128]{3,2,1,0:T(8,128)S(1)} %fusion.13), channel_id=1, source_target_pairs={{0,4},{1,3},{2,6},{3,1},{4,0},{5,7},{6,2},{7,5},{8,12},{9,11},{10,... | collective-permute-start | bytes 245768 | tf_op jit(solution)/shard_map/ppermute | solution.py:316
  56.2 1.6 %collective-permute-done.14 = f32[1,9,32,128]{3,2,1,0:T(8,128)S(1)} collective-permute-done((f32[1,9,32,128]{3,2,1,0:T(8,128)S(1)}, f32[1,9,32,128]{3,2,1,0:T(8,128)S(1)}, u32[]{:S(2)}, u32[]{:S(2)}) %collective-permute-start.14) | collective-permute-done | bytes 147488 | tf_op jit(solution)/shard_map/ppermute | solution.py:316
  59.1 2.3 %collective-permute-start.17 = (f32[2,4,32,128]{3,2,1,0:T(8,128)S(1)}, f32[2,4,32,128]{3,2,1,0:T(8,128)S(1)}, u32[]{:S(2)}, u32[]{:S(2)}) collective-permute-start(f32[2,4,32,128]{3,2,1,0:T(8,128)S(1)} %pad_maximum_fusion.3), channel_id=1, source_target_pairs={{0,8},{1,17},{2,10},{3,19},{4,12},{5,21},{6,14},{7,23},{8,0},{9,25... | collective-permute-start | bytes 393224 | tf_op jit(solution)/shard_map/ppermute | solution.py:316
  61.5 1.6 %collective-permute-start.15 = (f32[2,4,32,128]{3,2,1,0:T(8,128)S(1)}, f32[2,4,32,128]{3,2,1,0:T(8,128)S(1)}, u32[]{:S(2)}, u32[]{:S(2)}) collective-permute-start(f32[2,4,32,128]{3,2,1,0:T(8,128)S(1)} %pad_maximum_fusion.1), channel_id=1, source_target_pairs={{0,2},{1,5},{2,0},{3,7},{4,6},{5,1},{6,4},{7,3},{8,10},{9,13},{10,... | collective-permute-start | bytes 393224 | tf_op jit(solution)/shard_map/ppermute | solution.py:316
  63.1 2.6 %collective-permute-done.17 = f32[2,4,32,128]{3,2,1,0:T(8,128)S(1)} collective-permute-done((f32[2,4,32,128]{3,2,1,0:T(8,128)S(1)}, f32[2,4,32,128]{3,2,1,0:T(8,128)S(1)}, u32[]{:S(2)}, u32[]{:S(2)}) %collective-permute-start.17) | collective-permute-done | bytes 131104 | tf_op jit(solution)/shard_map/ppermute | solution.py:316
  65.7 1.7 %collective-permute-start.18 = (f32[2,4,32,128]{3,2,1,0:T(8,128)S(1)}, f32[2,4,32,128]{3,2,1,0:T(8,128)S(1)}, u32[]{:S(2)}, u32[]{:S(2)}) collective-permute-start(f32[2,4,32,128]{3,2,1,0:T(8,128)S(1)} %pad_maximum_fusion.4), channel_id=1, source_target_pairs={{0,16},{1,9},{2,18},{3,11},{4,20},{5,13},{6,22},{7,15},{8,24},{9,1... | collective-permute-start | bytes 393224 | tf_op jit(solution)/shard_map/ppermute | solution.py:316
  67.4 1.6 %collective-permute-start.16 = (f32[2,4,32,128]{3,2,1,0:T(8,128)S(1)}, f32[2,4,32,128]{3,2,1,0:T(8,128)S(1)}, u32[]{:S(2)}, u32[]{:S(2)}) collective-permute-start(f32[2,4,32,128]{3,2,1,0:T(8,128)S(1)} %pad_maximum_fusion.2), channel_id=1, source_target_pairs={{0,4},{1,3},{2,6},{3,1},{4,0},{5,7},{6,2},{7,5},{8,12},{9,11},{10,... | collective-permute-start | bytes 393224 | tf_op jit(solution)/shard_map/ppermute | solution.py:316
  69.0 3.4 %collective-permute-done.16 = f32[2,4,32,128]{3,2,1,0:T(8,128)S(1)} collective-permute-done((f32[2,4,32,128]{3,2,1,0:T(8,128)S(1)}, f32[2,4,32,128]{3,2,1,0:T(8,128)S(1)}, u32[]{:S(2)}, u32[]{:S(2)}) %collective-permute-start.16) | collective-permute-done | bytes 131104 | tf_op jit(solution)/shard_map/ppermute | solution.py:316
  75.1 1.6 %place.1 = f32[128,1024]{1,0:T(8,128)} custom-call(s32[16]{0:T(128)S(1)} %copy-done, f32[8,32,128]{2,1,0:T(8,128)S(1)} %pad_maximum_fusion.refs_0_, f32[24,32,128]{2,1,0:T(8,128)S(1)} %fusion.14.refs_1_, f32[8,32,128]{2,1,0:T(8,128)S(1)} %collective-permute-done.19.refs_2_, f32[24,32,128]{2,1,0:T(8,128)S(1)} %collective-permute-done.20.refs_3_), custom_call_target="tpu_custom_call" | custom-call | tf_op jit(solution)/shard_map/place/pallas_call | solution.py:363
  (85 shorter events, 9.5 us)
Async XLA Ops:
  10.1 3.0 %collective-permute-start = (f32[2304,128]{1,0:T(8,128)S(1)}, f32[2304,128]{1,0:T(8,128)S(1)}, u32[]{:S(2)}, u32[]{:S(2)}) collective-permute-start(f32[2304,128]{1,0:T(8,128)S(1)} %slice_bitcast_fusion), channel_id=1, source_target_pairs={{0,1},{1,0},{2,3},{3,2},{4,5},{5,4},{6,7},{7,6},{8,9},{9,8},{10,11... | collective-permute-start | bytes 3538952 | tf_op jit(solution)/shard_map/ppermute | solution.py:261
  13.2 3.9 %collective-permute-start.2 = (f32[2048,128]{1,0:T(8,128)S(1)}, f32[2048,128]{1,0:T(8,128)S(1)}, u32[]{:S(2)}, u32[]{:S(2)}) collective-permute-start(f32[2048,128]{1,0:T(8,128)S(1)} %bitcast_add_fusion.1), channel_id=1, source_target_pairs={{0,1},{1,0},{2,3},{3,2},{4,5},{5,4},{6,7},{7,6},{8,9},{9,8},{10,11... | collective-permute-start | bytes 3145736 | tf_op jit(solution)/shard_map/ppermute | solution.py:261
  13.8 7.0 %collective-permute-start.1 = (f32[4352,128]{1,0:T(8,128)S(1)}, f32[4352,128]{1,0:T(8,128)S(1)}, u32[]{:S(2)}, u32[]{:S(2)}) collective-permute-start(f32[4352,128]{1,0:T(8,128)S(1)} %bitcast_add_fusion), channel_id=1, source_target_pairs={{0,1},{1,0},{2,3},{3,2},{4,5},{5,4},{6,7},{7,6},{8,9},{9,8},{10,11... | collective-permute-start | bytes 6684680 | tf_op jit(solution)/shard_map/ppermute | solution.py:261
  14.1 17.1 %collective-permute-start.5 = (f32[8,9,32,128]{3,2,1,0:T(8,128)S(1)}, f32[8,9,32,128]{3,2,1,0:T(8,128)S(1)}, u32[]{:S(2)}, u32[]{:S(2)}) collective-permute-start(f32[8,9,32,128]{3,2,1,0:T(8,128)S(1)} %bitcast.116), channel_id=1, source_target_pairs={{0,2},{1,5},{2,0},{3,7},{4,6},{5,1},{6,4},{7,3},{8,10},{9,13},{10,... | collective-permute-start | bytes 3538952 | tf_op jit(solution)/shard_map/ppermute | solution.py:316
  17.2 17.5 %collective-permute-start.4 = (f32[8,5,32,128]{3,2,1,0:T(8,128)S(1)}, f32[8,5,32,128]{3,2,1,0:T(8,128)S(1)}, u32[]{:S(2)}, u32[]{:S(2)}) collective-permute-start(f32[8,5,32,128]{3,2,1,0:T(8,128)S(1)} %broadcast_add_fusion), channel_id=1, source_target_pairs={{0,8},{1,17},{2,10},{3,19},{4,12},{5,21},{6,14},{7,23},{8,0},{9,25... | collective-permute-start | bytes 1966088 | tf_op jit(solution)/shard_map/ppermute | solution.py:316
  19.2 18.0 %collective-permute-start.3 = (f32[8,3,32,128]{3,2,1,0:T(8,128)S(1)}, f32[8,3,32,128]{3,2,1,0:T(8,128)S(1)}, u32[]{:S(2)}, u32[]{:S(2)}) collective-permute-start(f32[8,3,32,128]{3,2,1,0:T(8,128)S(1)} %broadcast_add_fusion.1), channel_id=1, source_target_pairs={{0,2},{1,5},{2,0},{3,7},{4,6},{5,1},{6,4},{7,3},{8,10},{9,13},{10,... | collective-permute-start | bytes 1179656 | tf_op jit(solution)/shard_map/ppermute | solution.py:316
  31.3 10.0 %collective-permute-start.8 = (f32[4,9,32,128]{3,2,1,0:T(8,128)S(1)}, f32[4,9,32,128]{3,2,1,0:T(8,128)S(1)}, u32[]{:S(2)}, u32[]{:S(2)}) collective-permute-start(f32[4,9,32,128]{3,2,1,0:T(8,128)S(1)} %fusion), channel_id=1, source_target_pairs={{0,4},{1,3},{2,6},{3,1},{4,0},{5,7},{6,2},{7,5},{8,12},{9,11},{10,... | collective-permute-start | bytes 1769480 | tf_op jit(solution)/shard_map/ppermute | solution.py:316
  34.7 10.4 %collective-permute-start.7 = (f32[4,5,32,128]{3,2,1,0:T(8,128)S(1)}, f32[4,5,32,128]{3,2,1,0:T(8,128)S(1)}, u32[]{:S(2)}, u32[]{:S(2)}) collective-permute-start(f32[4,5,32,128]{3,2,1,0:T(8,128)S(1)} %fusion.1), channel_id=1, source_target_pairs={{0,16},{1,9},{2,18},{3,11},{4,20},{5,13},{6,22},{7,15},{8,24},{9,1... | collective-permute-start | bytes 983048 | tf_op jit(solution)/shard_map/ppermute | solution.py:316
  37.2 10.1 %collective-permute-start.6 = (f32[4,3,32,128]{3,2,1,0:T(8,128)S(1)}, f32[4,3,32,128]{3,2,1,0:T(8,128)S(1)}, u32[]{:S(2)}, u32[]{:S(2)}) collective-permute-start(f32[4,3,32,128]{3,2,1,0:T(8,128)S(1)} %fusion.3), channel_id=1, source_target_pairs={{0,4},{1,3},{2,6},{3,1},{4,0},{5,7},{6,2},{7,5},{8,12},{9,11},{10,... | collective-permute-start | bytes 589832 | tf_op jit(solution)/shard_map/ppermute | solution.py:316
  41.4 9.0 %collective-permute-start.11 = (f32[2,9,32,128]{3,2,1,0:T(8,128)S(1)}, f32[2,9,32,128]{3,2,1,0:T(8,128)S(1)}, u32[]{:S(2)}, u32[]{:S(2)}) collective-permute-start(f32[2,9,32,128]{3,2,1,0:T(8,128)S(1)} %fusion.2), channel_id=1, source_target_pairs={{0,8},{1,17},{2,10},{3,19},{4,12},{5,21},{6,14},{7,23},{8,0},{9,25... | collective-permute-start | bytes 884744 | tf_op jit(solution)/shard_map/ppermute | solution.py:316
  45.2 9.3 %collective-permute-start.10 = (f32[2,5,32,128]{3,2,1,0:T(8,128)S(1)}, f32[2,5,32,128]{3,2,1,0:T(8,128)S(1)}, u32[]{:S(2)}, u32[]{:S(2)}) collective-permute-start(f32[2,5,32,128]{3,2,1,0:T(8,128)S(1)} %fusion.4), channel_id=1, source_target_pairs={{0,2},{1,5},{2,0},{3,7},{4,6},{5,1},{6,4},{7,3},{8,10},{9,13},{10,... | collective-permute-start | bytes 491528 | tf_op jit(solution)/shard_map/ppermute | solution.py:316
  47.4 8.7 %collective-permute-start.9 = (f32[2,3,32,128]{3,2,1,0:T(8,128)S(1)}, f32[2,3,32,128]{3,2,1,0:T(8,128)S(1)}, u32[]{:S(2)}, u32[]{:S(2)}) collective-permute-start(f32[2,3,32,128]{3,2,1,0:T(8,128)S(1)} %fusion.9), channel_id=1, source_target_pairs={{0,8},{1,17},{2,10},{3,19},{4,12},{5,21},{6,14},{7,23},{8,0},{9,25... | collective-permute-start | bytes 294920 | tf_op jit(solution)/shard_map/ppermute | solution.py:316
  50.4 7.4 %collective-permute-start.14 = (f32[1,9,32,128]{3,2,1,0:T(8,128)S(1)}, f32[1,9,32,128]{3,2,1,0:T(8,128)S(1)}, u32[]{:S(2)}, u32[]{:S(2)}) collective-permute-start(f32[1,9,32,128]{3,2,1,0:T(8,128)S(1)} %fusion.6), channel_id=1, source_target_pairs={{0,16},{1,9},{2,18},{3,11},{4,20},{5,13},{6,22},{7,15},{8,24},{9,1... | collective-permute-start | bytes 442376 | tf_op jit(solution)/shard_map/ppermute | solution.py:316
  54.5 4.5 %collective-permute-start.13 = (f32[1,5,32,128]{3,2,1,0:T(8,128)S(1)}, f32[1,5,32,128]{3,2,1,0:T(8,128)S(1)}, u32[]{:S(2)}, u32[]{:S(2)}) collective-permute-start(f32[1,5,32,128]{3,2,1,0:T(8,128)S(1)} %fusion.13), channel_id=1, source_target_pairs={{0,4},{1,3},{2,6},{3,1},{4,0},{5,7},{6,2},{7,5},{8,12},{9,11},{10,... | collective-permute-start | bytes 245768 | tf_op jit(solution)/shard_map/ppermute | solution.py:316
  56.1 5.3 %collective-permute-start.12 = (f32[1,3,32,128]{3,2,1,0:T(8,128)S(1)}, f32[1,3,32,128]{3,2,1,0:T(8,128)S(1)}, u32[]{:S(2)}, u32[]{:S(2)}) collective-permute-start(f32[1,3,32,128]{3,2,1,0:T(8,128)S(1)} %fusion.23), channel_id=1, source_target_pairs={{0,16},{1,9},{2,18},{3,11},{4,20},{5,13},{6,22},{7,15},{8,24},{9,1... | collective-permute-start | bytes 147464 | tf_op jit(solution)/shard_map/ppermute | solution.py:316
  59.0 16.0 %copy-start = (s32[16]{0:T(128)S(1)}, s32[16]{0:T(128)}, u32[]{:S(2)}) copy-start(s32[16]{0:T(128)} %owner_ref.1) | copy-start | bytes 196
  59.1 6.6 %collective-permute-start.17 = (f32[2,4,32,128]{3,2,1,0:T(8,128)S(1)}, f32[2,4,32,128]{3,2,1,0:T(8,128)S(1)}, u32[]{:S(2)}, u32[]{:S(2)}) collective-permute-start(f32[2,4,32,128]{3,2,1,0:T(8,128)S(1)} %pad_maximum_fusion.3), channel_id=1, source_target_pairs={{0,8},{1,17},{2,10},{3,19},{4,12},{5,21},{6,14},{7,23},{8,0},{9,25... | collective-permute-start | bytes 393224 | tf_op jit(solution)/shard_map/ppermute | solution.py:316
  61.5 5.9 %collective-permute-start.15 = (f32[2,4,32,128]{3,2,1,0:T(8,128)S(1)}, f32[2,4,32,128]{3,2,1,0:T(8,128)S(1)}, u32[]{:S(2)}, u32[]{:S(2)}) collective-permute-start(f32[2,4,32,128]{3,2,1,0:T(8,128)S(1)} %pad_maximum_fusion.1), channel_id=1, source_target_pairs={{0,2},{1,5},{2,0},{3,7},{4,6},{5,1},{6,4},{7,3},{8,10},{9,13},{10,... | collective-permute-start | bytes 393224 | tf_op jit(solution)/shard_map/ppermute | solution.py:316
  65.7 7.3 %collective-permute-start.18 = (f32[2,4,32,128]{3,2,1,0:T(8,128)S(1)}, f32[2,4,32,128]{3,2,1,0:T(8,128)S(1)}, u32[]{:S(2)}, u32[]{:S(2)}) collective-permute-start(f32[2,4,32,128]{3,2,1,0:T(8,128)S(1)} %pad_maximum_fusion.4), channel_id=1, source_target_pairs={{0,16},{1,9},{2,18},{3,11},{4,20},{5,13},{6,22},{7,15},{8,24},{9,1... | collective-permute-start | bytes 393224 | tf_op jit(solution)/shard_map/ppermute | solution.py:316
  67.4 5.0 %collective-permute-start.16 = (f32[2,4,32,128]{3,2,1,0:T(8,128)S(1)}, f32[2,4,32,128]{3,2,1,0:T(8,128)S(1)}, u32[]{:S(2)}, u32[]{:S(2)}) collective-permute-start(f32[2,4,32,128]{3,2,1,0:T(8,128)S(1)} %pad_maximum_fusion.2), channel_id=1, source_target_pairs={{0,4},{1,3},{2,6},{3,1},{4,0},{5,7},{6,2},{7,5},{8,12},{9,11},{10,... | collective-permute-start | bytes 393224 | tf_op jit(solution)/shard_map/ppermute | solution.py:316
  73.1 2.0 %collective-permute-start.20 = (f32[24,32,128]{2,1,0:T(8,128)S(1)}, f32[24,32,128]{2,1,0:T(8,128)S(1)}, u32[]{:S(2)}, u32[]{:S(2)}) collective-permute-start(f32[24,32,128]{2,1,0:T(8,128)S(1)} %fusion.14.refs_1_), channel_id=1, source_target_pairs={{0,1},{1,0},{2,3},{3,2},{4,5},{5,4},{6,7},{7,6},{8,9},{9,8},{10,11... | collective-permute-start | bytes 1179656 | tf_op jit(solution)/shard_map/ppermute | solution.py:261
  73.2 1.9 %collective-permute-start.19 = (f32[8,32,128]{2,1,0:T(8,128)S(1)}, f32[8,32,128]{2,1,0:T(8,128)S(1)}, u32[]{:S(2)}, u32[]{:S(2)}) collective-permute-start(f32[8,32,128]{2,1,0:T(8,128)S(1)} %pad_maximum_fusion.refs_0_), channel_id=1, source_target_pairs={{0,1},{1,0},{2,3},{3,2},{4,5},{5,4},{6,7},{7,6},{8,9},{9,8},{10,11... | collective-permute-start | bytes 393224 | tf_op jit(solution)/shard_map/ppermute | solution.py:261

commit v6 on v5

--- a/solution.py
+++ b/solution.py
@@ -17,13 +17,15 @@
         self.lines = chips // PLANE
         self.rows = tile // 2 // cores
         self.bits = chips.bit_length() - 1
-        self.count = {
-            "cross": (PLANE - 1) * (self.lines - 1), "plane": PLANE - 1, "line": self.lines + 1,
+        self.pack = self.rows // 2 if self.rows >= 16 else self.rows
+        self.size = {
+            "cross": (PLANE - 1) * (self.lines - 1) * self.rows,
+            "plane": (PLANE - 1) * self.rows + self.pack, "line": self.lines * self.rows,
         }
         self.at, total = {}, 0
         for half in ("s", "k"):
-            for name, n in self.count.items():
-                size = chips // 2 * n * self.rows
+            for name, n in self.size.items():
+                size = chips // 2 * n
                 self.at[name, half] = (total, total + size)
                 total += size
         self.sent, self.total = total // 2, total
@@ -46,20 +48,21 @@
                 dz, dp = (unit // PLANE, unit % PLANE) if unit < self.chips else (-1, 0)
                 for parity in range(2):
                     p, q = self.place(dp, 2, parity), self.place(dz, self.bits - 2, parity)
-                    if dp == 0:
-                        name, i = "line", 1 + q
+                    if dz < 0:
+                        name, i = "plane", (PLANE - 1) * self.rows
+                    elif dp == 0:
+                        name, i = "line", q * self.rows
                     elif dz == 0:
-                        name, i = "plane", p - 1
+                        name, i = "plane", (p - 1) * self.rows
                     else:
-                        name, i = "cross", (p - 1) * (self.lines - 1) + q - 1
+                        name, i = "cross", ((p - 1) * (self.lines - 1) + q - 1) * self.rows
                     row = 0
                     at = j ^ dp if name == "cross" else j
                     for bit in self.order(name, parity):
                         row = 2 * row + (at >> bit & 1)
                     half = self.chips // 2
                     base = self.at[name, "s" if row >= half else "k"][0]
-                    row = (row % half) * self.count[name] + i
-                    out[j, unit, parity] = base + row * self.rows
+                    out[j, unit, parity] = base + (row % half) * self.size[name] + i
         return out.reshape(-1)
 
 
@@ -166,12 +169,18 @@
             entry = (jr * (sz.chips + 1) + unit) * 2
             for o in range(sz.cores):
                 of_core = o ^ core
-                row = pl.multiple_of(table_ref[entry + (of_core & 1)], sz.rows)
+                row = pl.multiple_of(table_ref[entry + (of_core & 1)], sz.pack)
                 where = pl.ds(row, sz.rows)
                 at = pl.multiple_of(p * tile + h * half + of_core * sz.rows, sz.rows)
                 new = res[
                     slot, q // 2, pl.ds(at, sz.rows), (q % 2) * tile:(q % 2 + 1) * tile
                 ]
+                if h and p == q and sz.pack < sz.rows:
+                    where = pl.ds(row, sz.pack)
+                    lane = lax.broadcasted_iota(jnp.int32, (sz.pack, tile), 1)
+                    new = jnp.where(
+                        lane < half, pltpu.roll(new[:sz.pack], half, 1), new[sz.pack:]
+                    )
                 old = send[o - 1, where, :] if o else keep[where, :]
                 todo.append((o, where, old + new))
         for o, where, value in todo:
@@ -208,7 +217,8 @@
     core = lax.axis_index("occ")
     tile = out.shape[0]
     half = tile // 2
-    n_plane = sz.count["plane"]
+    n_plane = PLANE - 1
+    line_at = n_plane * sz.rows + sz.pack
     for o in range(sz.cores):
         own, far = refs[2 * o:2 * o + 2]
         shift = (o ^ core) * sz.rows
@@ -220,13 +230,15 @@
                 for x, bits in ((dp, 2), (dz, sz.bits - 2))
             ]
             if dp == 0:
-                mine = own[n_plane + 1 + q]
+                mine = own[pl.ds(pl.multiple_of(line_at + q * sz.rows, sz.pack), sz.rows)]
             elif dz == 0:
-                mine = own[p - 1]
+                mine = own[pl.ds(pl.multiple_of((p - 1) * sz.rows, sz.rows), sz.rows)]
             else:
                 mine = far[(p - 1) * sz.lines + q]
             if d == 0:
-                other = own[n_plane]
+                other = own[line_at - sz.pack:line_at]
+                if sz.pack < sz.rows:
+                    other = jnp.concatenate([pltpu.roll(other, half, 1), other])
             elif dz == 0:
                 other = far[(p - 1) * sz.lines]
             else:
@@ -234,6 +246,11 @@
             top = (me >> (d.bit_length() - 1)) & 1 if d else 0
             tiles[d, pl.ds(pl.multiple_of(top * half + shift, sz.rows), sz.rows), :] = mine
             tiles[d, pl.ds(pl.multiple_of((1 - top) * half + shift, sz.rows), sz.rows), :] = other
+    if sz.pack < sz.rows:
+        row = lax.broadcasted_iota(jnp.int32, (tile, tile), 0)
+        column = lax.broadcasted_iota(jnp.int32, (tile, tile), 1)
+        whole = tiles[0]
+        tiles[0] = jnp.where((row >= half) & (column < half), whole.T, whole)
     blocks = sz.chips // sz.cores
     for i in range(blocks):
         k = owner_ref[core * blocks + i]
@@ -320,7 +337,7 @@
 
     def terms(name, half):
         lo, hi = sz.at[name, half]
-        shape = (chips // 2, sz.count[name], rows, tile)
+        shape = (chips // 2, sz.size[name], tile)
         cut = 2 if half == "k" else int(name != "cross")
         off = cuts[cut][0]
         return [x.reshape(shape) for x in [keep[lo:hi]] + [g[lo - off:hi - off] for g in got[cut]]]
@@ -342,7 +359,9 @@
     cross = total(parts["cross"])[0]
     line = total(parts["line"])[0] + 0 * cross[:1]
     plane = total(parts["plane"])[0] + 0 * line[:1]
+    own = jnp.concatenate([plane, line])
     cross = cross.reshape(PLANE - 1, lines - 1, rows, tile)
+    plane, line = plane[:-sz.pack].reshape(-1, rows, tile), line.reshape(lines, rows, tile)
     def across(blocks, name):
         for k in range(len(blocks).bit_length() - 1):
             moved = [q for q in range(len(blocks)) if q >> k & 1]
@@ -351,10 +370,9 @@
                 blocks[q] = come[i]
         return blocks[1:]
 
-    far = [jnp.concatenate([line[1 + q:2 + q], cross[:, q - 1]]) for q in range(1, lines)]
+    far = [jnp.concatenate([line[q:q + 1], cross[:, q - 1]]) for q in range(1, lines)]
     near = [jnp.concatenate([plane[q - 1:q], cross[q - 1]]) for q in range(1, PLANE)]
     far, near = across([None] + far, "line"), across([None] + near, "plane")
-    own = jnp.concatenate([plane, line])
     far = jnp.concatenate(near + far)
     every = [own, far]
     for e in range(1, cores):

time: 76.8 us -> 76.4 us (level)
  starting transfers between devices: 33.6 us -> 31.1 us
  waiting for transfers between devices: 29.4 us -> 31.8 us
    ppermute x16, starting transfers between devices: 31.8 us -> 29.4 us  [step(): return lax.ppermute(x, ('aux', 'occ'), pairs)]
    ppermute x16, waiting for transfers between devices: 25.6 us -> 28 us  [step(): return lax.ppermute(x, ('aux', 'occ'), pairs)]
  transfers between devices with their start and end apart: 21 -> 21, of which waited for: 13 -> 11; matrix products, arithmetic and copies ran while one was open for 2% -> 2% of each run, Pallas kernels for 0% -> 0%
where the time goes in v6:
time: 76.4 us; the launch traced here: 76.2 us
  waiting for transfers between devices  31.8 us (42%)
  starting transfers between devices  31.1 us (41%)
  Pallas kernels  11.6 us (15%)
  other arithmetic  1.34 us (2%)
    ppermute x16, starting transfers between devices, step(): return lax.ppermute(x, ('aux', 'occ'), pairs)  29.4 us
    ppermute x16, waiting for transfers between devices, step(): return lax.ppermute(x, ('aux', 'occ'), pairs)  28 us
    pallas_call x1, Pallas kernels, local(): pl.pallas_call(functools.partial(pair_kernel, sz), out_shape=[space((sz.t...  9.88 us
    ppermute x5, waiting for transfers between devices, go(): return lax.ppermute(x, 'occ', [(j, j ^ core) for j in range(cores)])  3.79 us
    ppermute x5, starting transfers between devices, go(): return lax.ppermute(x, 'occ', [(j, j ^ core) for j in range(cores)])  1.71 us
    pallas_call x1, Pallas kernels, local(): pl.pallas_call(functools.partial(place_kernel, sz), out_shape=jax.ShapeDt...  1.7 us
  transfers between devices with their start and end apart: 21, of which 11 were waited for; matrix products, arithmetic and copies ran while one was open for 2% of the time, Pallas kernels for 0%

profile of v6, /device:TPU:0, one launch (start us, length us, event | category | flops | bytes accessed | tf_op | source)
XLA Modules:
  0.0 76.2 jit_solution(6317595559132240581)
XLA Ops:
  0.0 9.9 %pairs.1 = (f32[8448,128]{1,0:T(8,128)S(1)}, f32[1,8448,128]{2,1,0:T(8,128)S(1)}) custom-call(s32[1,4,6]{2,1,0:T(4,128)} %slots_hbm.1, s32[16]{0:T(128)} %owner_ref.1, s32[544]{0:T(1024)} %constant.3.clone.table_hbm, bf16[1,4,6,128,1024]{4,3,2,1,0:T(8,128)(2,1)} %x_ref.1, bf16[4,128,128]{2,1,0:T(8,128)(2,1)} %fit_hbm.1), custom_call_target="tpu_custom_call" | custom-call | tf_op jit(solution)/shard_map/pairs/pallas_call | solution.py:285
  10.5 2.5 %collective-permute-done = f32[2304,128]{1,0:T(8,128)S(1)} collective-permute-done((f32[2304,128]{1,0:T(8,128)S(1)}, f32[2304,128]{1,0:T(8,128)S(1)}, u32[]{:S(2)}, u32[]{:S(2)}) %collective-permute-start) | collective-permute-done | bytes 1179680 | tf_op jit(solution)/shard_map/ppermute | solution.py:278
  13.9 2.9 %collective-permute-start.5 = (f32[8,288,128]{2,1,0:T(8,128)S(1)}, f32[8,288,128]{2,1,0:T(8,128)S(1)}, u32[]{:S(2)}, u32[]{:S(2)}) collective-permute-start(f32[8,288,128]{2,1,0:T(8,128)S(1)} %bitcast.136), channel_id=1, source_target_pairs={{0,2},{1,5},{2,0},{3,7},{4,6},{5,1},{6,4},{7,3},{8,10},{9,13},{10,... | collective-permute-start | bytes 3538952 | tf_op jit(solution)/shard_map/ppermute | solution.py:333
  16.9 2.0 %collective-permute-start.4 = (f32[8,128,128]{2,1,0:T(8,128)S(1)}, f32[8,128,128]{2,1,0:T(8,128)S(1)}, u32[]{:S(2)}, u32[]{:S(2)}) collective-permute-start(f32[8,128,128]{2,1,0:T(8,128)S(1)} %broadcast_add_fusion), channel_id=1, source_target_pairs={{0,8},{1,17},{2,10},{3,19},{4,12},{5,21},{6,14},{7,23},{8,0},{9,25... | collective-permute-start | bytes 1572872 | tf_op jit(solution)/shard_map/ppermute | solution.py:333
  19.0 1.5 %collective-permute-start.3 = (f32[8,112,128]{2,1,0:T(8,128)S(1)}, f32[8,112,128]{2,1,0:T(8,128)S(1)}, u32[]{:S(2)}, u32[]{:S(2)}) collective-permute-start(f32[8,112,128]{2,1,0:T(8,128)S(1)} %broadcast_add_fusion.1), channel_id=1, source_target_pairs={{0,2},{1,5},{2,0},{3,7},{4,6},{5,1},{6,4},{7,3},{8,10},{9,13},{10,... | collective-permute-start | bytes 1376264 | tf_op jit(solution)/shard_map/ppermute | solution.py:333
  20.7 10.3 %collective-permute-done.5 = f32[8,288,128]{2,1,0:T(8,128)S(1)} collective-permute-done((f32[8,288,128]{2,1,0:T(8,128)S(1)}, f32[8,288,128]{2,1,0:T(8,128)S(1)}, u32[]{:S(2)}, u32[]{:S(2)}) %collective-permute-start.5) | collective-permute-done | bytes 1179680 | tf_op jit(solution)/shard_map/ppermute | solution.py:333
  31.1 2.1 %collective-permute-start.8 = (f32[4,288,128]{2,1,0:T(8,128)S(1)}, f32[4,288,128]{2,1,0:T(8,128)S(1)}, u32[]{:S(2)}, u32[]{:S(2)}) collective-permute-start(f32[4,288,128]{2,1,0:T(8,128)S(1)} %fusion), channel_id=1, source_target_pairs={{0,4},{1,3},{2,6},{3,1},{4,0},{5,7},{6,2},{7,5},{8,12},{9,11},{10,... | collective-permute-start | bytes 1769480 | tf_op jit(solution)/shard_map/ppermute | solution.py:333
  33.3 2.6 %collective-permute-start.7 = (f32[4,128,128]{2,1,0:T(8,128)S(1)}, f32[4,128,128]{2,1,0:T(8,128)S(1)}, u32[]{:S(2)}, u32[]{:S(2)}) collective-permute-start(f32[4,128,128]{2,1,0:T(8,128)S(1)} %fusion.2), channel_id=1, source_target_pairs={{0,16},{1,9},{2,18},{3,11},{4,20},{5,13},{6,22},{7,15},{8,24},{9,1... | collective-permute-start | bytes 786440 | tf_op jit(solution)/shard_map/ppermute | solution.py:333
  35.9 2.5 %collective-permute-done.3 = f32[8,112,128]{2,1,0:T(8,128)S(1)} collective-permute-done((f32[8,112,128]{2,1,0:T(8,128)S(1)}, f32[8,112,128]{2,1,0:T(8,128)S(1)}, u32[]{:S(2)}, u32[]{:S(2)}) %collective-permute-start.3) | collective-permute-done | bytes 458784 | tf_op jit(solution)/shard_map/ppermute | solution.py:333
  38.5 2.4 %collective-permute-start.6 = (f32[4,112,128]{2,1,0:T(8,128)S(1)}, f32[4,112,128]{2,1,0:T(8,128)S(1)}, u32[]{:S(2)}, u32[]{:S(2)}) collective-permute-start(f32[4,112,128]{2,1,0:T(8,128)S(1)} %fusion.3), channel_id=1, source_target_pairs={{0,4},{1,3},{2,6},{3,1},{4,0},{5,7},{6,2},{7,5},{8,12},{9,11},{10,... | collective-permute-start | bytes 688136 | tf_op jit(solution)/shard_map/ppermute | solution.py:333
  41.8 1.9 %collective-permute-start.11 = (f32[2,288,128]{2,1,0:T(8,128)S(1)}, f32[2,288,128]{2,1,0:T(8,128)S(1)}, u32[]{:S(2)}, u32[]{:S(2)}) collective-permute-start(f32[2,288,128]{2,1,0:T(8,128)S(1)} %fusion.1), channel_id=1, source_target_pairs={{0,8},{1,17},{2,10},{3,19},{4,12},{5,21},{6,14},{7,23},{8,0},{9,25... | collective-permute-start | bytes 884744 | tf_op jit(solution)/shard_map/ppermute | solution.py:333
  43.7 1.5 %collective-permute-start.10 = (f32[2,128,128]{2,1,0:T(8,128)S(1)}, f32[2,128,128]{2,1,0:T(8,128)S(1)}, u32[]{:S(2)}, u32[]{:S(2)}) collective-permute-start(f32[2,128,128]{2,1,0:T(8,128)S(1)} %fusion.8), channel_id=1, source_target_pairs={{0,2},{1,5},{2,0},{3,7},{4,6},{5,1},{6,4},{7,3},{8,10},{9,13},{10,... | collective-permute-start | bytes 393224 | tf_op jit(solution)/shard_map/ppermute | solution.py:333
  45.3 1.8 %collective-permute-start.9 = (f32[2,112,128]{2,1,0:T(8,128)S(1)}, f32[2,112,128]{2,1,0:T(8,128)S(1)}, u32[]{:S(2)}, u32[]{:S(2)}) collective-permute-start(f32[2,112,128]{2,1,0:T(8,128)S(1)} %fusion.9), channel_id=1, source_target_pairs={{0,8},{1,17},{2,10},{3,19},{4,12},{5,21},{6,14},{7,23},{8,0},{9,25... | collective-permute-start | bytes 344072 | tf_op jit(solution)/shard_map/ppermute | solution.py:333
  47.1 4.9 %collective-permute-done.11 = f32[2,288,128]{2,1,0:T(8,128)S(1)} collective-permute-done((f32[2,288,128]{2,1,0:T(8,128)S(1)}, f32[2,288,128]{2,1,0:T(8,128)S(1)}, u32[]{:S(2)}, u32[]{:S(2)}) %collective-permute-start.11) | collective-permute-done | bytes 294944 | tf_op jit(solution)/shard_map/ppermute | solution.py:333
  52.1 2.6 %collective-permute-start.14 = (f32[1,288,128]{2,1,0:T(8,128)S(1)}, f32[1,288,128]{2,1,0:T(8,128)S(1)}, u32[]{:S(2)}, u32[]{:S(2)}) collective-permute-start(f32[1,288,128]{2,1,0:T(8,128)S(1)} %fusion.6), channel_id=1, source_target_pairs={{0,16},{1,9},{2,18},{3,11},{4,20},{5,13},{6,22},{7,15},{8,24},{9,1... | collective-permute-start | bytes 442376 | tf_op jit(solution)/shard_map/ppermute | solution.py:333
  54.7 1.5 %collective-permute-start.13 = (f32[1,128,128]{2,1,0:T(8,128)S(1)}, f32[1,128,128]{2,1,0:T(8,128)S(1)}, u32[]{:S(2)}, u32[]{:S(2)}) collective-permute-start(f32[1,128,128]{2,1,0:T(8,128)S(1)} %fusion.20), channel_id=1, source_target_pairs={{0,4},{1,3},{2,6},{3,1},{4,0},{5,7},{6,2},{7,5},{8,12},{9,11},{10,... | collective-permute-start | bytes 196616 | tf_op jit(solution)/shard_map/ppermute | solution.py:333
  56.9 2.9 %collective-permute-done.14 = f32[1,288,128]{2,1,0:T(8,128)S(1)} collective-permute-done((f32[1,288,128]{2,1,0:T(8,128)S(1)}, f32[1,288,128]{2,1,0:T(8,128)S(1)}, u32[]{:S(2)}, u32[]{:S(2)}) %collective-permute-start.14) | collective-permute-done | bytes 147488 | tf_op jit(solution)/shard_map/ppermute | solution.py:333
  62.0 1.6 %collective-permute-start.15 = (f32[2,4,32,128]{3,2,1,0:T(8,128)S(1)}, f32[2,4,32,128]{3,2,1,0:T(8,128)S(1)}, u32[]{:S(2)}, u32[]{:S(2)}) collective-permute-start(f32[2,4,32,128]{3,2,1,0:T(8,128)S(1)} %pad_maximum_fusion), channel_id=1, source_target_pairs={{0,2},{1,5},{2,0},{3,7},{4,6},{5,1},{6,4},{7,3},{8,10},{9,13},{10,... | collective-permute-start | bytes 393224 | tf_op jit(solution)/shard_map/ppermute | solution.py:333
  63.6 1.6 %collective-permute-done.17 = f32[2,4,32,128]{3,2,1,0:T(8,128)S(1)} collective-permute-done((f32[2,4,32,128]{3,2,1,0:T(8,128)S(1)}, f32[2,4,32,128]{3,2,1,0:T(8,128)S(1)}, u32[]{:S(2)}, u32[]{:S(2)}) %collective-permute-start.17) | collective-permute-done | bytes 131104 | tf_op jit(solution)/shard_map/ppermute | solution.py:333
  65.2 2.2 %collective-permute-start.18 = (f32[2,4,32,128]{3,2,1,0:T(8,128)S(1)}, f32[2,4,32,128]{3,2,1,0:T(8,128)S(1)}, u32[]{:S(2)}, u32[]{:S(2)}) collective-permute-start(f32[2,4,32,128]{3,2,1,0:T(8,128)S(1)} %pad_maximum_fusion.3), channel_id=1, source_target_pairs={{0,16},{1,9},{2,18},{3,11},{4,20},{5,13},{6,22},{7,15},{8,24},{9,1... | collective-permute-start | bytes 393224 | tf_op jit(solution)/shard_map/ppermute | solution.py:333
  67.4 1.4 %collective-permute-start.16 = (f32[2,4,32,128]{3,2,1,0:T(8,128)S(1)}, f32[2,4,32,128]{3,2,1,0:T(8,128)S(1)}, u32[]{:S(2)}, u32[]{:S(2)}) collective-permute-start(f32[2,4,32,128]{3,2,1,0:T(8,128)S(1)} %pad_maximum_fusion.1), channel_id=1, source_target_pairs={{0,4},{1,3},{2,6},{3,1},{4,0},{5,7},{6,2},{7,5},{8,12},{9,11},{10,... | collective-permute-start | bytes 393224 | tf_op jit(solution)/shard_map/ppermute | solution.py:333
  68.8 3.6 %collective-permute-done.16 = f32[2,4,32,128]{3,2,1,0:T(8,128)S(1)} collective-permute-done((f32[2,4,32,128]{3,2,1,0:T(8,128)S(1)}, f32[2,4,32,128]{3,2,1,0:T(8,128)S(1)}, u32[]{:S(2)}, u32[]{:S(2)}) %collective-permute-start.16) | collective-permute-done | bytes 131104 | tf_op jit(solution)/shard_map/ppermute | solution.py:333
  73.2 1.3 %collective-permute-done.19.refs_2_ = f32[240,128]{1,0:T(8,128)S(1)} collective-permute-done((f32[240,128]{1,0:T(8,128)S(1)}, f32[240,128]{1,0:T(8,128)S(1)}, u32[]{:S(2)}, u32[]{:S(2)}) %collective-permute-start.19) | collective-permute-done | bytes 122912 | tf_op jit(solution)/shard_map/ppermute | solution.py:278
  74.5 1.7 %place.1 = f32[128,1024]{1,0:T(8,128)} custom-call(s32[16]{0:T(128)S(1)} %copy-done, f32[240,128]{1,0:T(8,128)S(1)} %pad_maximum_fusion.4.refs_0_, f32[24,32,128]{2,1,0:T(8,128)S(1)} %fusion.10.refs_1_, f32[240,128]{1,0:T(8,128)S(1)} %collective-permute-done.19.refs_2_, f32[24,32,128]{2,1,0:T(8,128)S(1)} %collective-permute-done.20.refs_3_), custom_call_target="tpu_custom_call" | custom-call | tf_op jit(solution)/shard_map/place/pallas_call | solution.py:381
  (83 shorter events, 6.7 us)
Async XLA Ops:
  10.0 3.0 %collective-permute-start = (f32[2304,128]{1,0:T(8,128)S(1)}, f32[2304,128]{1,0:T(8,128)S(1)}, u32[]{:S(2)}, u32[]{:S(2)}) collective-permute-start(f32[2304,128]{1,0:T(8,128)S(1)} %slice_bitcast_fusion), channel_id=1, source_target_pairs={{0,1},{1,0},{2,3},{3,2},{4,5},{5,4},{6,7},{7,6},{8,9},{9,8},{10,11... | collective-permute-start | bytes 3538952 | tf_op jit(solution)/shard_map/ppermute | solution.py:278
  13.2 3.6 %collective-permute-start.2 = (f32[1920,128]{1,0:T(8,128)S(1)}, f32[1920,128]{1,0:T(8,128)S(1)}, u32[]{:S(2)}, u32[]{:S(2)}) collective-permute-start(f32[1920,128]{1,0:T(8,128)S(1)} %bitcast_add_fusion.1), channel_id=1, source_target_pairs={{0,1},{1,0},{2,3},{3,2},{4,5},{5,4},{6,7},{7,6},{8,9},{9,8},{10,11... | collective-permute-start | bytes 2949128 | tf_op jit(solution)/shard_map/ppermute | solution.py:278
  13.6 7.0 %collective-permute-start.1 = (f32[4224,128]{1,0:T(8,128)S(1)}, f32[4224,128]{1,0:T(8,128)S(1)}, u32[]{:S(2)}, u32[]{:S(2)}) collective-permute-start(f32[4224,128]{1,0:T(8,128)S(1)} %bitcast_add_fusion), channel_id=1, source_target_pairs={{0,1},{1,0},{2,3},{3,2},{4,5},{5,4},{6,7},{7,6},{8,9},{9,8},{10,11... | collective-permute-start | bytes 6488072 | tf_op jit(solution)/shard_map/ppermute | solution.py:278
  13.9 17.1 %collective-permute-start.5 = (f32[8,288,128]{2,1,0:T(8,128)S(1)}, f32[8,288,128]{2,1,0:T(8,128)S(1)}, u32[]{:S(2)}, u32[]{:S(2)}) collective-permute-start(f32[8,288,128]{2,1,0:T(8,128)S(1)} %bitcast.136), channel_id=1, source_target_pairs={{0,2},{1,5},{2,0},{3,7},{4,6},{5,1},{6,4},{7,3},{8,10},{9,13},{10,... | collective-permute-start | bytes 3538952 | tf_op jit(solution)/shard_map/ppermute | solution.py:333
  16.9 16.3 %collective-permute-start.4 = (f32[8,128,128]{2,1,0:T(8,128)S(1)}, f32[8,128,128]{2,1,0:T(8,128)S(1)}, u32[]{:S(2)}, u32[]{:S(2)}) collective-permute-start(f32[8,128,128]{2,1,0:T(8,128)S(1)} %broadcast_add_fusion), channel_id=1, source_target_pairs={{0,8},{1,17},{2,10},{3,19},{4,12},{5,21},{6,14},{7,23},{8,0},{9,25... | collective-permute-start | bytes 1572872 | tf_op jit(solution)/shard_map/ppermute | solution.py:333
  19.0 19.4 %collective-permute-start.3 = (f32[8,112,128]{2,1,0:T(8,128)S(1)}, f32[8,112,128]{2,1,0:T(8,128)S(1)}, u32[]{:S(2)}, u32[]{:S(2)}) collective-permute-start(f32[8,112,128]{2,1,0:T(8,128)S(1)} %broadcast_add_fusion.1), channel_id=1, source_target_pairs={{0,2},{1,5},{2,0},{3,7},{4,6},{5,1},{6,4},{7,3},{8,10},{9,13},{10,... | collective-permute-start | bytes 1376264 | tf_op jit(solution)/shard_map/ppermute | solution.py:333
  31.1 10.6 %collective-permute-start.8 = (f32[4,288,128]{2,1,0:T(8,128)S(1)}, f32[4,288,128]{2,1,0:T(8,128)S(1)}, u32[]{:S(2)}, u32[]{:S(2)}) collective-permute-start(f32[4,288,128]{2,1,0:T(8,128)S(1)} %fusion), channel_id=1, source_target_pairs={{0,4},{1,3},{2,6},{3,1},{4,0},{5,7},{6,2},{7,5},{8,12},{9,11},{10,... | collective-permute-start | bytes 1769480 | tf_op jit(solution)/shard_map/ppermute | solution.py:333
  33.3 10.4 %collective-permute-start.7 = (f32[4,128,128]{2,1,0:T(8,128)S(1)}, f32[4,128,128]{2,1,0:T(8,128)S(1)}, u32[]{:S(2)}, u32[]{:S(2)}) collective-permute-start(f32[4,128,128]{2,1,0:T(8,128)S(1)} %fusion.2), channel_id=1, source_target_pairs={{0,16},{1,9},{2,18},{3,11},{4,20},{5,13},{6,22},{7,15},{8,24},{9,1... | collective-permute-start | bytes 786440 | tf_op jit(solution)/shard_map/ppermute | solution.py:333
  38.5 6.7 %collective-permute-start.6 = (f32[4,112,128]{2,1,0:T(8,128)S(1)}, f32[4,112,128]{2,1,0:T(8,128)S(1)}, u32[]{:S(2)}, u32[]{:S(2)}) collective-permute-start(f32[4,112,128]{2,1,0:T(8,128)S(1)} %fusion.3), channel_id=1, source_target_pairs={{0,4},{1,3},{2,6},{3,1},{4,0},{5,7},{6,2},{7,5},{8,12},{9,11},{10,... | collective-permute-start | bytes 688136 | tf_op jit(solution)/shard_map/ppermute | solution.py:333
  41.8 10.3 %collective-permute-start.11 = (f32[2,288,128]{2,1,0:T(8,128)S(1)}, f32[2,288,128]{2,1,0:T(8,128)S(1)}, u32[]{:S(2)}, u32[]{:S(2)}) collective-permute-start(f32[2,288,128]{2,1,0:T(8,128)S(1)} %fusion.1), channel_id=1, source_target_pairs={{0,8},{1,17},{2,10},{3,19},{4,12},{5,21},{6,14},{7,23},{8,0},{9,25... | collective-permute-start | bytes 884744 | tf_op jit(solution)/shard_map/ppermute | solution.py:333
  43.7 11.0 %collective-permute-start.10 = (f32[2,128,128]{2,1,0:T(8,128)S(1)}, f32[2,128,128]{2,1,0:T(8,128)S(1)}, u32[]{:S(2)}, u32[]{:S(2)}) collective-permute-start(f32[2,128,128]{2,1,0:T(8,128)S(1)} %fusion.8), channel_id=1, source_target_pairs={{0,2},{1,5},{2,0},{3,7},{4,6},{5,1},{6,4},{7,3},{8,10},{9,13},{10,... | collective-permute-start | bytes 393224 | tf_op jit(solution)/shard_map/ppermute | solution.py:333
  45.3 10.9 %collective-permute-start.9 = (f32[2,112,128]{2,1,0:T(8,128)S(1)}, f32[2,112,128]{2,1,0:T(8,128)S(1)}, u32[]{:S(2)}, u32[]{:S(2)}) collective-permute-start(f32[2,112,128]{2,1,0:T(8,128)S(1)} %fusion.9), channel_id=1, source_target_pairs={{0,8},{1,17},{2,10},{3,19},{4,12},{5,21},{6,14},{7,23},{8,0},{9,25... | collective-permute-start | bytes 344072 | tf_op jit(solution)/shard_map/ppermute | solution.py:333
  52.1 7.7 %collective-permute-start.14 = (f32[1,288,128]{2,1,0:T(8,128)S(1)}, f32[1,288,128]{2,1,0:T(8,128)S(1)}, u32[]{:S(2)}, u32[]{:S(2)}) collective-permute-start(f32[1,288,128]{2,1,0:T(8,128)S(1)} %fusion.6), channel_id=1, source_target_pairs={{0,16},{1,9},{2,18},{3,11},{4,20},{5,13},{6,22},{7,15},{8,24},{9,1... | collective-permute-start | bytes 442376 | tf_op jit(solution)/shard_map/ppermute | solution.py:333
  54.7 5.2 %collective-permute-start.13 = (f32[1,128,128]{2,1,0:T(8,128)S(1)}, f32[1,128,128]{2,1,0:T(8,128)S(1)}, u32[]{:S(2)}, u32[]{:S(2)}) collective-permute-start(f32[1,128,128]{2,1,0:T(8,128)S(1)} %fusion.20), channel_id=1, source_target_pairs={{0,4},{1,3},{2,6},{3,1},{4,0},{5,7},{6,2},{7,5},{8,12},{9,11},{10,... | collective-permute-start | bytes 196616 | tf_op jit(solution)/shard_map/ppermute | solution.py:333
  56.2 5.8 %collective-permute-start.12 = (f32[1,112,128]{2,1,0:T(8,128)S(1)}, f32[1,112,128]{2,1,0:T(8,128)S(1)}, u32[]{:S(2)}, u32[]{:S(2)}) collective-permute-start(f32[1,112,128]{2,1,0:T(8,128)S(1)} %fusion.22), channel_id=1, source_target_pairs={{0,16},{1,9},{2,18},{3,11},{4,20},{5,13},{6,22},{7,15},{8,24},{9,1... | collective-permute-start | bytes 172040 | tf_op jit(solution)/shard_map/ppermute | solution.py:333
  59.9 14.7 %copy-start = (s32[16]{0:T(128)S(1)}, s32[16]{0:T(128)}, u32[]{:S(2)}) copy-start(s32[16]{0:T(128)} %owner_ref.1) | copy-start | bytes 196
  60.0 5.2 %collective-permute-start.17 = (f32[2,4,32,128]{3,2,1,0:T(8,128)S(1)}, f32[2,4,32,128]{3,2,1,0:T(8,128)S(1)}, u32[]{:S(2)}, u32[]{:S(2)}) collective-permute-start(f32[2,4,32,128]{3,2,1,0:T(8,128)S(1)} %pad_maximum_fusion.2), channel_id=1, source_target_pairs={{0,8},{1,17},{2,10},{3,19},{4,12},{5,21},{6,14},{7,23},{8,0},{9,25... | collective-permute-start | bytes 393224 | tf_op jit(solution)/shard_map/ppermute | solution.py:333
  62.0 5.4 %collective-permute-start.15 = (f32[2,4,32,128]{3,2,1,0:T(8,128)S(1)}, f32[2,4,32,128]{3,2,1,0:T(8,128)S(1)}, u32[]{:S(2)}, u32[]{:S(2)}) collective-permute-start(f32[2,4,32,128]{3,2,1,0:T(8,128)S(1)} %pad_maximum_fusion), channel_id=1, source_target_pairs={{0,2},{1,5},{2,0},{3,7},{4,6},{5,1},{6,4},{7,3},{8,10},{9,13},{10,... | collective-permute-start | bytes 393224 | tf_op jit(solution)/shard_map/ppermute | solution.py:333
  65.2 7.3 %collective-permute-start.18 = (f32[2,4,32,128]{3,2,1,0:T(8,128)S(1)}, f32[2,4,32,128]{3,2,1,0:T(8,128)S(1)}, u32[]{:S(2)}, u32[]{:S(2)}) collective-permute-start(f32[2,4,32,128]{3,2,1,0:T(8,128)S(1)} %pad_maximum_fusion.3), channel_id=1, source_target_pairs={{0,16},{1,9},{2,18},{3,11},{4,20},{5,13},{6,22},{7,15},{8,24},{9,1... | collective-permute-start | bytes 393224 | tf_op jit(solution)/shard_map/ppermute | solution.py:333
  67.4 5.0 %collective-permute-start.16 = (f32[2,4,32,128]{3,2,1,0:T(8,128)S(1)}, f32[2,4,32,128]{3,2,1,0:T(8,128)S(1)}, u32[]{:S(2)}, u32[]{:S(2)}) collective-permute-start(f32[2,4,32,128]{3,2,1,0:T(8,128)S(1)} %pad_maximum_fusion.1), channel_id=1, source_target_pairs={{0,4},{1,3},{2,6},{3,1},{4,0},{5,7},{6,2},{7,5},{8,12},{9,11},{10,... | collective-permute-start | bytes 393224 | tf_op jit(solution)/shard_map/ppermute | solution.py:333
  72.6 2.0 %collective-permute-start.20 = (f32[24,32,128]{2,1,0:T(8,128)S(1)}, f32[24,32,128]{2,1,0:T(8,128)S(1)}, u32[]{:S(2)}, u32[]{:S(2)}) collective-permute-start(f32[24,32,128]{2,1,0:T(8,128)S(1)} %fusion.10.refs_1_), channel_id=1, source_target_pairs={{0,1},{1,0},{2,3},{3,2},{4,5},{5,4},{6,7},{7,6},{8,9},{9,8},{10,11... | collective-permute-start | bytes 1179656 | tf_op jit(solution)/shard_map/ppermute | solution.py:278
  72.7 1.9 %collective-permute-start.19 = (f32[240,128]{1,0:T(8,128)S(1)}, f32[240,128]{1,0:T(8,128)S(1)}, u32[]{:S(2)}, u32[]{:S(2)}) collective-permute-start(f32[240,128]{1,0:T(8,128)S(1)} %pad_maximum_fusion.4.refs_0_), channel_id=1, source_target_pairs={{0,1},{1,0},{2,3},{3,2},{4,5},{5,4},{6,7},{7,6},{8,9},{9,8},{10,11... | collective-permute-start | bytes 368648 | tf_op jit(solution)/shard_map/ppermute | solution.py:278

commit v7 on v6

--- a/solution.py
+++ b/solution.py
@@ -348,14 +348,19 @@
             if k:
                 n = parts[name][0].shape[0] // 2
                 sent, parts[name] = [x[n:] for x in parts[name]], [x[:n] for x in parts[name]]
+                if k == 1 and name == "line":
+                    sent, parts[name] = sent + [upper], parts[name] + [lower]
             else:
                 sent, parts[name] = terms(name, "s"), terms(name, "k")
             sent = total(sent)
             if before is not None:
                 sent = sent + 0 * before[:sent.shape[0], :1]
             before = sent
-            come = step(sent, name, k)
-            parts[name].append(come)
+            if k == 0 and name == "line":
+                n = chips // 4
+                upper, lower = step(sent[n:], name, k), step(sent[:n], name, k)
+            else:
+                parts[name].append(step(sent, name, k))
     cross = total(parts["cross"])[0]
     line = total(parts["line"])[0] + 0 * cross[:1]
     plane = total(parts["plane"])[0] + 0 * line[:1]

time: 76.4 us -> 76.4 us (level)
  waiting for transfers between devices: 31.8 us -> 30.4 us
  starting transfers between devices: 31.1 us -> 32.4 us
    ppermute x16 -> x17, waiting for transfers between devices: 28 us -> 26.6 us  [step(): return lax.ppermute(x, ('aux', 'occ'), pairs)]
    ppermute x16 -> x17, starting transfers between devices: 29.4 us -> 30.6 us  [step(): return lax.ppermute(x, ('aux', 'occ'), pairs)]
  transfers between devices with their start and end apart: 21 -> 22, of which waited for: 11 -> 10; matrix products, arithmetic and copies ran while one was open for 2% -> 2% of each run, Pallas kernels for 0% -> 0%
where the time goes in v7:
time: 76.4 us; the launch traced here: 76.2 us
  starting transfers between devices  32.4 us (42%)
  waiting for transfers between devices  30.4 us (40%)
  Pallas kernels  11.6 us (15%)
  other arithmetic  1.36 us (2%)
    ppermute x17, starting transfers between devices, step(): return lax.ppermute(x, ('aux', 'occ'), pairs)  30.6 us
    ppermute x17, waiting for transfers between devices, step(): return lax.ppermute(x, ('aux', 'occ'), pairs)  26.6 us
    pallas_call x1, Pallas kernels, local(): pl.pallas_call(functools.partial(pair_kernel, sz), out_shape=[space((sz.t...  9.85 us
    ppermute x5, waiting for transfers between devices, go(): return lax.ppermute(x, 'occ', [(j, j ^ core) for j in range(cores)])  3.79 us
    ppermute x5, starting transfers between devices, go(): return lax.ppermute(x, 'occ', [(j, j ^ core) for j in range(cores)])  1.74 us
    pallas_call x1, Pallas kernels, local(): pl.pallas_call(functools.partial(place_kernel, sz), out_shape=jax.ShapeDt...  1.7 us
  transfers between devices with their start and end apart: 22, of which 10 were waited for; matrix products, arithmetic and copies ran while one was open for 2% of the time, Pallas kernels for 0%

profile of v7, /device:TPU:0, one launch (start us, length us, event | category | flops | bytes accessed | tf_op | source)
XLA Modules:
  0.0 76.2 jit_solution(12789019204653269849)
XLA Ops:
  0.0 9.9 %pairs.1 = (f32[8448,128]{1,0:T(8,128)S(1)}, f32[1,8448,128]{2,1,0:T(8,128)S(1)}) custom-call(s32[1,4,6]{2,1,0:T(4,128)} %slots_hbm.1, s32[16]{0:T(128)} %owner_ref.1, s32[544]{0:T(1024)} %constant.3.clone.table_hbm, bf16[1,4,6,128,1024]{4,3,2,1,0:T(8,128)(2,1)} %x_ref.1, bf16[4,128,128]{2,1,0:T(8,128)(2,1)} %fit_hbm.1), custom_call_target="tpu_custom_call" | custom-call | tf_op jit(solution)/shard_map/pairs/pallas_call | solution.py:285
  10.5 2.5 %collective-permute-done = f32[2304,128]{1,0:T(8,128)S(1)} collective-permute-done((f32[2304,128]{1,0:T(8,128)S(1)}, f32[2304,128]{1,0:T(8,128)S(1)}, u32[]{:S(2)}, u32[]{:S(2)}) %collective-permute-start) | collective-permute-done | bytes 1179680 | tf_op jit(solution)/shard_map/ppermute | solution.py:278
  13.9 2.9 %collective-permute-start.5 = (f32[8,288,128]{2,1,0:T(8,128)S(1)}, f32[8,288,128]{2,1,0:T(8,128)S(1)}, u32[]{:S(2)}, u32[]{:S(2)}) collective-permute-start(f32[8,288,128]{2,1,0:T(8,128)S(1)} %bitcast.136), channel_id=1, source_target_pairs={{0,2},{1,5},{2,0},{3,7},{4,6},{5,1},{6,4},{7,3},{8,10},{9,13},{10,... | collective-permute-start | bytes 3538952 | tf_op jit(solution)/shard_map/ppermute | solution.py:333
  17.0 2.0 %collective-permute-start.4 = (f32[4,128,128]{2,1,0:T(8,128)S(1)}, f32[4,128,128]{2,1,0:T(8,128)S(1)}, u32[]{:S(2)}, u32[]{:S(2)}) collective-permute-start(f32[4,128,128]{2,1,0:T(8,128)S(1)} %get-tuple-element.10), channel_id=1, source_target_pairs={{0,8},{1,17},{2,10},{3,19},{4,12},{5,21},{6,14},{7,23},{8,0},{9,25... | collective-permute-start | bytes 786440 | tf_op jit(solution)/shard_map/ppermute | solution.py:333
  19.1 1.5 %collective-permute-start.3 = (f32[8,112,128]{2,1,0:T(8,128)S(1)}, f32[8,112,128]{2,1,0:T(8,128)S(1)}, u32[]{:S(2)}, u32[]{:S(2)}) collective-permute-start(f32[8,112,128]{2,1,0:T(8,128)S(1)} %broadcast_add_fusion.1), channel_id=1, source_target_pairs={{0,2},{1,5},{2,0},{3,7},{4,6},{5,1},{6,4},{7,3},{8,10},{9,13},{10,... | collective-permute-start | bytes 1376264 | tf_op jit(solution)/shard_map/ppermute | solution.py:333
  21.1 9.8 %collective-permute-done.5 = f32[8,288,128]{2,1,0:T(8,128)S(1)} collective-permute-done((f32[8,288,128]{2,1,0:T(8,128)S(1)}, f32[8,288,128]{2,1,0:T(8,128)S(1)}, u32[]{:S(2)}, u32[]{:S(2)}) %collective-permute-start.5) | collective-permute-done | bytes 1179680 | tf_op jit(solution)/shard_map/ppermute | solution.py:333
  31.1 2.1 %collective-permute-start.9 = (f32[4,288,128]{2,1,0:T(8,128)S(1)}, f32[4,288,128]{2,1,0:T(8,128)S(1)}, u32[]{:S(2)}, u32[]{:S(2)}) collective-permute-start(f32[4,288,128]{2,1,0:T(8,128)S(1)} %fusion), channel_id=1, source_target_pairs={{0,4},{1,3},{2,6},{3,1},{4,0},{5,7},{6,2},{7,5},{8,12},{9,11},{10,... | collective-permute-start | bytes 1769480 | tf_op jit(solution)/shard_map/ppermute | solution.py:333
  33.2 2.6 %collective-permute-start.8 = (f32[4,128,128]{2,1,0:T(8,128)S(1)}, f32[4,128,128]{2,1,0:T(8,128)S(1)}, u32[]{:S(2)}, u32[]{:S(2)}) collective-permute-start(f32[4,128,128]{2,1,0:T(8,128)S(1)} %add_add_fusion), channel_id=1, source_target_pairs={{0,16},{1,9},{2,18},{3,11},{4,20},{5,13},{6,22},{7,15},{8,24},{9,1... | collective-permute-start | bytes 786440 | tf_op jit(solution)/shard_map/ppermute | solution.py:333
  35.9 2.5 %collective-permute-done.3 = f32[8,112,128]{2,1,0:T(8,128)S(1)} collective-permute-done((f32[8,112,128]{2,1,0:T(8,128)S(1)}, f32[8,112,128]{2,1,0:T(8,128)S(1)}, u32[]{:S(2)}, u32[]{:S(2)}) %collective-permute-start.3) | collective-permute-done | bytes 458784 | tf_op jit(solution)/shard_map/ppermute | solution.py:333
  38.4 2.4 %collective-permute-start.6 = (f32[4,112,128]{2,1,0:T(8,128)S(1)}, f32[4,112,128]{2,1,0:T(8,128)S(1)}, u32[]{:S(2)}, u32[]{:S(2)}) collective-permute-start(f32[4,112,128]{2,1,0:T(8,128)S(1)} %fusion.2), channel_id=1, source_target_pairs={{0,4},{1,3},{2,6},{3,1},{4,0},{5,7},{6,2},{7,5},{8,12},{9,11},{10,... | collective-permute-start | bytes 688136 | tf_op jit(solution)/shard_map/ppermute | solution.py:333
  41.8 1.9 %collective-permute-start.12 = (f32[2,288,128]{2,1,0:T(8,128)S(1)}, f32[2,288,128]{2,1,0:T(8,128)S(1)}, u32[]{:S(2)}, u32[]{:S(2)}) collective-permute-start(f32[2,288,128]{2,1,0:T(8,128)S(1)} %fusion.1), channel_id=1, source_target_pairs={{0,8},{1,17},{2,10},{3,19},{4,12},{5,21},{6,14},{7,23},{8,0},{9,25... | collective-permute-start | bytes 884744 | tf_op jit(solution)/shard_map/ppermute | solution.py:333
  43.7 1.5 %collective-permute-start.11 = (f32[2,128,128]{2,1,0:T(8,128)S(1)}, f32[2,128,128]{2,1,0:T(8,128)S(1)}, u32[]{:S(2)}, u32[]{:S(2)}) collective-permute-start(f32[2,128,128]{2,1,0:T(8,128)S(1)} %fusion.7), channel_id=1, source_target_pairs={{0,2},{1,5},{2,0},{3,7},{4,6},{5,1},{6,4},{7,3},{8,10},{9,13},{10,... | collective-permute-start | bytes 393224 | tf_op jit(solution)/shard_map/ppermute | solution.py:333
  45.3 1.8 %collective-permute-start.10 = (f32[2,112,128]{2,1,0:T(8,128)S(1)}, f32[2,112,128]{2,1,0:T(8,128)S(1)}, u32[]{:S(2)}, u32[]{:S(2)}) collective-permute-start(f32[2,112,128]{2,1,0:T(8,128)S(1)} %fusion.8), channel_id=1, source_target_pairs={{0,8},{1,17},{2,10},{3,19},{4,12},{5,21},{6,14},{7,23},{8,0},{9,25... | collective-permute-start | bytes 344072 | tf_op jit(solution)/shard_map/ppermute | solution.py:333
  47.1 4.9 %collective-permute-done.12 = f32[2,288,128]{2,1,0:T(8,128)S(1)} collective-permute-done((f32[2,288,128]{2,1,0:T(8,128)S(1)}, f32[2,288,128]{2,1,0:T(8,128)S(1)}, u32[]{:S(2)}, u32[]{:S(2)}) %collective-permute-start.12) | collective-permute-done | bytes 294944 | tf_op jit(solution)/shard_map/ppermute | solution.py:333
  52.0 2.6 %collective-permute-start.15 = (f32[1,288,128]{2,1,0:T(8,128)S(1)}, f32[1,288,128]{2,1,0:T(8,128)S(1)}, u32[]{:S(2)}, u32[]{:S(2)}) collective-permute-start(f32[1,288,128]{2,1,0:T(8,128)S(1)} %fusion.5), channel_id=1, source_target_pairs={{0,16},{1,9},{2,18},{3,11},{4,20},{5,13},{6,22},{7,15},{8,24},{9,1... | collective-permute-start | bytes 442376 | tf_op jit(solution)/shard_map/ppermute | solution.py:333
  54.7 1.5 %collective-permute-start.14 = (f32[1,128,128]{2,1,0:T(8,128)S(1)}, f32[1,128,128]{2,1,0:T(8,128)S(1)}, u32[]{:S(2)}, u32[]{:S(2)}) collective-permute-start(f32[1,128,128]{2,1,0:T(8,128)S(1)} %fusion.19), channel_id=1, source_target_pairs={{0,4},{1,3},{2,6},{3,1},{4,0},{5,7},{6,2},{7,5},{8,12},{9,11},{10,... | collective-permute-start | bytes 196616 | tf_op jit(solution)/shard_map/ppermute | solution.py:333
  56.9 2.8 %collective-permute-done.15 = f32[1,288,128]{2,1,0:T(8,128)S(1)} collective-permute-done((f32[1,288,128]{2,1,0:T(8,128)S(1)}, f32[1,288,128]{2,1,0:T(8,128)S(1)}, u32[]{:S(2)}, u32[]{:S(2)}) %collective-permute-start.15) | collective-permute-done | bytes 147488 | tf_op jit(solution)/shard_map/ppermute | solution.py:333
  61.4 2.2 %collective-permute-start.16 = (f32[2,4,32,128]{3,2,1,0:T(8,128)S(1)}, f32[2,4,32,128]{3,2,1,0:T(8,128)S(1)}, u32[]{:S(2)}, u32[]{:S(2)}) collective-permute-start(f32[2,4,32,128]{3,2,1,0:T(8,128)S(1)} %pad_maximum_fusion), channel_id=1, source_target_pairs={{0,2},{1,5},{2,0},{3,7},{4,6},{5,1},{6,4},{7,3},{8,10},{9,13},{10,... | collective-permute-start | bytes 393224 | tf_op jit(solution)/shard_map/ppermute | solution.py:333
  63.6 1.5 %collective-permute-done.18 = f32[2,4,32,128]{3,2,1,0:T(8,128)S(1)} collective-permute-done((f32[2,4,32,128]{3,2,1,0:T(8,128)S(1)}, f32[2,4,32,128]{3,2,1,0:T(8,128)S(1)}, u32[]{:S(2)}, u32[]{:S(2)}) %collective-permute-start.18) | collective-permute-done | bytes 131104 | tf_op jit(solution)/shard_map/ppermute | solution.py:333
  65.1 2.2 %collective-permute-start.19 = (f32[2,4,32,128]{3,2,1,0:T(8,128)S(1)}, f32[2,4,32,128]{3,2,1,0:T(8,128)S(1)}, u32[]{:S(2)}, u32[]{:S(2)}) collective-permute-start(f32[2,4,32,128]{3,2,1,0:T(8,128)S(1)} %pad_maximum_fusion.3), channel_id=1, source_target_pairs={{0,16},{1,9},{2,18},{3,11},{4,20},{5,13},{6,22},{7,15},{8,24},{9,1... | collective-permute-start | bytes 393224 | tf_op jit(solution)/shard_map/ppermute | solution.py:333
  67.4 1.4 %collective-permute-start.17 = (f32[2,4,32,128]{3,2,1,0:T(8,128)S(1)}, f32[2,4,32,128]{3,2,1,0:T(8,128)S(1)}, u32[]{:S(2)}, u32[]{:S(2)}) collective-permute-start(f32[2,4,32,128]{3,2,1,0:T(8,128)S(1)} %pad_maximum_fusion.1), channel_id=1, source_target_pairs={{0,4},{1,3},{2,6},{3,1},{4,0},{5,7},{6,2},{7,5},{8,12},{9,11},{10,... | collective-permute-start | bytes 393224 | tf_op jit(solution)/shard_map/ppermute | solution.py:333
  68.8 3.6 %collective-permute-done.17 = f32[2,4,32,128]{3,2,1,0:T(8,128)S(1)} collective-permute-done((f32[2,4,32,128]{3,2,1,0:T(8,128)S(1)}, f32[2,4,32,128]{3,2,1,0:T(8,128)S(1)}, u32[]{:S(2)}, u32[]{:S(2)}) %collective-permute-start.17) | collective-permute-done | bytes 131104 | tf_op jit(solution)/shard_map/ppermute | solution.py:333
  73.2 1.3 %collective-permute-done.20.refs_2_ = f32[240,128]{1,0:T(8,128)S(1)} collective-permute-done((f32[240,128]{1,0:T(8,128)S(1)}, f32[240,128]{1,0:T(8,128)S(1)}, u32[]{:S(2)}, u32[]{:S(2)}) %collective-permute-start.20) | collective-permute-done | bytes 122912 | tf_op jit(solution)/shard_map/ppermute | solution.py:278
  74.5 1.7 %place.1 = f32[128,1024]{1,0:T(8,128)} custom-call(s32[16]{0:T(128)S(1)} %copy-done, f32[240,128]{1,0:T(8,128)S(1)} %pad_maximum_fusion.4.refs_0_, f32[24,32,128]{2,1,0:T(8,128)S(1)} %fusion.9.refs_1_, f32[240,128]{1,0:T(8,128)S(1)} %collective-permute-done.20.refs_2_, f32[24,32,128]{2,1,0:T(8,128)S(1)} %collective-permute-done.21.refs_3_), custom_call_target="tpu_custom_call" | custom-call | tf_op jit(solution)/shard_map/place/pallas_call | solution.py:386
  (86 shorter events, 6.6 us)
Async XLA Ops:
  9.9 3.0 %collective-permute-start = (f32[2304,128]{1,0:T(8,128)S(1)}, f32[2304,128]{1,0:T(8,128)S(1)}, u32[]{:S(2)}, u32[]{:S(2)}) collective-permute-start(f32[2304,128]{1,0:T(8,128)S(1)} %slice_bitcast_fusion), channel_id=1, source_target_pairs={{0,1},{1,0},{2,3},{3,2},{4,5},{5,4},{6,7},{7,6},{8,9},{9,8},{10,11... | collective-permute-start | bytes 3538952 | tf_op jit(solution)/shard_map/ppermute | solution.py:278
  13.2 3.6 %collective-permute-start.2 = (f32[1920,128]{1,0:T(8,128)S(1)}, f32[1920,128]{1,0:T(8,128)S(1)}, u32[]{:S(2)}, u32[]{:S(2)}) collective-permute-start(f32[1920,128]{1,0:T(8,128)S(1)} %bitcast_add_fusion.1), channel_id=1, source_target_pairs={{0,1},{1,0},{2,3},{3,2},{4,5},{5,4},{6,7},{7,6},{8,9},{9,8},{10,11... | collective-permute-start | bytes 2949128 | tf_op jit(solution)/shard_map/ppermute | solution.py:278
  13.6 7.5 %collective-permute-start.1 = (f32[4224,128]{1,0:T(8,128)S(1)}, f32[4224,128]{1,0:T(8,128)S(1)}, u32[]{:S(2)}, u32[]{:S(2)}) collective-permute-start(f32[4224,128]{1,0:T(8,128)S(1)} %bitcast_add_fusion), channel_id=1, source_target_pairs={{0,1},{1,0},{2,3},{3,2},{4,5},{5,4},{6,7},{7,6},{8,9},{9,8},{10,11... | collective-permute-start | bytes 6488072 | tf_op jit(solution)/shard_map/ppermute | solution.py:278
  13.9 17.1 %collective-permute-start.5 = (f32[8,288,128]{2,1,0:T(8,128)S(1)}, f32[8,288,128]{2,1,0:T(8,128)S(1)}, u32[]{:S(2)}, u32[]{:S(2)}) collective-permute-start(f32[8,288,128]{2,1,0:T(8,128)S(1)} %bitcast.136), channel_id=1, source_target_pairs={{0,2},{1,5},{2,0},{3,7},{4,6},{5,1},{6,4},{7,3},{8,10},{9,13},{10,... | collective-permute-start | bytes 3538952 | tf_op jit(solution)/shard_map/ppermute | solution.py:333
  17.0 16.2 %collective-permute-start.4 = (f32[4,128,128]{2,1,0:T(8,128)S(1)}, f32[4,128,128]{2,1,0:T(8,128)S(1)}, u32[]{:S(2)}, u32[]{:S(2)}) collective-permute-start(f32[4,128,128]{2,1,0:T(8,128)S(1)} %get-tuple-element.10), channel_id=1, source_target_pairs={{0,8},{1,17},{2,10},{3,19},{4,12},{5,21},{6,14},{7,23},{8,0},{9,25... | collective-permute-start | bytes 786440 | tf_op jit(solution)/shard_map/ppermute | solution.py:333
  19.1 19.3 %collective-permute-start.3 = (f32[8,112,128]{2,1,0:T(8,128)S(1)}, f32[8,112,128]{2,1,0:T(8,128)S(1)}, u32[]{:S(2)}, u32[]{:S(2)}) collective-permute-start(f32[8,112,128]{2,1,0:T(8,128)S(1)} %broadcast_add_fusion.1), channel_id=1, source_target_pairs={{0,2},{1,5},{2,0},{3,7},{4,6},{5,1},{6,4},{7,3},{8,10},{9,13},{10,... | collective-permute-start | bytes 1376264 | tf_op jit(solution)/shard_map/ppermute | solution.py:333
  20.6 23.0 %collective-permute-start.7 = (f32[4,128,128]{2,1,0:T(8,128)S(1)}, f32[4,128,128]{2,1,0:T(8,128)S(1)}, u32[]{:S(2)}, u32[]{:S(2)}) collective-permute-start(f32[4,128,128]{2,1,0:T(8,128)S(1)} %get-tuple-element.9), channel_id=1, source_target_pairs={{0,8},{1,17},{2,10},{3,19},{4,12},{5,21},{6,14},{7,23},{8,0},{9,25... | collective-permute-start | bytes 786440 | tf_op jit(solution)/shard_map/ppermute | solution.py:333
  31.1 10.6 %collective-permute-start.9 = (f32[4,288,128]{2,1,0:T(8,128)S(1)}, f32[4,288,128]{2,1,0:T(8,128)S(1)}, u32[]{:S(2)}, u32[]{:S(2)}) collective-permute-start(f32[4,288,128]{2,1,0:T(8,128)S(1)} %fusion), channel_id=1, source_target_pairs={{0,4},{1,3},{2,6},{3,1},{4,0},{5,7},{6,2},{7,5},{8,12},{9,11},{10,... | collective-permute-start | bytes 1769480 | tf_op jit(solution)/shard_map/ppermute | solution.py:333
  33.2 10.4 %collective-permute-start.8 = (f32[4,128,128]{2,1,0:T(8,128)S(1)}, f32[4,128,128]{2,1,0:T(8,128)S(1)}, u32[]{:S(2)}, u32[]{:S(2)}) collective-permute-start(f32[4,128,128]{2,1,0:T(8,128)S(1)} %add_add_fusion), channel_id=1, source_target_pairs={{0,16},{1,9},{2,18},{3,11},{4,20},{5,13},{6,22},{7,15},{8,24},{9,1... | collective-permute-start | bytes 786440 | tf_op jit(solution)/shard_map/ppermute | solution.py:333
  38.4 6.8 %collective-permute-start.6 = (f32[4,112,128]{2,1,0:T(8,128)S(1)}, f32[4,112,128]{2,1,0:T(8,128)S(1)}, u32[]{:S(2)}, u32[]{:S(2)}) collective-permute-start(f32[4,112,128]{2,1,0:T(8,128)S(1)} %fusion.2), channel_id=1, source_target_pairs={{0,4},{1,3},{2,6},{3,1},{4,0},{5,7},{6,2},{7,5},{8,12},{9,11},{10,... | collective-permute-start | bytes 688136 | tf_op jit(solution)/shard_map/ppermute | solution.py:333
  41.8 10.2 %collective-permute-start.12 = (f32[2,288,128]{2,1,0:T(8,128)S(1)}, f32[2,288,128]{2,1,0:T(8,128)S(1)}, u32[]{:S(2)}, u32[]{:S(2)}) collective-permute-start(f32[2,288,128]{2,1,0:T(8,128)S(1)} %fusion.1), channel_id=1, source_target_pairs={{0,8},{1,17},{2,10},{3,19},{4,12},{5,21},{6,14},{7,23},{8,0},{9,25... | collective-permute-start | bytes 884744 | tf_op jit(solution)/shard_map/ppermute | solution.py:333
  43.7 11.0 %collective-permute-start.11 = (f32[2,128,128]{2,1,0:T(8,128)S(1)}, f32[2,128,128]{2,1,0:T(8,128)S(1)}, u32[]{:S(2)}, u32[]{:S(2)}) collective-permute-start(f32[2,128,128]{2,1,0:T(8,128)S(1)} %fusion.7), channel_id=1, source_target_pairs={{0,2},{1,5},{2,0},{3,7},{4,6},{5,1},{6,4},{7,3},{8,10},{9,13},{10,... | collective-permute-start | bytes 393224 | tf_op jit(solution)/shard_map/ppermute | solution.py:333
  45.3 10.9 %collective-permute-start.10 = (f32[2,112,128]{2,1,0:T(8,128)S(1)}, f32[2,112,128]{2,1,0:T(8,128)S(1)}, u32[]{:S(2)}, u32[]{:S(2)}) collective-permute-start(f32[2,112,128]{2,1,0:T(8,128)S(1)} %fusion.8), channel_id=1, source_target_pairs={{0,8},{1,17},{2,10},{3,19},{4,12},{5,21},{6,14},{7,23},{8,0},{9,25... | collective-permute-start | bytes 344072 | tf_op jit(solution)/shard_map/ppermute | solution.py:333
  52.0 7.7 %collective-permute-start.15 = (f32[1,288,128]{2,1,0:T(8,128)S(1)}, f32[1,288,128]{2,1,0:T(8,128)S(1)}, u32[]{:S(2)}, u32[]{:S(2)}) collective-permute-start(f32[1,288,128]{2,1,0:T(8,128)S(1)} %fusion.5), channel_id=1, source_target_pairs={{0,16},{1,9},{2,18},{3,11},{4,20},{5,13},{6,22},{7,15},{8,24},{9,1... | collective-permute-start | bytes 442376 | tf_op jit(solution)/shard_map/ppermute | solution.py:333
  54.7 5.1 %collective-permute-start.14 = (f32[1,128,128]{2,1,0:T(8,128)S(1)}, f32[1,128,128]{2,1,0:T(8,128)S(1)}, u32[]{:S(2)}, u32[]{:S(2)}) collective-permute-start(f32[1,128,128]{2,1,0:T(8,128)S(1)} %fusion.19), channel_id=1, source_target_pairs={{0,4},{1,3},{2,6},{3,1},{4,0},{5,7},{6,2},{7,5},{8,12},{9,11},{10,... | collective-permute-start | bytes 196616 | tf_op jit(solution)/shard_map/ppermute | solution.py:333
  56.2 5.2 %collective-permute-start.13 = (f32[1,112,128]{2,1,0:T(8,128)S(1)}, f32[1,112,128]{2,1,0:T(8,128)S(1)}, u32[]{:S(2)}, u32[]{:S(2)}) collective-permute-start(f32[1,112,128]{2,1,0:T(8,128)S(1)} %fusion.21), channel_id=1, source_target_pairs={{0,16},{1,9},{2,18},{3,11},{4,20},{5,13},{6,22},{7,15},{8,24},{9,1... | collective-permute-start | bytes 172040 | tf_op jit(solution)/shard_map/ppermute | solution.py:333
  59.8 14.7 %copy-start = (s32[16]{0:T(128)S(1)}, s32[16]{0:T(128)}, u32[]{:S(2)}) copy-start(s32[16]{0:T(128)} %owner_ref.1) | copy-start | bytes 196
  59.9 5.2 %collective-permute-start.18 = (f32[2,4,32,128]{3,2,1,0:T(8,128)S(1)}, f32[2,4,32,128]{3,2,1,0:T(8,128)S(1)}, u32[]{:S(2)}, u32[]{:S(2)}) collective-permute-start(f32[2,4,32,128]{3,2,1,0:T(8,128)S(1)} %pad_maximum_fusion.2), channel_id=1, source_target_pairs={{0,8},{1,17},{2,10},{3,19},{4,12},{5,21},{6,14},{7,23},{8,0},{9,25... | collective-permute-start | bytes 393224 | tf_op jit(solution)/shard_map/ppermute | solution.py:333
  61.4 5.9 %collective-permute-start.16 = (f32[2,4,32,128]{3,2,1,0:T(8,128)S(1)}, f32[2,4,32,128]{3,2,1,0:T(8,128)S(1)}, u32[]{:S(2)}, u32[]{:S(2)}) collective-permute-start(f32[2,4,32,128]{3,2,1,0:T(8,128)S(1)} %pad_maximum_fusion), channel_id=1, source_target_pairs={{0,2},{1,5},{2,0},{3,7},{4,6},{5,1},{6,4},{7,3},{8,10},{9,13},{10,... | collective-permute-start | bytes 393224 | tf_op jit(solution)/shard_map/ppermute | solution.py:333
  65.1 7.3 %collective-permute-start.19 = (f32[2,4,32,128]{3,2,1,0:T(8,128)S(1)}, f32[2,4,32,128]{3,2,1,0:T(8,128)S(1)}, u32[]{:S(2)}, u32[]{:S(2)}) collective-permute-start(f32[2,4,32,128]{3,2,1,0:T(8,128)S(1)} %pad_maximum_fusion.3), channel_id=1, source_target_pairs={{0,16},{1,9},{2,18},{3,11},{4,20},{5,13},{6,22},{7,15},{8,24},{9,1... | collective-permute-start | bytes 393224 | tf_op jit(solution)/shard_map/ppermute | solution.py:333
  67.4 5.0 %collective-permute-start.17 = (f32[2,4,32,128]{3,2,1,0:T(8,128)S(1)}, f32[2,4,32,128]{3,2,1,0:T(8,128)S(1)}, u32[]{:S(2)}, u32[]{:S(2)}) collective-permute-start(f32[2,4,32,128]{3,2,1,0:T(8,128)S(1)} %pad_maximum_fusion.1), channel_id=1, source_target_pairs={{0,4},{1,3},{2,6},{3,1},{4,0},{5,7},{6,2},{7,5},{8,12},{9,11},{10,... | collective-permute-start | bytes 393224 | tf_op jit(solution)/shard_map/ppermute | solution.py:333
  72.5 2.0 %collective-permute-start.21 = (f32[24,32,128]{2,1,0:T(8,128)S(1)}, f32[24,32,128]{2,1,0:T(8,128)S(1)}, u32[]{:S(2)}, u32[]{:S(2)}) collective-permute-start(f32[24,32,128]{2,1,0:T(8,128)S(1)} %fusion.9.refs_1_), channel_id=1, source_target_pairs={{0,1},{1,0},{2,3},{3,2},{4,5},{5,4},{6,7},{7,6},{8,9},{9,8},{10,11... | collective-permute-start | bytes 1179656 | tf_op jit(solution)/shard_map/ppermute | solution.py:278
  72.6 1.9 %collective-permute-start.20 = (f32[240,128]{1,0:T(8,128)S(1)}, f32[240,128]{1,0:T(8,128)S(1)}, u32[]{:S(2)}, u32[]{:S(2)}) collective-permute-start(f32[240,128]{1,0:T(8,128)S(1)} %pad_maximum_fusion.4.refs_0_), channel_id=1, source_target_pairs={{0,1},{1,0},{2,3},{3,2},{4,5},{5,4},{6,7},{7,6},{8,9},{9,8},{10,11... | collective-permute-start | bytes 368648 | tf_op jit(solution)/shard_map/ppermute | solution.py:278
